TPU v7x, 256 devices: a whole 4x4x8 slice. The times are simulated.
256 devices in a mesh: ctx: 64 (over y, z, core), head: 4 (over x).
Axes of the slice: x: 4, y: 4, z: 8, core: 2. Of those that a mesh axis runs over, the one named last changes fastest.
Arguments:
- queries: bfloat16 [16384, 4096], P('ctx', 'head'), may hold values from -6 to 6
- keys: bfloat16 [16384, 4096], P('ctx', 'head'), may hold values from -6 to 6
- values: bfloat16 [16384, 4096], P('ctx', 'head'), may hold values from -150 to 150
- out_grad: bfloat16 [16384, 4096], P('ctx', 'head'), may hold values from -6 to 6
- gain: bfloat16 [4096], P('head'), may hold values from 0.099609375 to 1.8984375
Outputs:
- query_grad: bfloat16 [16384, 4096], P('ctx', 'head')
- key_grad: bfloat16 [16384, 4096], P('ctx', 'head')
- value_grad: bfloat16 [16384, 4096], P('ctx', 'head')
All inputs are finite; a program needn't handle non-finite values.
Results may differ from a plain program's by a relative error of at most 0.0058.
Values sent between devices are 32-bit elements; how exact they have to be, the bound alone decides.
No kernel may reach another device: no remote copies, remote signals or barrier semaphores. Data moves between devices by JAX's collectives and lax.ppermute only.
A program may use at most 128 MiB of HBM per device.

v0:
```python
import jax
import jax.numpy as jnp
from jax import lax
from jax.sharding import PartitionSpec as P

HEADS = 32
HEAD_DIM = 128
BLOCK = 128


EPSILON = 1e-05


def entering(part, axis, combine, identity, reverse):
    count = lax.axis_size(axis)
    place = lax.axis_index(axis)
    ahead = count - 1 - place if reverse else place
    gathered = lax.all_gather(part, axis)
    state = jnp.zeros_like(part) + jnp.asarray(identity, part.dtype)

    def one(turn, state):
        source = count - 1 - turn if reverse else turn
        return combine(state, lax.dynamic_index_in_dim(gathered, source, 0, False))

    return lax.fori_loop(0, ahead, one, state)


def add_states(earlier, later):
    return earlier + later


def order_mask(count, later):
    row_index = lax.broadcasted_iota(jnp.int32, (count, count), 0)
    col_index = lax.broadcasted_iota(jnp.int32, (count, count), 1)
    if later:
        return (col_index > row_index).astype(jnp.float32)
    return (col_index < row_index).astype(jnp.float32)


def masked_sums(stack, later):
    mask = order_mask(stack.shape[0], later)
    return jnp.einsum("mn,n...->m...", mask, stack, precision=lax.Precision.HIGHEST)


def on_device(queries, keys, values, out_grad, gain):
    tokens, width = queries.shape
    heads = width // HEAD_DIM
    blocks = tokens // BLOCK
    factor = HEAD_DIM ** (-0.5)
    features = HEADS * HEAD_DIM
    shape = (blocks, BLOCK, heads, HEAD_DIM)
    query_blocks = queries.reshape(shape)
    key_blocks = keys.reshape(shape)
    value_blocks = values.reshape(shape)
    row_index = lax.broadcasted_iota(jnp.int32, (BLOCK, BLOCK), 0)
    col_index = lax.broadcasted_iota(jnp.int32, (BLOCK, BLOCK), 1)
    causal = (col_index <= row_index)[None, None]
    raw_scores = jnp.einsum(
        "nthd,nshd->nhts", query_blocks, key_blocks, preferred_element_type=jnp.float32
    )
    probs = jnp.where(causal, raw_scores * factor, 0.0).astype(jnp.bfloat16)
    within = jnp.einsum("nhts,nshd->nthd", probs, value_blocks, preferred_element_type=jnp.float32)
    key_value = jnp.einsum(
        "nshi,nshj->nhij", key_blocks, value_blocks, preferred_element_type=jnp.float32
    )
    local_before = masked_sums(key_value, False)
    own_total = jnp.sum(key_value, axis=0)
    zero_state = jnp.zeros_like(own_total)
    prefix = entering(own_total, "ctx", add_states, zero_state, False)
    state_low = (prefix[None] + local_before).astype(jnp.bfloat16)
    carried = jnp.einsum(
        "nthi,nhij->nthj", query_blocks, state_low, preferred_element_type=jnp.float32
    )
    output = within + factor * carried
    upstream = out_grad.reshape(shape).astype(jnp.float32) * gain.reshape(heads, HEAD_DIM).astype(
        jnp.float32
    )
    square_local = jnp.sum(output * output, axis=(2, 3))
    mixed_local = jnp.sum(upstream * output, axis=(2, 3))
    squares = lax.psum(square_local, "head")
    inv_rms = lax.rsqrt(squares / features + EPSILON)
    mixed = lax.psum(mixed_local, "head")
    delta = (
        inv_rms[..., None, None] * upstream
        - (inv_rms**3 * (mixed / features))[..., None, None] * output
    )
    out_delta = delta.astype(jnp.bfloat16)
    raw_delta = jnp.einsum(
        "nthj,nshj->nhts", out_delta, value_blocks, preferred_element_type=jnp.float32
    )
    delta_scores = jnp.where(causal, raw_delta * factor, 0.0).astype(jnp.bfloat16)
    query_grad = jnp.einsum(
        "nhts,nshi->nthi", delta_scores, key_blocks, preferred_element_type=jnp.float32
    )
    query_grad = query_grad + factor * jnp.einsum(
        "nthj,nhij->nthi", out_delta, state_low, preferred_element_type=jnp.float32
    )
    delta_query = jnp.einsum(
        "nthj,nthi->nhji", out_delta, query_blocks, preferred_element_type=jnp.float32
    )
    back_total = jnp.sum(delta_query, axis=0)
    local_after = masked_sums(delta_query, True)
    suffix = entering(back_total, "ctx", add_states, zero_state, True)
    later_low = (suffix[None] + local_after).astype(jnp.bfloat16)
    key_grad = jnp.einsum(
        "nhts,nthi->nshi", delta_scores, query_blocks, preferred_element_type=jnp.float32
    )
    key_grad = key_grad + factor * jnp.einsum(
        "nshj,nhji->nshi", value_blocks, later_low, preferred_element_type=jnp.float32
    )
    value_grad = jnp.einsum("nhts,nthj->nshj", probs, out_delta, preferred_element_type=jnp.float32)
    value_grad = value_grad + factor * jnp.einsum(
        "nshi,nhji->nshj", key_blocks, later_low, preferred_element_type=jnp.float32
    )
    return (
        query_grad.reshape(tokens, width).astype(jnp.bfloat16),
        key_grad.reshape(tokens, width).astype(jnp.bfloat16),
        value_grad.reshape(tokens, width).astype(jnp.bfloat16),
    )


def solution(mesh):
    in_specs = (P("ctx", "head"), P("ctx", "head"), P("ctx", "head"), P("ctx", "head"), P("head"))
    out_specs = (P("ctx", "head"), P("ctx", "head"), P("ctx", "head"))
    return jax.shard_map(
        on_device, mesh=mesh, in_specs=in_specs, out_specs=out_specs, check_vma=False
    )
```

profile of v0, /device:TPU:1, one launch (start us, length us, event | category | flops | bytes accessed | tf_op | source)
XLA Modules:
  0.0 477.6 jit_solution(5002671313167619276)
XLA Ops:
  9.5 2.2 fusion.48
  12.9 1.3 convert_bitcast_fusion
  14.2 1.2 copy.124
  15.4 1.6 copy.94
  18.2 1.5 convolution_bitcast_fusion.2
  19.7 3.7 fusion.19
  23.5 135.1 %all-gather.5.cloned.1.call-done = f32[512,128,128]{2,1,0:T(8,128)} async-done(((f32[8,128,128]{2,1,0:T(8,128)}), f32[512,128,128]{2,1,0:T(8,128)}) %all-gather.5.cloned.1.call-update) | async-done | bytes 33554448 | tf_op jit(solution)/shard_map/all_gather | solution.py:18
  158.6 1.2 while.22
  158.7 1.2 bitcast_add_fusion.4
  159.8 2.9 multiply_reduce_fusion.1
  162.7 8.4 %all-reduce = (f32[2,128]{1,0:T(2,128)S(1)}, f32[2,128]{1,0:T(2,128)S(1)}) all-reduce(f32[2,128]{1,0:T(2,128)S(1)} %get-tuple-element.85, f32[2,128]{1,0:T(2,128)S(1)} %get-tuple-element.84), channel_id=1, replica_groups=mesh['ctx'=64,'head'=4] {'head'}, use_global_device_ids=true, to_apply=%region_6.7 | all-reduce | flops 512 | bytes 4096 | tf_op jit(solution)/shard_map/psum | solution.py:82
  171.1 1.5 subtract_convert_fusion
  173.4 3.2 fusion.49
  176.6 1.7 fusion.12
  178.8 1.4 fusion.9
  181.4 2.4 convolution_bitcast_fusion
  183.8 1.5 fusion.50
  185.3 3.7 fusion.17
  189.0 197.9 %all-gather.7.cloned.1.call-done = f32[512,128,128]{2,1,0:T(8,128)} async-done(((f32[8,128,128]{2,1,0:T(8,128)}), f32[512,128,128]{2,1,0:T(8,128)}) %all-gather.7.cloned.1.call-update) | async-done | bytes 33554448 | tf_op jit(solution)/shard_map/all_gather | solution.py:18
  386.9 74.2 %while.23 = (s32[]{:T(128)}, f32[8,128,128]{2,1,0:T(8,128)S(1)}, s32[]{:T(128)}, f32[64,8,128,128]{3,2,1,0:T(8,128)}, s32[]{:T(128)}, /*index=5*/s32[]{:T(128)}, s32[]{:T(128)}, s32[]{:T(128)}) while((s32[]{:T(128)}, f32[8,128,128]{2,1,0:T(8,128)S(1)}, s32[]{:T(128)}, f32[64,8,128,128]{3,2,1,0:T(8,128)}, s32[]{:T(128)}, /*index=5*/s32[]{:T(128)}, ...), condition=%wide.region_9.10_spmd, body=%wide.region_8.9_spmd.sunk | while | flops 131078 | bytes 1572999 | solution.py:25
  386.9 1.2 bitcast_add_fusion.5
  388.1 1.2 bitcast_add_fusion.5
  392.9 1.2 bitcast_add_fusion.5
  394.1 1.2 bitcast_add_fusion.5
  398.9 1.2 bitcast_add_fusion.5
  400.1 1.2 bitcast_add_fusion.5
  404.9 1.2 bitcast_add_fusion.5
  406.1 1.2 bitcast_add_fusion.5
  410.9 1.2 bitcast_add_fusion.5
  415.6 1.2 bitcast_add_fusion.5
  416.8 1.2 bitcast_add_fusion.5
  421.6 1.2 bitcast_add_fusion.5
  422.8 1.2 bitcast_add_fusion.5
  427.6 1.2 bitcast_add_fusion.5
  428.8 1.2 bitcast_add_fusion.5
  433.6 1.2 bitcast_add_fusion.5
  438.4 1.2 bitcast_add_fusion.5
  439.6 1.2 bitcast_add_fusion.5
  444.4 1.2 bitcast_add_fusion.5
  445.6 1.2 bitcast_add_fusion.5
  450.3 1.2 bitcast_add_fusion.5
  451.5 1.2 bitcast_add_fusion.5
  456.3 1.2 bitcast_add_fusion.5
  461.1 2.7 fusion.10
  463.8 2.1 copy.109
  465.9 1.3 fusion.14
  467.2 1.3 copy.111
  468.5 2.2 copy_bitcast_fusion
  (63 shorter events, 52.9 us)
Async XLA Ops:
  7.2 151.4 %all-gather.5.cloned.1.call-start = ((), (), s32[]{:S(2)}) async-start(), calls=%async_computation | async-start | bytes 34078720 | tf_op jit(solution)/shard_map/all_gather | solution.py:18
  9.5 10.2 %copy-start = (bf16[32,8,8,128]{3,2,1,0:T(8,128)(2,1)}, bf16[32,8,8,128]{3,2,1,0:T(8,128)(2,1)S(1)}, u32[]{:S(2)}) copy-start(bf16[32,8,8,128]{3,2,1,0:T(8,128)(2,1)S(1)} %copy.123) | copy-start | bytes 1572868
  11.7 375.2 %all-gather.7.cloned.1.call-start = ((), (), s32[]{:S(2)}) async-start(), calls=%async_computation.1 | async-start | bytes 34078720 | tf_op jit(solution)/shard_map/all_gather | solution.py:18
  12.9 6.9 %copy-start.2 = (bf16[32,8,8,128]{3,2,1,0:T(8,128)(2,1)}, bf16[32,8,8,128]{3,2,1,0:T(8,128)(2,1)S(1)}, u32[]{:S(2)}) copy-start(bf16[32,8,8,128]{3,2,1,0:T(8,128)(2,1)S(1)} %copy.121) | copy-start | bytes 1572868
  18.2 140.4 %copy-start.3 = (bf16[2,8,128,128]{3,2,1,0:T(8,128)(2,1)}, bf16[2,8,128,128]{3,2,1,0:T(8,128)(2,1)S(1)}, u32[]{:S(2)}) copy-start(bf16[2,8,128,128]{3,2,1,0:T(8,128)(2,1)S(1)} %fusion.13) | copy-start | bytes 1572868
  172.6 0.8 copy-start.1
Sparse Core Ops, SparseCore 0:
  11.8 146.7 all-gather.4
  176.7 210.0 all-gather.6
where the time goes:
time: 481 us; the launch traced here: 478 us
  waiting for transfers between devices  333 us (69%)
  other arithmetic  77.2 us (16%)
  matrix products  29.1 us (6%)
  between operations  14.2 us (3%)
  local copies, waits for them, and re-layouts  13.9 us (3%)
  blocking collectives  8.37 us (2%)
    all_gather x2, waiting for transfers between devices, entering(): gathered = lax.all_gather(part, axis)  333 us
    add x63, other arithmetic, add_states(): return earlier + later  73.6 us
  transfers between devices with their start and end apart: 2, of which 2 were waited for; matrix products, arithmetic and copies ran while one was open for 5% of the time, Pallas kernels for 0%

commit v1 on v0

v1 whole, which is shorter than its diff:
```python
import functools

import jax
import jax.numpy as jnp
from jax import lax
from jax.experimental import pallas as pl
from jax.experimental.pallas import tpu as pltpu
from jax.sharding import Mesh
from jax.sharding import PartitionSpec as P

HEADS = 32
HEAD_DIM = 128
EPSILON = 1e-05
FEATURES = HEADS * HEAD_DIM
FACTOR = HEAD_DIM ** (-0.5)
F32 = jnp.float32
BF16 = jnp.bfloat16
VMEM_LIMIT = 48 * 1024 * 1024


def dot_nn(a, b):
    return lax.dot_general(a, b, (((1,), (0,)), ((), ())), preferred_element_type=F32)


def dot_nt(a, b):
    return lax.dot_general(a, b, (((1,), (1,)), ((), ())), preferred_element_type=F32)


def dot_tn(a, b):
    return lax.dot_general(a, b, (((0,), (0,)), ((), ())), preferred_element_type=F32)


def columns(head):
    return pl.ds(head * HEAD_DIM, HEAD_DIM)


def causal(count, transposed):
    row = lax.broadcasted_iota(jnp.int32, (count, count), 0)
    col = lax.broadcasted_iota(jnp.int32, (count, count), 1)
    return row <= col if transposed else col <= row


def scores(a, b, mask):
    return jnp.where(mask, dot_nt(a, b) * FACTOR, 0.0).astype(BF16)


def call(kernel, out_shape, **kwargs):
    return pl.pallas_call(
        kernel,
        out_shape=out_shape,
        compiler_params=pltpu.CompilerParams(vmem_limit_bytes=VMEM_LIMIT),
        **kwargs,
    )


def totals_kernel(keys, values, out):
    for head in range(out.shape[0]):
        out[head] = dot_tn(keys[:, columns(head)], values[:, columns(head)])


def scan_kernel(reverse, parts, out):
    count = parts.shape[0]
    order = range(count - 1, -1, -1) if reverse else range(count)
    total = jnp.zeros(parts.shape[1:], F32)
    for at in order:
        out[at] = total
        total = total + parts[at]


def forward_kernel(queries, keys, values, out_grad, gain, state, output, low, sums):
    tokens = queries.shape[0]
    mask = causal(tokens, False)
    square = jnp.zeros((tokens, HEAD_DIM), F32)
    mixed = jnp.zeros((tokens, HEAD_DIM), F32)
    for head in range(state.shape[0]):
        at = columns(head)
        query = queries[:, at]
        probs = scores(query, keys[:, at], mask)
        state_low = state[head].astype(BF16)
        low[head] = state_low
        out = dot_nn(probs, values[:, at]) + FACTOR * dot_nn(query, state_low)
        output[:, at] = out
        upstream = out_grad[:, at].astype(F32) * gain[:, at].astype(F32)
        square = square + out * out
        mixed = mixed + upstream * out
    sums[0:1] = jnp.sum(square.T, axis=0, keepdims=True)
    sums[1:2] = jnp.sum(mixed.T, axis=0, keepdims=True)


def delta_kernel(queries, keys, values, out_grad, gain, output, low, sums, delta, back, query_grad):
    tokens = queries.shape[0]
    mask = causal(tokens, False)
    inv_rms = lax.rsqrt(sums[0:1] / FEATURES + EPSILON)
    pull = inv_rms * inv_rms * inv_rms * (sums[1:2] / FEATURES)
    inv_rms = jnp.broadcast_to(inv_rms, (HEAD_DIM, tokens)).T
    pull = jnp.broadcast_to(pull, (HEAD_DIM, tokens)).T
    for head in range(low.shape[0]):
        at = columns(head)
        upstream = out_grad[:, at].astype(F32) * gain[:, at].astype(F32)
        out_delta = (inv_rms * upstream - pull * output[:, at]).astype(BF16)
        delta[:, at] = out_delta
        back[head] = dot_tn(out_delta, queries[:, at])
        delta_scores = scores(out_delta, values[:, at], mask)
        grad = dot_nn(delta_scores, keys[:, at]) + FACTOR * dot_nt(out_delta, low[head])
        query_grad[:, at] = grad.astype(BF16)


def backward_kernel(queries, keys, values, delta, state, key_grad, value_grad):
    tokens = queries.shape[0]
    mask = causal(tokens, True)
    for head in range(state.shape[0]):
        at = columns(head)
        query, key, value, out_delta = queries[:, at], keys[:, at], values[:, at], delta[:, at]
        later_low = state[head].astype(BF16)
        delta_scores = scores(value, out_delta, mask)
        grad = dot_nn(delta_scores, query) + FACTOR * dot_nn(value, later_low)
        key_grad[:, at] = grad.astype(BF16)
        probs = scores(key, query, mask)
        grad = dot_nn(probs, out_delta) + FACTOR * dot_nt(key, later_low)
        value_grad[:, at] = grad.astype(BF16)


def entering(total, reverse):
    chips = lax.axis_size("chip")
    core = lax.axis_index("core")
    heads = total.shape[0]
    half = heads // 2
    rows = half * HEAD_DIM // chips
    swap = [(0, 1), (1, 0)]
    mine = lax.dynamic_slice_in_dim(total, core * half, half)
    other = lax.dynamic_slice_in_dim(total, (1 - core) * half, half)
    got = lax.ppermute(other, "core", swap)
    parts = (mine + got).reshape(chips, rows, HEAD_DIM)
    parts = lax.all_to_all(parts, "chip", 0, 0, tiled=True)
    parts = call(
        functools.partial(scan_kernel, reverse), jax.ShapeDtypeStruct(parts.shape, F32)
    )(parts)
    pair = lax.all_to_all(parts, "chip", 0, 0, tiled=True).reshape(half, HEAD_DIM, HEAD_DIM)
    ahead = core == (1 if reverse else 0)
    own = pair + jnp.where(ahead, 0.0, got)
    theirs = lax.ppermute(pair + jnp.where(ahead, mine, 0.0), "core", swap)
    return jnp.where(
        core == 0, jnp.concatenate([own, theirs]), jnp.concatenate([theirs, own])
    )


def on_device(queries, keys, values, out_grad, gain):
    tokens, width = queries.shape
    heads = width // HEAD_DIM
    gain = gain.reshape(1, width)
    wide = jax.ShapeDtypeStruct((tokens, width), BF16)
    states = jax.ShapeDtypeStruct((heads, HEAD_DIM, HEAD_DIM), F32)
    total = call(totals_kernel, states)(keys, values)
    state = entering(total, False)
    output, low, sums = call(
        forward_kernel,
        (
            jax.ShapeDtypeStruct((tokens, width), F32),
            jax.ShapeDtypeStruct(states.shape, BF16),
            jax.ShapeDtypeStruct((2, tokens), F32),
        ),
    )(queries, keys, values, out_grad, gain, state)
    sums = lax.psum(sums, "head")
    delta, back, query_grad = call(delta_kernel, (wide, states, wide))(
        queries, keys, values, out_grad, gain, output, low, sums
    )
    state = entering(back, True)
    key_grad, value_grad = call(backward_kernel, (wide, wide))(
        queries, keys, values, delta, state
    )
    return query_grad, key_grad, value_grad


def solution(mesh):
    count, across = mesh.devices.shape
    inner = Mesh(mesh.devices.reshape(count // 2, 2, across), ("chip", "core", "head"))
    spec = P(("chip", "core"), "head")
    return jax.shard_map(
        on_device,
        mesh=inner,
        in_specs=(spec, spec, spec, spec, P("head")),
        out_specs=(spec, spec, spec),
        check_vma=False,
    )
```

time: 481 us -> 107 us (0.22)
  waiting for transfers between devices: 333 us -> 23.9 us
  other arithmetic: 77.2 us -> 0.23 us
  blocking collectives: 8.37 us -> 41.1 us
  matrix products: 29.1 us -> 0 us
  starting transfers between devices: 0.08 us -> 26.6 us
  between operations: 14.2 us -> 0.75 us
  local copies, waits for them, and re-layouts: 13.9 us -> 5.47 us
  Pallas kernels: 0 us -> 8.1 us
    all_gather x2 -> x0, waiting for transfers between devices: 333 us -> none  [entering(): gathered = lax.all_gather(part, axis)]
    add x63 -> x4, other arithmetic: 73.6 us -> 0.15 us  [the longest x2 0.09 us: entering(): own = pair + jnp.where(ahead, 0.0, got)]
    all_to_all x0 -> x2, blocking collectives: none -> 32.7 us  [entering(): parts = lax.all_to_all(parts, 'chip', 0, 0, tiled=True)]
    dot_general x14 -> x0, matrix products: 29.1 us -> none  [the longest x2 7.48 us: masked_sums(): jnp.einsum('mn,n...->m...', mask, stack, precision=lax.Precision.HIGHEST)]
    all_to_all x0 -> x2, waiting for transfers between devices: none -> 19.3 us  [entering(): lax.all_to_all(parts, 'chip', 0, 0, tiled=True)]
    all_to_all x0 -> x2, starting transfers between devices: none -> 13.4 us  [entering(): lax.all_to_all(parts, 'chip', 0, 0, tiled=True)]
    ppermute x0 -> x4, starting transfers between devices: none -> 13.2 us  [the longest x2 7.36 us: entering(): theirs = lax.ppermute(pair + jnp.where(ahead, mine, 0.0), 'core', swap)]
    pallas_call x0 -> x6, Pallas kernels: none -> 8.1 us  [the longest x1 2.89 us: on_device(): call(backward_kernel, (wide, wide))(queries, keys, values, delta, state)]
  transfers between devices with their start and end apart: 2 -> 6, of which waited for: 2 -> 6; matrix products, arithmetic and copies ran while one was open for 5% -> 0% of each run, Pallas kernels for 0% -> 0%
where the time goes in v1:
time: 107 us; the launch traced here: 106 us
  blocking collectives  41.1 us (38%)
  starting transfers between devices  26.6 us (25%)
  waiting for transfers between devices  23.9 us (22%)
  Pallas kernels  8.1 us (8%)
  local copies, waits for them, and re-layouts  5.47 us (5%)
    all_to_all x2, blocking collectives, entering(): parts = lax.all_to_all(parts, 'chip', 0, 0, tiled=True)  32.7 us
    all_to_all x2, waiting for transfers between devices, entering(): lax.all_to_all(parts, 'chip', 0, 0, tiled=True)  19.3 us
    all_to_all x2, starting transfers between devices, entering(): lax.all_to_all(parts, 'chip', 0, 0, tiled=True)  13.4 us
    psum x1, blocking collectives, on_device(): sums = lax.psum(sums, 'head')  8.44 us
    ppermute x2, starting transfers between devices, entering(): theirs = lax.ppermute(pair + jnp.where(ahead, mine, 0.0), 'core', swap)  7.36 us
    ppermute x2, starting transfers between devices, entering(): got = lax.ppermute(other, 'core', swap)  5.81 us
    unnamed x18, local copies, waits for them, and re-layouts  5.42 us
    pallas_call x1, Pallas kernels, on_device(): call(backward_kernel, (wide, wide))(queries, keys, values, delta, state)  2.89 us
  transfers between devices with their start and end apart: 6, of which 6 were waited for; matrix products, arithmetic and copies ran while one was open for 0% of the time, Pallas kernels for 0%

profile of v1, /device:TPU:1, one launch (start us, length us, event | category | flops | bytes accessed | tf_op | source)
XLA Modules:
  0.0 106.2 jit_solution(17002513807619102087)
XLA Ops:
  0.6 0.0 copy-start
  0.6 1.0 copy-done
  1.7 0.0 copy-start.2
  1.7 1.0 copy-done.2
  2.7 0.3 shard_map.76
  3.1 3.3 %collective-permute-start = (f32[4,128,128]{2,1,0:T(8,128)S(1)}, f32[4,128,128]{2,1,0:T(8,128)S(1)}, u32[]{:S(2)}, u32[]{:S(2)}) collective-permute-start(f32[4,128,128]{2,1,0:T(8,128)S(1)} %constant_dynamic-slice_fusion.1), channel_id=1, source_target_pairs={{0,4},{4,0},{1,5},{5,1},{2,6},{6,2},{3,7},{7,3},{8,12},{12,8},{9,1... | collective-permute-start | bytes 786440 | tf_op jit(solution)/shard_map/ppermute | solution.py:132
  6.4 1.2 %collective-permute-done = f32[4,128,128]{2,1,0:T(8,128)S(1)} collective-permute-done((f32[4,128,128]{2,1,0:T(8,128)S(1)}, f32[4,128,128]{2,1,0:T(8,128)S(1)}, u32[]{:S(2)}, u32[]{:S(2)}) %collective-permute-start) | collective-permute-done | bytes 262176 | tf_op jit(solution)/shard_map/ppermute | solution.py:132
  7.6 18.9 %all_to_all.20.parts = f32[32,16,128]{2,1,0:T(8,128)S(1)} all-to-all(f32[32,16,128]{2,1,0:T(8,128)S(1)} %bitcast.12), channel_id=1, replica_groups=mesh['chip'=32,'core'=2,'head'=4] {'chip'}, dimensions={0} | all-to-all | bytes 524288 | tf_op jit(solution)/shard_map/all_to_all | solution.py:134
  26.6 0.7 shard_map.77
  27.3 6.7 %all-to-all-start.1 = ((f32[32,16,128]{2,1,0:T(8,128)}), f32[32,16,128]{2,1,0:T(8,128)S(1)}, u32[]{:S(2)}, u32[]{:S(2)}) async-start(f32[32,16,128]{2,1,0:T(8,128)} %shard_map.77), calls=%async_computation.1 | async-start | bytes 524288 | tf_op jit(solution)/shard_map/all_to_all | solution.py:138
  34.1 9.6 %all-to-all-done.1 = f32[32,16,128]{2,1,0:T(8,128)S(1)} async-done(((f32[32,16,128]{2,1,0:T(8,128)}), f32[32,16,128]{2,1,0:T(8,128)S(1)}, u32[]{:S(2)}, u32[]{:S(2)}) %all-to-all-start.1) | async-done | bytes 262176 | tf_op jit(solution)/shard_map/all_to_all | solution.py:138
  43.7 0.0 copy-start.8
  43.7 0.0 copy-start.4
  43.7 0.0 copy-start.5
  43.8 3.7 %collective-permute-start.1 = (f32[4,128,128]{2,1,0:T(8,128)S(1)}, f32[4,128,128]{2,1,0:T(8,128)S(1)}, u32[]{:S(2)}, u32[]{:S(2)}) collective-permute-start(f32[4,128,128]{2,1,0:T(8,128)S(1)} %get-tuple-element.22), channel_id=1, source_target_pairs={{0,4},{4,0},{1,5},{5,1},{2,6},{6,2},{3,7},{7,3},{8,12},{12,8},{9,1... | collective-permute-start | bytes 786440 | tf_op jit(solution)/shard_map/ppermute | solution.py:141
  47.4 0.0 copy-done.8
  47.4 1.2 %collective-permute-done.1 = f32[4,128,128]{2,1,0:T(8,128)S(1)} collective-permute-done((f32[4,128,128]{2,1,0:T(8,128)S(1)}, f32[4,128,128]{2,1,0:T(8,128)S(1)}, u32[]{:S(2)}, u32[]{:S(2)}) %collective-permute-start.1) | collective-permute-done | bytes 262176 | tf_op jit(solution)/shard_map/ppermute | solution.py:141
  48.6 0.0 copy-start.1
  48.6 0.0 copy-start.3
  48.6 0.0 copy-done.4
  48.7 0.0 copy-done.5
  48.7 1.0 copy-done.1
  49.6 0.2 copy-done.3
  49.8 1.3 %shard_map.78 = (f32[256,1024]{1,0:T(8,128)S(1)}, bf16[8,128,128]{2,1,0:T(8,128)(2,1)S(1)}, f32[2,256]{1,0:T(2,128)S(1)}) custom-call(bf16[256,1024]{1,0:T(8,128)(2,1)S(1)} %copy-done.4, bf16[256,1024]{1,0:T(8,128)(2,1)S(1)} %copy-done.1, bf16[256,1024]{1,0:T(8,128)(2,1)S(1)} %copy-done.3, bf16[256,1024]{1,0:T(8,128)(2,1)S(1)} %copy-done.5, ...), custom_call_target="tpu_custom_call" | custom-call | tf_op jit(solution)/shard_map/pallas_call | solution.py:155
  51.1 0.0 copy-start.6
  51.1 1.0 copy-done.6
  52.1 8.4 %psum.7.sums = f32[2,256]{1,0:T(2,128)S(1)} all-reduce(f32[2,256]{1,0:T(2,128)S(1)} %get-tuple-element.13), channel_id=1, replica_groups=mesh['chip'=32,'core'=2,'head'=4] {'head'}, use_global_device_ids=true, to_apply=%region_0.1 | all-reduce | flops 512 | bytes 4096 | tf_op jit(solution)/shard_map/psum | solution.py:163
  60.5 0.0 copy-start.7
  60.5 1.2 %copy-done.7 = f32[256,1024]{1,0:T(8,128)S(1)} copy-done((f32[256,1024]{1,0:T(8,128)S(1)}, f32[256,1024]{1,0:T(8,128)}, u32[]{:S(2)}) %copy-start.7) | copy-done | bytes 1048600
  61.7 2.1 %shard_map.79 = (bf16[256,1024]{1,0:T(8,128)(2,1)S(1)}, f32[8,128,128]{2,1,0:T(8,128)S(1)}, bf16[256,1024]{1,0:T(8,128)(2,1)}) custom-call(bf16[256,1024]{1,0:T(8,128)(2,1)S(1)} %copy-done.4, bf16[256,1024]{1,0:T(8,128)(2,1)S(1)} %copy-done.1, bf16[256,1024]{1,0:T(8,128)(2,1)S(1)} %copy-done.3, bf16[256,1024]{1,0:T(8,128)(2,1)S(1)} %copy-done.5, ...), custom_call_target="tpu_custom_call" | custom-call | tf_op jit(solution)/shard_map/pallas_call | solution.py:164
  63.9 2.5 %collective-permute-start.2 = (f32[4,128,128]{2,1,0:T(8,128)S(1)}, f32[4,128,128]{2,1,0:T(8,128)S(1)}, u32[]{:S(2)}, u32[]{:S(2)}) collective-permute-start(f32[4,128,128]{2,1,0:T(8,128)S(1)} %constant_dynamic-slice_fusion), channel_id=1, source_target_pairs={{0,4},{4,0},{1,5},{5,1},{2,6},{6,2},{3,7},{7,3},{8,12},{12,8},{9,1... | collective-permute-start | bytes 786440 | tf_op jit(solution)/shard_map/ppermute | solution.py:132
  66.3 1.2 %collective-permute-done.2 = f32[4,128,128]{2,1,0:T(8,128)S(1)} collective-permute-done((f32[4,128,128]{2,1,0:T(8,128)S(1)}, f32[4,128,128]{2,1,0:T(8,128)S(1)}, u32[]{:S(2)}, u32[]{:S(2)}) %collective-permute-start.2) | collective-permute-done | bytes 262176 | tf_op jit(solution)/shard_map/ppermute | solution.py:132
  67.5 13.8 %all_to_all.21.parts = f32[32,16,128]{2,1,0:T(8,128)S(1)} all-to-all(f32[32,16,128]{2,1,0:T(8,128)S(1)} %bitcast.13), channel_id=1, replica_groups=mesh['chip'=32,'core'=2,'head'=4] {'chip'}, dimensions={0} | all-to-all | bytes 524288 | tf_op jit(solution)/shard_map/all_to_all | solution.py:134
  81.3 0.7 shard_map.80
  82.0 6.7 %all-to-all-start.3 = ((f32[32,16,128]{2,1,0:T(8,128)}), f32[32,16,128]{2,1,0:T(8,128)S(1)}, u32[]{:S(2)}, u32[]{:S(2)}) async-start(f32[32,16,128]{2,1,0:T(8,128)} %shard_map.80), calls=%async_computation.3 | async-start | bytes 524288 | tf_op jit(solution)/shard_map/all_to_all | solution.py:138
  88.8 9.7 %all-to-all-done.3 = f32[32,16,128]{2,1,0:T(8,128)S(1)} async-done(((f32[32,16,128]{2,1,0:T(8,128)}), f32[32,16,128]{2,1,0:T(8,128)S(1)}, u32[]{:S(2)}, u32[]{:S(2)}) %all-to-all-start.3) | async-done | bytes 262176 | tf_op jit(solution)/shard_map/all_to_all | solution.py:138
  98.5 3.7 %collective-permute-start.3 = (f32[4,128,128]{2,1,0:T(8,128)S(1)}, f32[4,128,128]{2,1,0:T(8,128)S(1)}, u32[]{:S(2)}, u32[]{:S(2)}) collective-permute-start(f32[4,128,128]{2,1,0:T(8,128)S(1)} %get-tuple-element.20), channel_id=1, source_target_pairs={{0,4},{4,0},{1,5},{5,1},{2,6},{6,2},{3,7},{7,3},{8,12},{12,8},{9,1... | collective-permute-start | bytes 786440 | tf_op jit(solution)/shard_map/ppermute | solution.py:141
  102.1 1.2 %collective-permute-done.3 = f32[4,128,128]{2,1,0:T(8,128)S(1)} collective-permute-done((f32[4,128,128]{2,1,0:T(8,128)S(1)}, f32[4,128,128]{2,1,0:T(8,128)S(1)}, u32[]{:S(2)}, u32[]{:S(2)}) %collective-permute-start.3) | collective-permute-done | bytes 262176 | tf_op jit(solution)/shard_map/ppermute | solution.py:141
  103.3 2.9 %shard_map.81 = (bf16[256,1024]{1,0:T(8,128)(2,1)}, bf16[256,1024]{1,0:T(8,128)(2,1)}) custom-call(bf16[256,1024]{1,0:T(8,128)(2,1)S(1)} %copy-done.4, bf16[256,1024]{1,0:T(8,128)(2,1)S(1)} %copy-done.1, bf16[256,1024]{1,0:T(8,128)(2,1)S(1)} %copy-done.3, bf16[256,1024]{1,0:T(8,128)(2,1)S(1)} %get-tuple-element.15.delta, ...), custom_call_target="tpu_custom_call" | custom-call | tf_op jit(solution)/shard_map/pallas_call | solution.py:168
  (9 shorter events, 0.3 us)
Async XLA Ops:
  0.6 1.0 copy-start
  1.7 1.0 copy-start.2
  3.1 4.5 %collective-permute-start = (f32[4,128,128]{2,1,0:T(8,128)S(1)}, f32[4,128,128]{2,1,0:T(8,128)S(1)}, u32[]{:S(2)}, u32[]{:S(2)}) collective-permute-start(f32[4,128,128]{2,1,0:T(8,128)S(1)} %constant_dynamic-slice_fusion.1), channel_id=1, source_target_pairs={{0,4},{4,0},{1,5},{5,1},{2,6},{6,2},{3,7},{7,3},{8,12},{12,8},{9,1... | collective-permute-start | bytes 786440 | tf_op jit(solution)/shard_map/ppermute | solution.py:132
  27.3 16.4 %all-to-all-start.1 = ((f32[32,16,128]{2,1,0:T(8,128)}), f32[32,16,128]{2,1,0:T(8,128)S(1)}, u32[]{:S(2)}, u32[]{:S(2)}) async-start(f32[32,16,128]{2,1,0:T(8,128)} %shard_map.77), calls=%async_computation.1 | async-start | bytes 524288 | tf_op jit(solution)/shard_map/all_to_all | solution.py:138
  43.7 3.7 %copy-start.8 = (bf16[1024]{0:T(1024)(128)(2,1)S(1)}, bf16[1024]{0:T(1024)(128)(2,1)}, u32[]{:S(2)}) copy-start(bf16[1024]{0:T(1024)(128)(2,1)} %param.9) | copy-start | bytes 6148
  43.7 4.9 %copy-start.4 = (bf16[256,1024]{1,0:T(8,128)(2,1)S(1)}, bf16[256,1024]{1,0:T(8,128)(2,1)}, u32[]{:S(2)}) copy-start(bf16[256,1024]{1,0:T(8,128)(2,1)} %queries.5) | copy-start | bytes 1572868
  43.7 5.0 %copy-start.5 = (bf16[256,1024]{1,0:T(8,128)(2,1)S(1)}, bf16[256,1024]{1,0:T(8,128)(2,1)}, u32[]{:S(2)}) copy-start(bf16[256,1024]{1,0:T(8,128)(2,1)} %out_grad.3) | copy-start | bytes 1572868
  43.8 4.8 %collective-permute-start.1 = (f32[4,128,128]{2,1,0:T(8,128)S(1)}, f32[4,128,128]{2,1,0:T(8,128)S(1)}, u32[]{:S(2)}, u32[]{:S(2)}) collective-permute-start(f32[4,128,128]{2,1,0:T(8,128)S(1)} %get-tuple-element.22), channel_id=1, source_target_pairs={{0,4},{4,0},{1,5},{5,1},{2,6},{6,2},{3,7},{7,3},{8,12},{12,8},{9,1... | collective-permute-start | bytes 786440 | tf_op jit(solution)/shard_map/ppermute | solution.py:141
  48.6 1.0 copy-start.1
  48.6 1.2 %copy-start.3 = (bf16[256,1024]{1,0:T(8,128)(2,1)S(1)}, bf16[256,1024]{1,0:T(8,128)(2,1)}, u32[]{:S(2)}) copy-start(bf16[256,1024]{1,0:T(8,128)(2,1)} %values.7) | copy-start | bytes 1572868
  51.1 1.0 copy-start.6
  60.5 1.2 %copy-start.7 = (f32[256,1024]{1,0:T(8,128)S(1)}, f32[256,1024]{1,0:T(8,128)}, u32[]{:S(2)}) copy-start(f32[256,1024]{1,0:T(8,128)} %copy-done.6) | copy-start | bytes 3145732
  63.9 3.6 %collective-permute-start.2 = (f32[4,128,128]{2,1,0:T(8,128)S(1)}, f32[4,128,128]{2,1,0:T(8,128)S(1)}, u32[]{:S(2)}, u32[]{:S(2)}) collective-permute-start(f32[4,128,128]{2,1,0:T(8,128)S(1)} %constant_dynamic-slice_fusion), channel_id=1, source_target_pairs={{0,4},{4,0},{1,5},{5,1},{2,6},{6,2},{3,7},{7,3},{8,12},{12,8},{9,1... | collective-permute-start | bytes 786440 | tf_op jit(solution)/shard_map/ppermute | solution.py:132
  82.0 16.4 %all-to-all-start.3 = ((f32[32,16,128]{2,1,0:T(8,128)}), f32[32,16,128]{2,1,0:T(8,128)S(1)}, u32[]{:S(2)}, u32[]{:S(2)}) async-start(f32[32,16,128]{2,1,0:T(8,128)} %shard_map.80), calls=%async_computation.3 | async-start | bytes 524288 | tf_op jit(solution)/shard_map/all_to_all | solution.py:138
  98.5 4.8 %collective-permute-start.3 = (f32[4,128,128]{2,1,0:T(8,128)S(1)}, f32[4,128,128]{2,1,0:T(8,128)S(1)}, u32[]{:S(2)}, u32[]{:S(2)}) collective-permute-start(f32[4,128,128]{2,1,0:T(8,128)S(1)} %get-tuple-element.20), channel_id=1, source_target_pairs={{0,4},{4,0},{1,5},{5,1},{2,6},{6,2},{3,7},{7,3},{8,12},{12,8},{9,1... | collective-permute-start | bytes 786440 | tf_op jit(solution)/shard_map/ppermute | solution.py:141

commit v2 on v1

v2 whole, which is shorter than its diff:
```python
import functools

import jax
import jax.numpy as jnp
from jax import lax
from jax.experimental import pallas as pl
from jax.experimental.pallas import tpu as pltpu
from jax.sharding import Mesh
from jax.sharding import PartitionSpec as P

HEADS = 32
HEAD_DIM = 128
EPSILON = 1e-05
FEATURES = HEADS * HEAD_DIM
FACTOR = HEAD_DIM ** (-0.5)
F32 = jnp.float32
BF16 = jnp.bfloat16
VMEM_LIMIT = 16 * 1024 * 1024


def dot_nn(a, b):
    return lax.dot_general(a, b, (((1,), (0,)), ((), ())), preferred_element_type=F32)


def dot_nt(a, b):
    return lax.dot_general(a, b, (((1,), (1,)), ((), ())), preferred_element_type=F32)


def dot_tn(a, b):
    return lax.dot_general(a, b, (((0,), (0,)), ((), ())), preferred_element_type=F32)


def columns(head):
    return pl.ds(head * HEAD_DIM, HEAD_DIM)


def causal(count, transposed):
    row = lax.broadcasted_iota(jnp.int32, (count, count), 0)
    col = lax.broadcasted_iota(jnp.int32, (count, count), 1)
    return row <= col if transposed else col <= row


def scores(a, b, mask):
    return jnp.where(mask, dot_nt(a, b) * FACTOR, 0.0).astype(BF16)


def here(name):
    return lax.axis_index(name)


def near(shape, dtype=F32):
    return pltpu.VMEM(shape, dtype)


def call(kernel, out_shape, far=0, **kwargs):
    def run(*operands):
        spaces = [pltpu.HBM] * far + [pltpu.VMEM] * (len(operands) - far)
        return pl.pallas_call(
            kernel,
            out_shape=out_shape,
            in_specs=[pl.BlockSpec(memory_space=space) for space in spaces],
            compiler_params=pltpu.CompilerParams(vmem_limit_bytes=VMEM_LIMIT),
            **kwargs,
        )(*map(pltpu.with_memory_space_constraint, operands, spaces))

    return run


def totals_kernel(keys_far, values_far, mine, other, keys, values, sems):
    heads = mine.shape[0]
    half = heads * HEAD_DIM
    copies = []
    for part in range(2):
        core = here("core") if part else 1 - here("core")
        there = pl.ds(pl.multiple_of(core * half, half), half)
        at = pl.ds(part * half, half)
        pair = []
        for which, (source, target) in enumerate(((keys_far, keys), (values_far, values))):
            copy = pltpu.make_async_copy(
                source.at[:, there], target.at[:, at], sems.at[part, which]
            )
            copy.start()
            pair.append(copy)
        copies.append(pair)
    for part, out in enumerate((other, mine)):
        for copy in copies[part]:
            copy.wait()
        for head in range(heads):
            at = columns(part * heads + head)
            out[head] = dot_tn(keys[:, at], values[:, at])


def within_kernel(
    queries_far, keys_far, values_far, grad_far, gain_far, after,
    within, upstream, queries, keys, values, grad, gain, sems,
):
    del after
    copies = [
        pltpu.make_async_copy(far, near, sems.at[at])
        for at, (far, near) in enumerate(
            (
                (queries_far, queries),
                (keys_far, keys),
                (values_far, values),
                (grad_far, grad),
                (gain_far, gain),
            )
        )
    ]
    for copy in copies:
        copy.start()
    mask = causal(queries.shape[0], False)
    for copy in copies:
        copy.wait()
    for head in range(queries.shape[1] // HEAD_DIM):
        at = columns(head)
        within[:, at] = dot_nn(scores(queries[:, at], keys[:, at], mask), values[:, at])
        upstream[:, at] = grad[:, at].astype(F32) * gain[:, at].astype(F32)


def split_kernel(mine, got, *pieces):
    for step, piece in enumerate(pieces):
        at = owner() ^ step
        piece[...] = mine[at] + got[at]


def join_kernel(count, *refs):
    total = refs[0][...]
    for ref in refs[1:count]:
        total = total + ref[...]
    refs[-1][...] = total


def members_kernel(reverse, group, rows, *refs):
    parts, refs = refs[:group], refs[group:]
    mirror, there, outs = refs[0], refs[1:rows], refs[rows:]
    row, low, high = here("row"), here("low"), here("high")
    ahead = jnp.where(before(1 - high, high, reverse), mirror[...], 0.0)
    for step in range(1, rows):
        sooner = before(row ^ step, row, reverse)
        ahead = ahead + jnp.where(sooner, there[step - 1][...], 0.0)
    for at, out in enumerate(outs):
        result = ahead
        for step in range(group):
            if step != at:
                sooner = before(low ^ step, low ^ at, reverse)
                result = result + jnp.where(sooner, parts[step][...], 0.0)
        out[...] = result


def merge_kernel(reverse, group, *refs):
    back, (mine, got, own, theirs) = refs[:group], refs[group:]
    first = before(here("core"), 1 - here("core"), reverse)
    for step in range(group):
        at = owner() ^ step
        own[at] = back[step][...] + jnp.where(first, 0.0, got[at])
        theirs[at] = back[step][...] + jnp.where(first, mine[at], 0.0)


def by_head(own, theirs, refs=False):
    half = own.shape[0]
    for part, states in enumerate((own, theirs)):
        core = 1 - here("core") if part else here("core")
        for at in range(half):
            head = core * half + at
            yield head, pl.ds(pl.multiple_of(head * HEAD_DIM, HEAD_DIM), HEAD_DIM), states.at[at] if refs else states[at]


def forward_kernel(queries, upstream, within, own, theirs, output, low, sums):
    tokens = queries.shape[0]
    square = jnp.zeros((tokens, HEAD_DIM), F32)
    mixed = jnp.zeros((tokens, HEAD_DIM), F32)
    for head, at, state in by_head(own, theirs):
        state_low = state.astype(BF16)
        low[head] = state_low
        out = within[:, at] + FACTOR * dot_nn(queries[:, at], state_low)
        output[:, at] = out
        square = square + out * out
        mixed = mixed + upstream[:, at] * out
    sums[0:1] = jnp.sum(square.T, axis=0, keepdims=True)
    sums[1:2] = jnp.sum(mixed.T, axis=0, keepdims=True)


def delta_kernel(queries, upstream, output, sums, sums_1, sums_2, sums_3, delta, mine, other):
    tokens = queries.shape[0]
    total = sums[...] + sums_1[...] + sums_2[...] + sums_3[...]
    inv_rms = lax.rsqrt(total[0:1] / FEATURES + EPSILON)
    pull = inv_rms * inv_rms * inv_rms * (total[1:2] / FEATURES)
    inv_rms = jnp.broadcast_to(inv_rms, (HEAD_DIM, tokens)).T
    pull = jnp.broadcast_to(pull, (HEAD_DIM, tokens)).T
    for head, at, back in by_head(mine, other, True):
        out_delta = (inv_rms * upstream[:, at] - pull * output[:, at]).astype(BF16)
        delta[:, at] = out_delta
        back[...] = dot_tn(out_delta, queries[:, at])


def query_kernel(keys, values, delta, low, after, query_grad):
    del after
    mask = causal(keys.shape[0], False)
    for head in range(low.shape[0]):
        at = columns(head)
        out_delta = delta[:, at]
        delta_scores = scores(out_delta, values[:, at], mask)
        grad = dot_nn(delta_scores, keys[:, at]) + FACTOR * dot_nt(out_delta, low[head])
        query_grad[:, at] = grad.astype(BF16)


def inner_kernel(queries, keys, values, delta, after, key_inner, value_inner):
    del after
    mask = causal(keys.shape[0], True)
    for head in range(queries.shape[1] // HEAD_DIM):
        at = columns(head)
        query, out_delta = queries[:, at], delta[:, at]
        key_inner[:, at] = dot_nn(scores(values[:, at], out_delta, mask), query)
        value_inner[:, at] = dot_nn(scores(keys[:, at], query, mask), out_delta)


def backward_kernel(keys, values, key_inner, value_inner, own, theirs, key_grad, value_grad):
    for _, at, state in by_head(own, theirs):
        later_low = state.astype(BF16)
        grad = key_inner[:, at] + FACTOR * dot_nn(values[:, at], later_low)
        key_grad[:, at] = grad.astype(BF16)
        grad = value_inner[:, at] + FACTOR * dot_nt(keys[:, at], later_low)
        value_grad[:, at] = grad.astype(BF16)


def swap(array, axis, distance):
    count = lax.axis_size(axis)
    return lax.ppermute(array, axis, [(at, at ^ distance) for at in range(count)])


def before(one, other, reverse):
    return one > other if reverse else one < other


def owner():
    return here("low") ^ ((lax.axis_size("low") - 1) * here("high"))


def entering(mine, other, reverse, beside):
    group, rows = lax.axis_size("low"), lax.axis_size("row")
    piece = near(mine.shape[1:])
    got = swap(other, "core", 1)
    parts = call(split_kernel, [piece] * group)(mine, got)
    made = beside(parts[0])
    parts = [parts[0]] + [swap(parts[step], "low", step) for step in range(1, group)]
    whole = call(functools.partial(join_kernel, group), piece)(*parts, *made)
    mirror = swap(whole, ("high", "low"), 2 * group - 1)
    whole = call(functools.partial(join_kernel, 2), piece)(whole, mirror)
    there = [swap(whole, "row", step) for step in range(1, rows)]
    back = call(functools.partial(members_kernel, reverse, group, rows), [piece] * group)(
        *parts, mirror, *there
    )
    back = [back[0]] + [swap(back[step], "low", step) for step in range(1, group)]
    half = near(mine.shape)
    own, theirs = call(functools.partial(merge_kernel, reverse, group), (half, half))(
        *back, mine, got
    )
    return own, swap(theirs, "core", 1), made


def on_device(queries, keys, values, out_grad, gain):
    tokens, width = queries.shape
    heads = width // HEAD_DIM
    gain = gain.reshape(1, width)
    wide = near((tokens, width), BF16)
    full = near((tokens, width))
    half = near((heads // 2, HEAD_DIM, HEAD_DIM))
    mine, other = call(
        totals_kernel,
        (half, half),
        far=2,
        scratch_shapes=[wide, wide, pltpu.SemaphoreType.DMA((2, 2))],
    )(keys, values)

    def beside_forward(after):
        return call(
            within_kernel,
            (full, full, wide, wide, wide),
            far=5,
            scratch_shapes=[wide, near((1, width), BF16), pltpu.SemaphoreType.DMA((5,))],
        )(queries, keys, values, out_grad, gain, after)

    own, theirs, (within, upstream, queries, keys, values) = entering(
        mine, other, False, beside_forward
    )
    output, low, sums = call(
        forward_kernel,
        (full, near((heads, HEAD_DIM, HEAD_DIM), BF16), near((2, tokens))),
    )(queries, upstream, within, own, theirs)
    others = [swap(sums, "head", step) for step in range(1, lax.axis_size("head"))]
    delta, mine, other = call(delta_kernel, (wide, half, half))(
        queries, upstream, output, sums, *others
    )

    def beside_backward(after):
        query_grad = call(query_kernel, wide)(keys, values, delta, low, after)
        inner = call(inner_kernel, (full, full))(queries, keys, values, delta, after)
        return query_grad, *inner

    own, theirs, (query_grad, key_inner, value_inner) = entering(
        mine, other, True, beside_backward
    )
    grads = jax.ShapeDtypeStruct((tokens, width), BF16)
    key_grad, value_grad = call(backward_kernel, (grads, grads))(
        keys, values, key_inner, value_inner, own, theirs
    )
    return query_grad, key_grad, value_grad


def solution(mesh):
    _, across = mesh.devices.shape
    shape = (4, 2, 4, 2, across)
    inner = Mesh(mesh.devices.reshape(shape), ("row", "high", "low", "core", "head"))
    spec = P(("row", "high", "low", "core"), "head")
    return jax.shard_map(
        on_device,
        mesh=inner,
        in_specs=(spec, spec, spec, spec, P("head")),
        out_specs=(spec, spec, spec),
        check_vma=False,
    )
```

time: 107 us -> 91.1 us (0.85)
  blocking collectives: 41.1 us -> 0 us
  starting transfers between devices: 26.6 us -> 51.9 us
  local copies, waits for them, and re-layouts: 5.47 us -> 1.4 us
  waiting for transfers between devices: 23.9 us -> 26.7 us
  Pallas kernels: 8.1 us -> 10.2 us
    ppermute x4 -> x27, starting transfers between devices: 13.2 us -> 51.9 us  [swap(): lax.ppermute(array, axis, [(at, at ^ distance) for at in range(count)])]
    all_to_all x2 -> x0, blocking collectives: 32.7 us -> none  [entering(): parts = lax.all_to_all(parts, 'chip', 0, 0, tiled=True)]
    ppermute x4 -> x27, waiting for transfers between devices: 4.64 us -> 26.7 us  [swap(): lax.ppermute(array, axis, [(at, at ^ distance) for at in range(count)])]
    all_to_all x2 -> x0, waiting for transfers between devices: 19.3 us -> none  [entering(): lax.all_to_all(parts, 'chip', 0, 0, tiled=True)]
    all_to_all x2 -> x0, starting transfers between devices: 13.4 us -> none  [entering(): lax.all_to_all(parts, 'chip', 0, 0, tiled=True)]
    psum x1 -> x0, blocking collectives: 8.44 us -> none  [on_device(): sums = lax.psum(sums, 'head')]
    unnamed x18 -> x3, local copies, waits for them, and re-layouts: 5.42 us -> 0.8 us
    pallas_call x6 -> x17, Pallas kernels: 8.1 us -> 10.2 us  [run(): pl.pallas_call(kernel, out_shape=out_shape, in_specs=[pl.BlockSpec(memory...]
  transfers between devices with their start and end apart: 6 -> 27, of which waited for: 6 -> 19; matrix products, arithmetic and copies ran while one was open for 0% -> 2% of each run, Pallas kernels for 0% -> 6%
where the time goes in v2:
time: 91.1 us; the launch traced here: 90.9 us
  starting transfers between devices  51.9 us (57%)
  waiting for transfers between devices  26.7 us (29%)
  Pallas kernels  10.2 us (11%)
  local copies, waits for them, and re-layouts  1.4 us (2%)
    ppermute x27, starting transfers between devices, swap(): lax.ppermute(array, axis, [(at, at ^ distance) for at in range(count)])  51.9 us
    ppermute x27, waiting for transfers between devices, swap(): lax.ppermute(array, axis, [(at, at ^ distance) for at in range(count)])  26.7 us
    pallas_call x17, Pallas kernels, run(): pl.pallas_call(kernel, out_shape=out_shape, in_specs=[pl.BlockSpec(memory...  10.2 us
  transfers between devices with their start and end apart: 27, of which 19 were waited for; matrix products, arithmetic and copies ran while one was open for 2% of the time, Pallas kernels for 6%

profile of v2, /device:TPU:1, one launch (start us, length us, event | category | flops | bytes accessed | tf_op | source)
XLA Modules:
  0.0 90.9 jit_solution(16478016248989436509)
XLA Ops:
  0.6 1.6 %shard_map.76 = (f32[4,128,128]{2,1,0:T(8,128)S(1)}, f32[4,128,128]{2,1,0:T(8,128)S(1)}) custom-call(bf16[256,1024]{1,0:T(8,128)(2,1)} %keys_far.3, bf16[256,1024]{1,0:T(8,128)(2,1)} %values_far.3), custom_call_target="tpu_custom_call" | custom-call | tf_op jit(solution)/shard_map/pallas_call | solution.py:58
  2.3 3.3 %collective-permute-start = (f32[4,128,128]{2,1,0:T(8,128)S(1)}, f32[4,128,128]{2,1,0:T(8,128)S(1)}, u32[]{:S(2)}, u32[]{:S(2)}) collective-permute-start(f32[4,128,128]{2,1,0:T(8,128)S(1)} %get-tuple-element.41), channel_id=1, source_target_pairs={{0,4},{4,0},{1,5},{5,1},{2,6},{6,2},{3,7},{7,3},{8,12},{12,8},{9,1... | collective-permute-start | bytes 786440 | tf_op jit(solution)/shard_map/ppermute | solution.py:229
  5.6 1.2 %collective-permute-done.got.refs_5_ = f32[4,128,128]{2,1,0:T(8,128)S(1)} collective-permute-done((f32[4,128,128]{2,1,0:T(8,128)S(1)}, f32[4,128,128]{2,1,0:T(8,128)S(1)}, u32[]{:S(2)}, u32[]{:S(2)}) %collective-permute-start) | collective-permute-done | bytes 262176 | tf_op jit(solution)/shard_map/ppermute | solution.py:229
  6.9 2.9 %collective-permute-start.2 = (f32[128,128]{1,0:T(8,128)S(1)}, f32[128,128]{1,0:T(8,128)S(1)}, u32[]{:S(2)}, u32[]{:S(2)}) collective-permute-start(f32[128,128]{1,0:T(8,128)S(1)} %get-tuple-element.49), channel_id=1, source_target_pairs={{0,16},{8,24},{16,0},{24,8},{1,17},{9,25},{17,1},{25,9},{2,18},{10... | collective-permute-start | bytes 196616 | tf_op jit(solution)/shard_map/ppermute | solution.py:229
  9.8 0.7 collective-permute-start.3
  10.4 0.6 reshape.9.gain_far
  11.0 2.6 %shard_map.78 = (f32[256,1024]{1,0:T(8,128)S(1)}, f32[256,1024]{1,0:T(8,128)S(1)}, bf16[256,1024]{1,0:T(8,128)(2,1)S(1)}, bf16[256,1024]{1,0:T(8,128)(2,1)S(1)}, bf16[256,1024]{1,0:T(8,128)(2,1)S(1)}) custom-call(bf16[256,1024]{1,0:T(8,128)(2,1)} %queries_far.1, bf16[256,1024]{1,0:T(8,128)(2,1)} %keys_far.3, bf16[256,1024]{1,0:T(8,128)(2,1)} %values_far.3, ...), custom_call_target="tpu_custom_call" | custom-call | tf_op jit(solution)/shard_map/pallas_call | solution.py:58
  13.7 1.1 %collective-permute-done.3.refs_3_ = f32[128,128]{1,0:T(8,128)S(1)} collective-permute-done((f32[128,128]{1,0:T(8,128)S(1)}, f32[128,128]{1,0:T(8,128)S(1)}, u32[]{:S(2)}, u32[]{:S(2)}) %collective-permute-start.3) | collective-permute-done | bytes 65568 | tf_op jit(solution)/shard_map/ppermute | solution.py:229
  14.8 3.0 %collective-permute-start.4 = (f32[128,128]{1,0:T(8,128)S(1)}, f32[128,128]{1,0:T(8,128)S(1)}, u32[]{:S(2)}, u32[]{:S(2)}) collective-permute-start(f32[128,128]{1,0:T(8,128)S(1)} %shard_map.79.refs_0_), channel_id=1, source_target_pairs={{0,56},{8,48},{16,40},{24,32},{32,24},{40,16},{48,8},{56,0},{1,57}... | collective-permute-start | bytes 196616 | tf_op jit(solution)/shard_map/ppermute | solution.py:229
  17.8 1.7 %collective-permute-done.4.refs_1_.refs_4_ = f32[128,128]{1,0:T(8,128)S(1)} collective-permute-done((f32[128,128]{1,0:T(8,128)S(1)}, f32[128,128]{1,0:T(8,128)S(1)}, u32[]{:S(2)}, u32[]{:S(2)}) %collective-permute-start.4) | collective-permute-done | bytes 65568 | tf_op jit(solution)/shard_map/ppermute | solution.py:229
  19.5 1.4 %collective-permute-start.5 = (f32[128,128]{1,0:T(8,128)S(1)}, f32[128,128]{1,0:T(8,128)S(1)}, u32[]{:S(2)}, u32[]{:S(2)}) collective-permute-start(f32[128,128]{1,0:T(8,128)S(1)} %shard_map.80), channel_id=1, source_target_pairs={{0,64},{64,0},{128,192},{192,128},{1,65},{65,1},{129,193},{193,129... | collective-permute-start | bytes 196616 | tf_op jit(solution)/shard_map/ppermute | solution.py:229
  20.9 2.6 %collective-permute-start.6 = (f32[128,128]{1,0:T(8,128)S(1)}, f32[128,128]{1,0:T(8,128)S(1)}, u32[]{:S(2)}, u32[]{:S(2)}) collective-permute-start(f32[128,128]{1,0:T(8,128)S(1)} %shard_map.80), channel_id=1, source_target_pairs={{0,128},{64,192},{128,0},{192,64},{1,129},{65,193},{129,1},{193,65... | collective-permute-start | bytes 196616 | tf_op jit(solution)/shard_map/ppermute | solution.py:229
  23.5 2.3 %collective-permute-done.6.refs_6_ = f32[128,128]{1,0:T(8,128)S(1)} collective-permute-done((f32[128,128]{1,0:T(8,128)S(1)}, f32[128,128]{1,0:T(8,128)S(1)}, u32[]{:S(2)}, u32[]{:S(2)}) %collective-permute-start.6) | collective-permute-done | bytes 65568 | tf_op jit(solution)/shard_map/ppermute | solution.py:229
  25.9 2.0 %collective-permute-done.7.refs_7_ = f32[128,128]{1,0:T(8,128)S(1)} collective-permute-done((f32[128,128]{1,0:T(8,128)S(1)}, f32[128,128]{1,0:T(8,128)S(1)}, u32[]{:S(2)}, u32[]{:S(2)}) %collective-permute-start.7) | collective-permute-done | bytes 65568 | tf_op jit(solution)/shard_map/ppermute | solution.py:229
  27.9 1.8 %collective-permute-start.10 = (f32[128,128]{1,0:T(8,128)S(1)}, f32[128,128]{1,0:T(8,128)S(1)}, u32[]{:S(2)}, u32[]{:S(2)}) collective-permute-start(f32[128,128]{1,0:T(8,128)S(1)} %get-tuple-element.54), channel_id=1, source_target_pairs={{0,24},{8,16},{16,8},{24,0},{1,25},{9,17},{17,9},{25,1},{2,26},{10... | collective-permute-start | bytes 196616 | tf_op jit(solution)/shard_map/ppermute | solution.py:229
  29.7 2.1 %collective-permute-start.8 = (f32[128,128]{1,0:T(8,128)S(1)}, f32[128,128]{1,0:T(8,128)S(1)}, u32[]{:S(2)}, u32[]{:S(2)}) collective-permute-start(f32[128,128]{1,0:T(8,128)S(1)} %get-tuple-element.52), channel_id=1, source_target_pairs={{0,8},{8,0},{16,24},{24,16},{1,9},{9,1},{17,25},{25,17},{2,10},{10... | collective-permute-start | bytes 196616 | tf_op jit(solution)/shard_map/ppermute | solution.py:229
  32.3 0.7 collective-permute-done.10.refs_3_
  32.9 0.7 collective-permute-done.8.refs_1_
  33.6 2.9 %collective-permute-done.9.refs_2_ = f32[128,128]{1,0:T(8,128)S(1)} collective-permute-done((f32[128,128]{1,0:T(8,128)S(1)}, f32[128,128]{1,0:T(8,128)S(1)}, u32[]{:S(2)}, u32[]{:S(2)}) %collective-permute-start.9) | collective-permute-done | bytes 65568 | tf_op jit(solution)/shard_map/ppermute | solution.py:229
  36.6 6.0 %collective-permute-start.11 = (f32[4,128,128]{2,1,0:T(8,128)S(1)}, f32[4,128,128]{2,1,0:T(8,128)S(1)}, u32[]{:S(2)}, u32[]{:S(2)}) collective-permute-start(f32[4,128,128]{2,1,0:T(8,128)S(1)} %get-tuple-element.56), channel_id=1, source_target_pairs={{0,4},{4,0},{1,5},{5,1},{2,6},{6,2},{3,7},{7,3},{8,12},{12,8},{9,1... | collective-permute-start | bytes 786440 | tf_op jit(solution)/shard_map/ppermute | solution.py:229
  42.6 1.2 %collective-permute-done.11.theirs = f32[4,128,128]{2,1,0:T(8,128)S(1)} collective-permute-done((f32[4,128,128]{2,1,0:T(8,128)S(1)}, f32[4,128,128]{2,1,0:T(8,128)S(1)}, u32[]{:S(2)}, u32[]{:S(2)}) %collective-permute-start.11) | collective-permute-done | bytes 262176 | tf_op jit(solution)/shard_map/ppermute | solution.py:229
  43.8 0.6 shard_map.83
  44.4 1.3 %collective-permute-start.12 = (f32[2,256]{1,0:T(2,128)S(1)}, f32[2,256]{1,0:T(2,128)S(1)}, u32[]{:S(2)}, u32[]{:S(2)}) collective-permute-start(f32[2,256]{1,0:T(2,128)S(1)} %get-tuple-element.58.sums), channel_id=1, source_target_pairs={{0,1},{1,0},{2,3},{3,2},{4,5},{5,4},{6,7},{7,6},{8,9},{9,8},{10,11... | collective-permute-start | bytes 6152 | tf_op jit(solution)/shard_map/ppermute | solution.py:229
  45.7 2.4 %collective-permute-start.13 = (f32[2,256]{1,0:T(2,128)S(1)}, f32[2,256]{1,0:T(2,128)S(1)}, u32[]{:S(2)}, u32[]{:S(2)}) collective-permute-start(f32[2,256]{1,0:T(2,128)S(1)} %get-tuple-element.58.sums), channel_id=1, source_target_pairs={{0,2},{1,3},{2,0},{3,1},{4,6},{5,7},{6,4},{7,5},{8,10},{9,11},{10,... | collective-permute-start | bytes 6152 | tf_op jit(solution)/shard_map/ppermute | solution.py:229
  48.4 1.3 %collective-permute-done.13.sums_2 = f32[2,256]{1,0:T(2,128)S(1)} collective-permute-done((f32[2,256]{1,0:T(2,128)S(1)}, f32[2,256]{1,0:T(2,128)S(1)}, u32[]{:S(2)}, u32[]{:S(2)}) %collective-permute-start.13) | collective-permute-done | bytes 2080 | tf_op jit(solution)/shard_map/ppermute | solution.py:229
  49.7 2.1 %collective-permute-done.14.sums_3 = f32[2,256]{1,0:T(2,128)S(1)} collective-permute-done((f32[2,256]{1,0:T(2,128)S(1)}, f32[2,256]{1,0:T(2,128)S(1)}, u32[]{:S(2)}, u32[]{:S(2)}) %collective-permute-start.14) | collective-permute-done | bytes 2080 | tf_op jit(solution)/shard_map/ppermute | solution.py:229
  51.8 0.7 shard_map.84
  52.6 2.2 %collective-permute-start.15 = (f32[4,128,128]{2,1,0:T(8,128)S(1)}, f32[4,128,128]{2,1,0:T(8,128)S(1)}, u32[]{:S(2)}, u32[]{:S(2)}) collective-permute-start(f32[4,128,128]{2,1,0:T(8,128)S(1)} %get-tuple-element.62), channel_id=1, source_target_pairs={{0,4},{4,0},{1,5},{5,1},{2,6},{6,2},{3,7},{7,3},{8,12},{12,8},{9,1... | collective-permute-start | bytes 786440 | tf_op jit(solution)/shard_map/ppermute | solution.py:229
  54.7 1.2 %collective-permute-done.15.got.refs_5_ = f32[4,128,128]{2,1,0:T(8,128)S(1)} collective-permute-done((f32[4,128,128]{2,1,0:T(8,128)S(1)}, f32[4,128,128]{2,1,0:T(8,128)S(1)}, u32[]{:S(2)}, u32[]{:S(2)}) %collective-permute-start.15) | collective-permute-done | bytes 262176 | tf_op jit(solution)/shard_map/ppermute | solution.py:229
  56.2 1.7 %collective-permute-start.17 = (f32[128,128]{1,0:T(8,128)S(1)}, f32[128,128]{1,0:T(8,128)S(1)}, u32[]{:S(2)}, u32[]{:S(2)}) collective-permute-start(f32[128,128]{1,0:T(8,128)S(1)} %get-tuple-element.67), channel_id=1, source_target_pairs={{0,16},{8,24},{16,0},{24,8},{1,17},{9,25},{17,1},{25,9},{2,18},{10... | collective-permute-start | bytes 196616 | tf_op jit(solution)/shard_map/ppermute | solution.py:229
  57.9 1.8 %collective-permute-start.18 = (f32[128,128]{1,0:T(8,128)S(1)}, f32[128,128]{1,0:T(8,128)S(1)}, u32[]{:S(2)}, u32[]{:S(2)}) collective-permute-start(f32[128,128]{1,0:T(8,128)S(1)} %get-tuple-element.68), channel_id=1, source_target_pairs={{0,24},{8,16},{16,8},{24,0},{1,25},{9,17},{17,9},{25,1},{2,26},{10... | collective-permute-start | bytes 196616 | tf_op jit(solution)/shard_map/ppermute | solution.py:229
  59.7 1.5 %shard_map.87 = (f32[256,1024]{1,0:T(8,128)S(1)}, f32[256,1024]{1,0:T(8,128)S(1)}) custom-call(bf16[256,1024]{1,0:T(8,128)(2,1)S(1)} %get-tuple-element.45.refs_6_.queries, bf16[256,1024]{1,0:T(8,128)(2,1)S(1)} %get-tuple-element.43.refs_7_.keys, bf16[256,1024]{1,0:T(8,128)(2,1)S(1)} %get-tuple-element.44.refs_8_.values, ...), custom_call_target="tpu_custom_call" | custom-call | tf_op jit(solution)/shard_map/pallas_call | solution.py:58
  61.2 1.1 %shard_map.86.refs_4_ = bf16[256,1024]{1,0:T(8,128)(2,1)S(1)} custom-call(bf16[256,1024]{1,0:T(8,128)(2,1)S(1)} %get-tuple-element.43.refs_7_.keys, bf16[256,1024]{1,0:T(8,128)(2,1)S(1)} %get-tuple-element.44.refs_8_.values, bf16[256,1024]{1,0:T(8,128)(2,1)S(1)} %get-tuple-element.59.delta, bf16[8,128,128]{2,1,0:T(8,128)(2,1)S(1)} %get-tuple-element.60.low, ...), custom_call_target="tpu_custom_call" | custom-call | tf_op jit(solution)/shard_map/pallas_call | solution.py:58
  62.3 0.9 collective-permute-done.18.refs_3_
  63.2 3.4 %collective-permute-start.19 = (f32[128,128]{1,0:T(8,128)S(1)}, f32[128,128]{1,0:T(8,128)S(1)}, u32[]{:S(2)}, u32[]{:S(2)}) collective-permute-start(f32[128,128]{1,0:T(8,128)S(1)} %shard_map.88.refs_0_), channel_id=1, source_target_pairs={{0,56},{8,48},{16,40},{24,32},{32,24},{40,16},{48,8},{56,0},{1,57}... | collective-permute-start | bytes 196616 | tf_op jit(solution)/shard_map/ppermute | solution.py:229
  66.7 1.7 %collective-permute-done.19.refs_1_.refs_4_ = f32[128,128]{1,0:T(8,128)S(1)} collective-permute-done((f32[128,128]{1,0:T(8,128)S(1)}, f32[128,128]{1,0:T(8,128)S(1)}, u32[]{:S(2)}, u32[]{:S(2)}) %collective-permute-start.19) | collective-permute-done | bytes 65568 | tf_op jit(solution)/shard_map/ppermute | solution.py:229
  68.4 1.2 %collective-permute-start.21 = (f32[128,128]{1,0:T(8,128)S(1)}, f32[128,128]{1,0:T(8,128)S(1)}, u32[]{:S(2)}, u32[]{:S(2)}) collective-permute-start(f32[128,128]{1,0:T(8,128)S(1)} %shard_map.89), channel_id=1, source_target_pairs={{0,128},{64,192},{128,0},{192,64},{1,129},{65,193},{129,1},{193,65... | collective-permute-start | bytes 196616 | tf_op jit(solution)/shard_map/ppermute | solution.py:229
  69.6 2.7 %collective-permute-start.22 = (f32[128,128]{1,0:T(8,128)S(1)}, f32[128,128]{1,0:T(8,128)S(1)}, u32[]{:S(2)}, u32[]{:S(2)}) collective-permute-start(f32[128,128]{1,0:T(8,128)S(1)} %shard_map.89), channel_id=1, source_target_pairs={{0,192},{64,128},{128,64},{192,0},{1,193},{65,129},{129,65},{193,1... | collective-permute-start | bytes 196616 | tf_op jit(solution)/shard_map/ppermute | solution.py:229
  72.3 0.9 collective-permute-done.21.refs_6_
  73.1 0.8 collective-permute-done.22.refs_7_
  74.0 2.7 %collective-permute-start.23 = (f32[128,128]{1,0:T(8,128)S(1)}, f32[128,128]{1,0:T(8,128)S(1)}, u32[]{:S(2)}, u32[]{:S(2)}) collective-permute-start(f32[128,128]{1,0:T(8,128)S(1)} %get-tuple-element.70), channel_id=1, source_target_pairs={{0,8},{8,0},{16,24},{24,16},{1,9},{9,1},{17,25},{25,17},{2,10},{10... | collective-permute-start | bytes 196616 | tf_op jit(solution)/shard_map/ppermute | solution.py:229
  76.7 1.0 %collective-permute-start.24 = (f32[128,128]{1,0:T(8,128)S(1)}, f32[128,128]{1,0:T(8,128)S(1)}, u32[]{:S(2)}, u32[]{:S(2)}) collective-permute-start(f32[128,128]{1,0:T(8,128)S(1)} %get-tuple-element.71), channel_id=1, source_target_pairs={{0,16},{8,24},{16,0},{24,8},{1,17},{9,25},{17,1},{25,9},{2,18},{10... | collective-permute-start | bytes 196616 | tf_op jit(solution)/shard_map/ppermute | solution.py:229
  77.7 1.2 %collective-permute-start.25 = (f32[128,128]{1,0:T(8,128)S(1)}, f32[128,128]{1,0:T(8,128)S(1)}, u32[]{:S(2)}, u32[]{:S(2)}) collective-permute-start(f32[128,128]{1,0:T(8,128)S(1)} %get-tuple-element.72), channel_id=1, source_target_pairs={{0,24},{8,16},{16,8},{24,0},{1,25},{9,17},{17,9},{25,1},{2,26},{10... | collective-permute-start | bytes 196616 | tf_op jit(solution)/shard_map/ppermute | solution.py:229
  78.9 2.5 %collective-permute-done.24.refs_2_ = f32[128,128]{1,0:T(8,128)S(1)} collective-permute-done((f32[128,128]{1,0:T(8,128)S(1)}, f32[128,128]{1,0:T(8,128)S(1)}, u32[]{:S(2)}, u32[]{:S(2)}) %collective-permute-start.24) | collective-permute-done | bytes 65568 | tf_op jit(solution)/shard_map/ppermute | solution.py:229
  81.4 1.4 %collective-permute-done.25.refs_3_ = f32[128,128]{1,0:T(8,128)S(1)} collective-permute-done((f32[128,128]{1,0:T(8,128)S(1)}, f32[128,128]{1,0:T(8,128)S(1)}, u32[]{:S(2)}, u32[]{:S(2)}) %collective-permute-start.25) | collective-permute-done | bytes 65568 | tf_op jit(solution)/shard_map/ppermute | solution.py:229
  82.9 5.4 %collective-permute-start.26 = (f32[4,128,128]{2,1,0:T(8,128)S(1)}, f32[4,128,128]{2,1,0:T(8,128)S(1)}, u32[]{:S(2)}, u32[]{:S(2)}) collective-permute-start(f32[4,128,128]{2,1,0:T(8,128)S(1)} %get-tuple-element.74), channel_id=1, source_target_pairs={{0,4},{4,0},{1,5},{5,1},{2,6},{6,2},{3,7},{7,3},{8,12},{12,8},{9,1... | collective-permute-start | bytes 786440 | tf_op jit(solution)/shard_map/ppermute | solution.py:229
  88.2 0.8 copy.8
  89.4 1.5 %shard_map.92 = (bf16[256,1024]{1,0:T(8,128)(2,1)}, bf16[256,1024]{1,0:T(8,128)(2,1)}) custom-call(bf16[256,1024]{1,0:T(8,128)(2,1)S(1)} %get-tuple-element.43.refs_7_.keys, bf16[256,1024]{1,0:T(8,128)(2,1)S(1)} %get-tuple-element.44.refs_8_.values, f32[256,1024]{1,0:T(8,128)S(1)} %get-tuple-element.64.refs_5_.key_inner, ...), custom_call_target="tpu_custom_call" | custom-call | tf_op jit(solution)/shard_map/pallas_call | solution.py:58
  (27 shorter events, 1.9 us)
Async XLA Ops:
  2.3 4.5 %collective-permute-start = (f32[4,128,128]{2,1,0:T(8,128)S(1)}, f32[4,128,128]{2,1,0:T(8,128)S(1)}, u32[]{:S(2)}, u32[]{:S(2)}) collective-permute-start(f32[4,128,128]{2,1,0:T(8,128)S(1)} %get-tuple-element.41), channel_id=1, source_target_pairs={{0,4},{4,0},{1,5},{5,1},{2,6},{6,2},{3,7},{7,3},{8,12},{12,8},{9,1... | collective-permute-start | bytes 786440 | tf_op jit(solution)/shard_map/ppermute | solution.py:229
  6.8 3.6 %copy-start = (bf16[1024]{0:T(1024)(128)(2,1)S(1)}, bf16[1024]{0:T(1024)(128)(2,1)}, u32[]{:S(2)}) copy-start(bf16[1024]{0:T(1024)(128)(2,1)} %param.9) | copy-start | bytes 6148
  6.8 6.9 %collective-permute-start.1 = (f32[128,128]{1,0:T(8,128)S(1)}, f32[128,128]{1,0:T(8,128)S(1)}, u32[]{:S(2)}, u32[]{:S(2)}) collective-permute-start(f32[128,128]{1,0:T(8,128)S(1)} %get-tuple-element.48), channel_id=1, source_target_pairs={{0,8},{8,0},{16,24},{24,16},{1,9},{9,1},{17,25},{25,17},{2,10},{10... | collective-permute-start | bytes 196616 | tf_op jit(solution)/shard_map/ppermute | solution.py:229
  6.9 6.8 %collective-permute-start.2 = (f32[128,128]{1,0:T(8,128)S(1)}, f32[128,128]{1,0:T(8,128)S(1)}, u32[]{:S(2)}, u32[]{:S(2)}) collective-permute-start(f32[128,128]{1,0:T(8,128)S(1)} %get-tuple-element.49), channel_id=1, source_target_pairs={{0,16},{8,24},{16,0},{24,8},{1,17},{9,25},{17,1},{25,9},{2,18},{10... | collective-permute-start | bytes 196616 | tf_op jit(solution)/shard_map/ppermute | solution.py:229
  9.8 5.0 %collective-permute-start.3 = (f32[128,128]{1,0:T(8,128)S(1)}, f32[128,128]{1,0:T(8,128)S(1)}, u32[]{:S(2)}, u32[]{:S(2)}) collective-permute-start(f32[128,128]{1,0:T(8,128)S(1)} %get-tuple-element.50), channel_id=1, source_target_pairs={{0,24},{8,16},{16,8},{24,0},{1,25},{9,17},{17,9},{25,1},{2,26},{10... | collective-permute-start | bytes 196616 | tf_op jit(solution)/shard_map/ppermute | solution.py:229
  14.8 4.7 %collective-permute-start.4 = (f32[128,128]{1,0:T(8,128)S(1)}, f32[128,128]{1,0:T(8,128)S(1)}, u32[]{:S(2)}, u32[]{:S(2)}) collective-permute-start(f32[128,128]{1,0:T(8,128)S(1)} %shard_map.79.refs_0_), channel_id=1, source_target_pairs={{0,56},{8,48},{16,40},{24,32},{32,24},{40,16},{48,8},{56,0},{1,57}... | collective-permute-start | bytes 196616 | tf_op jit(solution)/shard_map/ppermute | solution.py:229
  19.5 4.0 %collective-permute-start.5 = (f32[128,128]{1,0:T(8,128)S(1)}, f32[128,128]{1,0:T(8,128)S(1)}, u32[]{:S(2)}, u32[]{:S(2)}) collective-permute-start(f32[128,128]{1,0:T(8,128)S(1)} %shard_map.80), channel_id=1, source_target_pairs={{0,64},{64,0},{128,192},{192,128},{1,65},{65,1},{129,193},{193,129... | collective-permute-start | bytes 196616 | tf_op jit(solution)/shard_map/ppermute | solution.py:229
  20.9 5.0 %collective-permute-start.6 = (f32[128,128]{1,0:T(8,128)S(1)}, f32[128,128]{1,0:T(8,128)S(1)}, u32[]{:S(2)}, u32[]{:S(2)}) collective-permute-start(f32[128,128]{1,0:T(8,128)S(1)} %shard_map.80), channel_id=1, source_target_pairs={{0,128},{64,192},{128,0},{192,64},{1,129},{65,193},{129,1},{193,65... | collective-permute-start | bytes 196616 | tf_op jit(solution)/shard_map/ppermute | solution.py:229
  23.5 4.3 %collective-permute-start.7 = (f32[128,128]{1,0:T(8,128)S(1)}, f32[128,128]{1,0:T(8,128)S(1)}, u32[]{:S(2)}, u32[]{:S(2)}) collective-permute-start(f32[128,128]{1,0:T(8,128)S(1)} %shard_map.80), channel_id=1, source_target_pairs={{0,192},{64,128},{128,64},{192,0},{1,193},{65,129},{129,65},{193,1... | collective-permute-start | bytes 196616 | tf_op jit(solution)/shard_map/ppermute | solution.py:229
  27.9 5.0 %collective-permute-start.10 = (f32[128,128]{1,0:T(8,128)S(1)}, f32[128,128]{1,0:T(8,128)S(1)}, u32[]{:S(2)}, u32[]{:S(2)}) collective-permute-start(f32[128,128]{1,0:T(8,128)S(1)} %get-tuple-element.54), channel_id=1, source_target_pairs={{0,24},{8,16},{16,8},{24,0},{1,25},{9,17},{17,9},{25,1},{2,26},{10... | collective-permute-start | bytes 196616 | tf_op jit(solution)/shard_map/ppermute | solution.py:229
  29.7 3.9 %collective-permute-start.8 = (f32[128,128]{1,0:T(8,128)S(1)}, f32[128,128]{1,0:T(8,128)S(1)}, u32[]{:S(2)}, u32[]{:S(2)}) collective-permute-start(f32[128,128]{1,0:T(8,128)S(1)} %get-tuple-element.52), channel_id=1, source_target_pairs={{0,8},{8,0},{16,24},{24,16},{1,9},{9,1},{17,25},{25,17},{2,10},{10... | collective-permute-start | bytes 196616 | tf_op jit(solution)/shard_map/ppermute | solution.py:229
  31.8 4.7 %collective-permute-start.9 = (f32[128,128]{1,0:T(8,128)S(1)}, f32[128,128]{1,0:T(8,128)S(1)}, u32[]{:S(2)}, u32[]{:S(2)}) collective-permute-start(f32[128,128]{1,0:T(8,128)S(1)} %get-tuple-element.53), channel_id=1, source_target_pairs={{0,16},{8,24},{16,0},{24,8},{1,17},{9,25},{17,1},{25,9},{2,18},{10... | collective-permute-start | bytes 196616 | tf_op jit(solution)/shard_map/ppermute | solution.py:229
  36.6 7.2 %collective-permute-start.11 = (f32[4,128,128]{2,1,0:T(8,128)S(1)}, f32[4,128,128]{2,1,0:T(8,128)S(1)}, u32[]{:S(2)}, u32[]{:S(2)}) collective-permute-start(f32[4,128,128]{2,1,0:T(8,128)S(1)} %get-tuple-element.56), channel_id=1, source_target_pairs={{0,4},{4,0},{1,5},{5,1},{2,6},{6,2},{3,7},{7,3},{8,12},{12,8},{9,1... | collective-permute-start | bytes 786440 | tf_op jit(solution)/shard_map/ppermute | solution.py:229
  44.4 3.9 %collective-permute-start.12 = (f32[2,256]{1,0:T(2,128)S(1)}, f32[2,256]{1,0:T(2,128)S(1)}, u32[]{:S(2)}, u32[]{:S(2)}) collective-permute-start(f32[2,256]{1,0:T(2,128)S(1)} %get-tuple-element.58.sums), channel_id=1, source_target_pairs={{0,1},{1,0},{2,3},{3,2},{4,5},{5,4},{6,7},{7,6},{8,9},{9,8},{10,11... | collective-permute-start | bytes 6152 | tf_op jit(solution)/shard_map/ppermute | solution.py:229
  45.7 3.9 %collective-permute-start.13 = (f32[2,256]{1,0:T(2,128)S(1)}, f32[2,256]{1,0:T(2,128)S(1)}, u32[]{:S(2)}, u32[]{:S(2)}) collective-permute-start(f32[2,256]{1,0:T(2,128)S(1)} %get-tuple-element.58.sums), channel_id=1, source_target_pairs={{0,2},{1,3},{2,0},{3,1},{4,6},{5,7},{6,4},{7,5},{8,10},{9,11},{10,... | collective-permute-start | bytes 6152 | tf_op jit(solution)/shard_map/ppermute | solution.py:229
  48.2 3.6 %collective-permute-start.14 = (f32[2,256]{1,0:T(2,128)S(1)}, f32[2,256]{1,0:T(2,128)S(1)}, u32[]{:S(2)}, u32[]{:S(2)}) collective-permute-start(f32[2,256]{1,0:T(2,128)S(1)} %get-tuple-element.58.sums), channel_id=1, source_target_pairs={{0,3},{1,2},{2,1},{3,0},{4,7},{5,6},{6,5},{7,4},{8,11},{9,10},{10,... | collective-permute-start | bytes 6152 | tf_op jit(solution)/shard_map/ppermute | solution.py:229
  52.6 3.3 %collective-permute-start.15 = (f32[4,128,128]{2,1,0:T(8,128)S(1)}, f32[4,128,128]{2,1,0:T(8,128)S(1)}, u32[]{:S(2)}, u32[]{:S(2)}) collective-permute-start(f32[4,128,128]{2,1,0:T(8,128)S(1)} %get-tuple-element.62), channel_id=1, source_target_pairs={{0,4},{4,0},{1,5},{5,1},{2,6},{6,2},{3,7},{7,3},{8,12},{12,8},{9,1... | collective-permute-start | bytes 786440 | tf_op jit(solution)/shard_map/ppermute | solution.py:229
  55.9 6.4 %collective-permute-start.16 = (f32[128,128]{1,0:T(8,128)S(1)}, f32[128,128]{1,0:T(8,128)S(1)}, u32[]{:S(2)}, u32[]{:S(2)}) collective-permute-start(f32[128,128]{1,0:T(8,128)S(1)} %get-tuple-element.66), channel_id=1, source_target_pairs={{0,8},{8,0},{16,24},{24,16},{1,9},{9,1},{17,25},{25,17},{2,10},{10... | collective-permute-start | bytes 196616 | tf_op jit(solution)/shard_map/ppermute | solution.py:229
  56.2 6.1 %collective-permute-start.17 = (f32[128,128]{1,0:T(8,128)S(1)}, f32[128,128]{1,0:T(8,128)S(1)}, u32[]{:S(2)}, u32[]{:S(2)}) collective-permute-start(f32[128,128]{1,0:T(8,128)S(1)} %get-tuple-element.67), channel_id=1, source_target_pairs={{0,16},{8,24},{16,0},{24,8},{1,17},{9,25},{17,1},{25,9},{2,18},{10... | collective-permute-start | bytes 196616 | tf_op jit(solution)/shard_map/ppermute | solution.py:229
  57.9 5.3 %collective-permute-start.18 = (f32[128,128]{1,0:T(8,128)S(1)}, f32[128,128]{1,0:T(8,128)S(1)}, u32[]{:S(2)}, u32[]{:S(2)}) collective-permute-start(f32[128,128]{1,0:T(8,128)S(1)} %get-tuple-element.68), channel_id=1, source_target_pairs={{0,24},{8,16},{16,8},{24,0},{1,25},{9,17},{17,9},{25,1},{2,26},{10... | collective-permute-start | bytes 196616 | tf_op jit(solution)/shard_map/ppermute | solution.py:229
  63.2 5.1 %collective-permute-start.19 = (f32[128,128]{1,0:T(8,128)S(1)}, f32[128,128]{1,0:T(8,128)S(1)}, u32[]{:S(2)}, u32[]{:S(2)}) collective-permute-start(f32[128,128]{1,0:T(8,128)S(1)} %shard_map.88.refs_0_), channel_id=1, source_target_pairs={{0,56},{8,48},{16,40},{24,32},{32,24},{40,16},{48,8},{56,0},{1,57}... | collective-permute-start | bytes 196616 | tf_op jit(solution)/shard_map/ppermute | solution.py:229
  68.3 3.9 %collective-permute-start.20 = (f32[128,128]{1,0:T(8,128)S(1)}, f32[128,128]{1,0:T(8,128)S(1)}, u32[]{:S(2)}, u32[]{:S(2)}) collective-permute-start(f32[128,128]{1,0:T(8,128)S(1)} %shard_map.89), channel_id=1, source_target_pairs={{0,64},{64,0},{128,192},{192,128},{1,65},{65,1},{129,193},{193,129... | collective-permute-start | bytes 196616 | tf_op jit(solution)/shard_map/ppermute | solution.py:229
  68.4 4.7 %collective-permute-start.21 = (f32[128,128]{1,0:T(8,128)S(1)}, f32[128,128]{1,0:T(8,128)S(1)}, u32[]{:S(2)}, u32[]{:S(2)}) collective-permute-start(f32[128,128]{1,0:T(8,128)S(1)} %shard_map.89), channel_id=1, source_target_pairs={{0,128},{64,192},{128,0},{192,64},{1,129},{65,193},{129,1},{193,65... | collective-permute-start | bytes 196616 | tf_op jit(solution)/shard_map/ppermute | solution.py:229
  69.6 4.3 %collective-permute-start.22 = (f32[128,128]{1,0:T(8,128)S(1)}, f32[128,128]{1,0:T(8,128)S(1)}, u32[]{:S(2)}, u32[]{:S(2)}) collective-permute-start(f32[128,128]{1,0:T(8,128)S(1)} %shard_map.89), channel_id=1, source_target_pairs={{0,192},{64,128},{128,64},{192,0},{1,193},{65,129},{129,65},{193,1... | collective-permute-start | bytes 196616 | tf_op jit(solution)/shard_map/ppermute | solution.py:229
  74.0 4.9 %collective-permute-start.23 = (f32[128,128]{1,0:T(8,128)S(1)}, f32[128,128]{1,0:T(8,128)S(1)}, u32[]{:S(2)}, u32[]{:S(2)}) collective-permute-start(f32[128,128]{1,0:T(8,128)S(1)} %get-tuple-element.70), channel_id=1, source_target_pairs={{0,8},{8,0},{16,24},{24,16},{1,9},{9,1},{17,25},{25,17},{2,10},{10... | collective-permute-start | bytes 196616 | tf_op jit(solution)/shard_map/ppermute | solution.py:229
  76.7 4.7 %collective-permute-start.24 = (f32[128,128]{1,0:T(8,128)S(1)}, f32[128,128]{1,0:T(8,128)S(1)}, u32[]{:S(2)}, u32[]{:S(2)}) collective-permute-start(f32[128,128]{1,0:T(8,128)S(1)} %get-tuple-element.71), channel_id=1, source_target_pairs={{0,16},{8,24},{16,0},{24,8},{1,17},{9,25},{17,1},{25,9},{2,18},{10... | collective-permute-start | bytes 196616 | tf_op jit(solution)/shard_map/ppermute | solution.py:229
  77.7 5.1 %collective-permute-start.25 = (f32[128,128]{1,0:T(8,128)S(1)}, f32[128,128]{1,0:T(8,128)S(1)}, u32[]{:S(2)}, u32[]{:S(2)}) collective-permute-start(f32[128,128]{1,0:T(8,128)S(1)} %get-tuple-element.72), channel_id=1, source_target_pairs={{0,24},{8,16},{16,8},{24,0},{1,25},{9,17},{17,9},{25,1},{2,26},{10... | collective-permute-start | bytes 196616 | tf_op jit(solution)/shard_map/ppermute | solution.py:229
  82.9 6.5 %collective-permute-start.26 = (f32[4,128,128]{2,1,0:T(8,128)S(1)}, f32[4,128,128]{2,1,0:T(8,128)S(1)}, u32[]{:S(2)}, u32[]{:S(2)}) collective-permute-start(f32[4,128,128]{2,1,0:T(8,128)S(1)} %get-tuple-element.74), channel_id=1, source_target_pairs={{0,4},{4,0},{1,5},{5,1},{2,6},{6,2},{3,7},{7,3},{8,12},{12,8},{9,1... | collective-permute-start | bytes 786440 | tf_op jit(solution)/shard_map/ppermute | solution.py:229

commit v3 on v2

v3 whole, which is shorter than its diff:
```python
import functools

import jax
import jax.numpy as jnp
from jax import lax
from jax.experimental import pallas as pl
from jax.experimental.pallas import tpu as pltpu
from jax.sharding import Mesh
from jax.sharding import PartitionSpec as P

HEADS = 32
HEAD_DIM = 128
EPSILON = 1e-05
FEATURES = HEADS * HEAD_DIM
FACTOR = HEAD_DIM ** (-0.5)
F32 = jnp.float32
BF16 = jnp.bfloat16
VMEM_LIMIT = 16 * 1024 * 1024


def dot_nn(a, b):
    return lax.dot_general(a, b, (((1,), (0,)), ((), ())), preferred_element_type=F32)


def dot_nt(a, b):
    return lax.dot_general(a, b, (((1,), (1,)), ((), ())), preferred_element_type=F32)


def dot_tn(a, b):
    return lax.dot_general(a, b, (((0,), (0,)), ((), ())), preferred_element_type=F32)


def columns(head):
    return pl.ds(head * HEAD_DIM, HEAD_DIM)


def causal(count, transposed):
    row = lax.broadcasted_iota(jnp.int32, (count, count), 0)
    col = lax.broadcasted_iota(jnp.int32, (count, count), 1)
    return row <= col if transposed else col <= row


def scores(a, b, mask):
    return jnp.where(mask, dot_nt(a, b) * FACTOR, 0.0).astype(BF16)


def here(name):
    return lax.axis_index(name)


def near(shape, dtype=F32):
    return pltpu.VMEM(shape, dtype)


def call(kernel, out_shape, far=0, loose=0, **kwargs):
    def run(*operands):
        close = len(operands) - far - loose
        spaces = [pltpu.HBM] * far + [pltpu.VMEM] * close + [pl.ANY] * loose
        return pl.pallas_call(
            kernel,
            out_shape=out_shape,
            in_specs=[pl.BlockSpec(memory_space=space) for space in spaces],
            compiler_params=pltpu.CompilerParams(vmem_limit_bytes=VMEM_LIMIT),
            **kwargs,
        )(*map(pltpu.with_memory_space_constraint, operands, spaces))

    return run


def halves(far, near, sems):
    half = far.shape[1] // 2
    result = []
    for part in range(2):
        core = 1 - here("core") if part else here("core")
        there = pl.ds(pl.multiple_of(core * half, half), half)
        result.append((far.at[:, there], near.at[:, pl.ds(part * half, half)], sems.at[part]))
    return result


def fetch(far, near, sems):
    return [pltpu.make_async_copy(there, at, sem) for there, at, sem in halves(far, near, sems)]


def totals_kernel(part, keys_far, values_far, out, keys, values, sems):
    chunks = sems.shape[1]
    rows = keys.shape[0] // chunks
    half = keys.shape[1]
    core = 1 - here("core") if part else here("core")
    there = pl.ds(pl.multiple_of(core * half, half), half)
    copies = []
    for chunk in range(chunks):
        at = pl.ds(chunk * rows, rows)
        for which, (far, near) in enumerate(((keys_far, keys), (values_far, values))):
            copy = pltpu.make_async_copy(far.at[at, there], near.at[at], sems.at[which, chunk])
            copy.start()
            copies.append(copy)
    for copy in copies:
        copy.wait()
    for head in range(out.shape[0]):
        at = columns(head)
        out[head] = dot_tn(keys[:, at], values[:, at])


def within_kernel(
    queries_far, grad_far, gain_far, keys_0, keys_1, values_0, values_1, after,
    within, upstream, queries, grad, gain, sems,
):
    del after
    copies = [
        fetch(queries_far, queries, sems.at[0]),
        fetch(grad_far, grad, sems.at[1]),
        fetch(gain_far, gain, sems.at[2]),
    ]
    for pair in copies:
        for copy in pair:
            copy.start()
    mask = causal(queries.shape[0], False)
    for pair in copies:
        for copy in pair:
            copy.wait()
    heads = queries.shape[1] // HEAD_DIM // 2
    for part, (keys, values) in enumerate(((keys_0, values_0), (keys_1, values_1))):
        for head in range(heads):
            at, near = columns(part * heads + head), columns(head)
            within[:, at] = dot_nn(scores(queries[:, at], keys[:, near], mask), values[:, near])
            upstream[:, at] = grad[:, at].astype(F32) * gain[:, at].astype(F32)


def split_kernel(mine, got, *pieces):
    for step, piece in enumerate(pieces):
        at = owner() ^ step
        piece[...] = mine[at] + got[at]


def join_kernel(skip, count, *refs):
    parts = refs[skip : skip + count]
    total = parts[0][...]
    for part in parts[1:]:
        total = total + part[...]
    refs[-1][...] = total


def members_kernel(reverse, group, rows, *refs):
    parts, refs = refs[:group], refs[group:]
    mirror, there, outs = refs[0], refs[1:rows], refs[rows:]
    row, low, high = here("row"), here("low"), here("high")
    ahead = jnp.where(before(1 - high, high, reverse), mirror[...], 0.0)
    for step in range(1, rows):
        sooner = before(row ^ step, row, reverse)
        ahead = ahead + jnp.where(sooner, there[step - 1][...], 0.0)
    for at, out in enumerate(outs):
        result = ahead
        for step in range(group):
            if step != at:
                sooner = before(low ^ step, low ^ at, reverse)
                result = result + jnp.where(sooner, parts[step][...], 0.0)
        out[...] = result


def merge_kernel(reverse, group, *refs):
    back, (mine, got, own, theirs) = refs[:group], refs[group:]
    first = before(here("core"), 1 - here("core"), reverse)
    for step in range(group):
        at = owner() ^ step
        own[at] = back[step][...] + jnp.where(first, 0.0, got[at])
        theirs[at] = back[step][...] + jnp.where(first, mine[at], 0.0)


def forward_kernel(part, queries, upstream, within, state, *refs):
    before_sums, (output, low, sums) = refs[:part], refs[part:]
    heads = state.shape[0]
    tokens = queries.shape[0]
    square = jnp.zeros((tokens, HEAD_DIM), F32)
    mixed = jnp.zeros((tokens, HEAD_DIM), F32)
    for head in range(heads):
        at = columns(part * heads + head)
        state_low = state[head].astype(BF16)
        low[head] = state_low
        out = within[:, at] + FACTOR * dot_nn(queries[:, at], state_low)
        output[:, columns(head)] = out
        square = square + out * out
        mixed = mixed + upstream[:, at] * out
    for row, array in enumerate((square, mixed)):
        total = jnp.sum(array.T, axis=0, keepdims=True)
        for ref in before_sums:
            total = total + ref[row : row + 1]
        sums[row : row + 1] = total


def delta_kernel(part, queries, upstream, output, sums, sums_1, sums_2, sums_3, delta, back):
    tokens = queries.shape[0]
    heads = back.shape[0]
    total = sums[...] + sums_1[...] + sums_2[...] + sums_3[...]
    inv_rms = lax.rsqrt(total[0:1] / FEATURES + EPSILON)
    pull = inv_rms * inv_rms * inv_rms * (total[1:2] / FEATURES)
    inv_rms = jnp.broadcast_to(inv_rms, (HEAD_DIM, tokens)).T
    pull = jnp.broadcast_to(pull, (HEAD_DIM, tokens)).T
    for head in range(heads):
        at = columns(part * heads + head)
        out_delta = inv_rms * upstream[:, at] - pull * output[:, columns(head)]
        out_delta = out_delta.astype(BF16)
        delta[:, columns(head)] = out_delta
        back[head] = dot_tn(out_delta, queries[:, at])


def write(near, far, part, sem):
    half = near.shape[1]
    core = 1 - here("core") if part else here("core")
    there = pl.ds(pl.multiple_of(core * half, half), half)
    copy = pltpu.make_async_copy(near, far.at[:, there], sem)
    copy.start()
    return copy


def query_kernel(*refs):
    *operands, _, far, near_0, near_1, sems = refs
    mask = causal(operands[0].shape[0], False)
    copies = []
    for part, near in enumerate((near_0, near_1)):
        keys, values, delta, low = operands[part::2]
        for head in range(low.shape[0]):
            at = columns(head)
            out_delta = delta[:, at]
            delta_scores = scores(out_delta, values[:, at], mask)
            grad = dot_nn(delta_scores, keys[:, at]) + FACTOR * dot_nt(out_delta, low[head])
            near[:, at] = grad.astype(BF16)
        copies.append(write(near, far, part, sems.at[part]))
    for copy in copies:
        copy.wait()


def inner_kernel(part, queries, keys, values, delta, after, key_inner, value_inner):
    del after
    mask = causal(keys.shape[0], True)
    heads = delta.shape[1] // HEAD_DIM
    for head in range(heads):
        at = columns(head)
        query, out_delta = queries[:, columns(part * heads + head)], delta[:, at]
        key_inner[:, at] = dot_nn(scores(values[:, at], out_delta, mask), query)
        value_inner[:, at] = dot_nn(scores(keys[:, at], query, mask), out_delta)


def key_value_grads(keys, values, key_inner, value_inner, state, key_near, value_near):
    lows = [state[head].astype(BF16) for head in range(state.shape[0])]
    for head, later_low in enumerate(lows):
        at = columns(head)
        grad = key_inner[:, at] + FACTOR * dot_nn(values[:, at], later_low)
        key_near[:, at] = grad.astype(BF16)
    yield
    for head, later_low in enumerate(lows):
        at = columns(head)
        grad = value_inner[:, at] + FACTOR * dot_nt(keys[:, at], later_low)
        value_near[:, at] = grad.astype(BF16)
    yield


def backward_kernel(*refs):
    for _ in key_value_grads(*refs):
        pass


def last_kernel(
    keys, values, key_inner, value_inner, state, key_0, value_0,
    key_far, value_far, key_1, value_1, sems,
):
    copies = [
        write(key_0, key_far, 0, sems.at[0]),
        write(value_0, value_far, 0, sems.at[1]),
    ]
    steps = key_value_grads(keys, values, key_inner, value_inner, state, key_1, value_1)
    next(steps)
    copies.append(write(key_1, key_far, 1, sems.at[2]))
    next(steps)
    copies.append(write(value_1, value_far, 1, sems.at[3]))
    for copy in copies:
        copy.wait()


def swap(array, axis, distance):
    count = lax.axis_size(axis)
    return lax.ppermute(array, axis, [(at, at ^ distance) for at in range(count)])


def before(one, other, reverse):
    return one > other if reverse else one < other


def owner():
    return here("low") ^ (lax.axis_size("low") // 2 * here("high"))


def swaps(arrays, axis, order):
    there = {step: swap(arrays[step], axis, step) for step in order}
    return [there[step] for step in sorted(there)]


def entering(mine, other, reverse, beside):
    group, rows = lax.axis_size("low"), lax.axis_size("row")
    line, ring = (3, 2, 1), (1, 3, 2)
    piece = near(mine.shape[1:])
    got = swap(other, "core", 1)
    parts = call(split_kernel, [piece] * group)(mine, got)
    made = beside(parts[0])
    parts = [parts[0]] + swaps(parts, "low", line)
    first, *ties = made
    whole = call(functools.partial(join_kernel, int(reverse), group), piece, far=int(reverse))(
        *((first, *parts) if reverse else (*parts, first)), *ties
    )
    mirror = swap(whole, ("high", "low"), group + group // 2)
    whole = call(functools.partial(join_kernel, 0, 2), piece)(whole, mirror)
    there = swaps([whole] * rows, "row", ring)
    back = call(functools.partial(members_kernel, reverse, group, rows), [piece] * group)(
        *parts, mirror, *there
    )
    back = [back[0]] + swaps(back, "low", line)
    half = near(mine.shape)
    own, theirs = call(functools.partial(merge_kernel, reverse, group), (half, half))(
        *back, mine, got
    )
    return (own, swap(theirs, "core", 1)), made


def on_device(queries, keys, values, out_grad, gain):
    tokens, width = queries.shape
    heads = width // HEAD_DIM
    gain = gain.reshape(1, width)
    wide = near((tokens, width), BF16)
    full = near((tokens, width))
    half = near((heads // 2, HEAD_DIM, HEAD_DIM))
    half_low = near(half.shape, BF16)
    half_wide = near((tokens, width // 2), BF16)
    half_full = near((tokens, width // 2))
    sums_shape = near((2, tokens))
    grads = pltpu.HBM((tokens, width), BF16)
    other, mine = (
        call(
            functools.partial(totals_kernel, part),
            (half, half_wide, half_wide),
            far=2,
            scratch_shapes=[pltpu.SemaphoreType.DMA((2, 4))],
        )(keys, values)
        for part in (1, 0)
    )
    mine, *near_0 = mine
    other, *near_1 = other
    keys, values = zip(near_0, near_1)

    def beside_forward(after):
        return call(
            within_kernel,
            (full, full, wide),
            far=3,
            scratch_shapes=[wide, near((1, width), BF16), pltpu.SemaphoreType.DMA((3, 2))],
        )(queries, out_grad, gain, *keys, *values, after)

    states, (within, upstream, queries) = entering(mine, other, False, beside_forward)
    outputs, lows, sums = [], [], []
    for part, state in enumerate(states):
        output, low, *sums = call(
            functools.partial(forward_kernel, part), (half_full, half_low, sums_shape)
        )(queries, upstream, within, state, *sums)
        outputs.append(output)
        lows.append(low)
    sums = swaps(sums * lax.axis_size("head"), "head", (1, 3, 2)) + sums
    deltas, backs = zip(
        *(
            call(functools.partial(delta_kernel, part), (half_wide, half))(
                queries, upstream, outputs[part], *sums
            )
            for part in (1, 0)
        )
    )
    deltas, backs = deltas[::-1], backs[::-1]

    def beside_backward(after):
        query_grad = call(
            query_kernel,
            grads,
            scratch_shapes=[half_wide, half_wide, pltpu.SemaphoreType.DMA((2,))],
        )(*keys, *values, *deltas, *lows, after)
        inner = [
            call(functools.partial(inner_kernel, part), (half_full, half_full))(
                queries, keys[part], values[part], deltas[part], after
            )
            for part in range(2)
        ]
        return query_grad, *inner[0], *inner[1]

    states, (query_grad, *inner) = entering(*backs, True, beside_backward)
    key_0, value_0 = call(backward_kernel, (half_wide, half_wide))(
        keys[0], values[0], *inner[:2], states[0]
    )
    key_grad, value_grad = call(
        last_kernel,
        (grads, grads),
        scratch_shapes=[half_wide, half_wide, pltpu.SemaphoreType.DMA((4,))],
    )(keys[1], values[1], *inner[2:], states[1], key_0, value_0)
    return query_grad, key_grad, value_grad


def solution(mesh):
    _, across = mesh.devices.shape
    shape = (4, 2, 4, 2, across)
    inner = Mesh(mesh.devices.reshape(shape), ("row", "high", "low", "core", "head"))
    spec = P(("row", "high", "low", "core"), "head")
    return jax.shard_map(
        on_device,
        mesh=inner,
        in_specs=(spec, spec, spec, spec, P("head")),
        out_specs=(spec, spec, spec),
        check_vma=False,
    )
```

time: 91.1 us -> 89 us (0.977)
  waiting for transfers between devices: 26.7 us -> 23.6 us
  Pallas kernels: 10.2 us -> 12.9 us
  starting transfers between devices: 51.9 us -> 50.6 us
    ppermute x27, waiting for transfers between devices: 26.7 us -> 23.6 us  [swap(): lax.ppermute(array, axis, [(at, at ^ distance) for at in range(count)])]
    pallas_call x17 -> x22, Pallas kernels: 10.2 us -> 12.9 us  [run(): pl.pallas_call(kernel, out_shape=out_shape, in_specs=[pl.BlockSpec(memory...]
    ppermute x27, starting transfers between devices: 51.9 us -> 50.6 us  [swap(): lax.ppermute(array, axis, [(at, at ^ distance) for at in range(count)])]
  transfers between devices with their start and end apart: 27 -> 27, of which waited for: 19 -> 16; matrix products, arithmetic and copies ran while one was open for 2% -> 1% of each run, Pallas kernels for 6% -> 10%
where the time goes in v3:
time: 89 us; the launch traced here: 88.7 us
  starting transfers between devices  50.6 us (57%)
  waiting for transfers between devices  23.6 us (27%)
  Pallas kernels  12.9 us (14%)
  between operations  1.01 us (1%)
    ppermute x27, starting transfers between devices, swap(): lax.ppermute(array, axis, [(at, at ^ distance) for at in range(count)])  50.6 us
    ppermute x27, waiting for transfers between devices, swap(): lax.ppermute(array, axis, [(at, at ^ distance) for at in range(count)])  23.6 us
    pallas_call x22, Pallas kernels, run(): pl.pallas_call(kernel, out_shape=out_shape, in_specs=[pl.BlockSpec(memory...  12.9 us
  transfers between devices with their start and end apart: 27, of which 16 were waited for; matrix products, arithmetic and copies ran while one was open for 1% of the time, Pallas kernels for 10%

profile of v3, /device:TPU:1, one launch (start us, length us, event | category | flops | bytes accessed | tf_op | source)
XLA Modules:
  0.0 88.7 jit_solution(18275928842808827569)
XLA Ops:
  0.6 1.4 %shard_map.77 = (f32[4,128,128]{2,1,0:T(8,128)S(1)}, bf16[256,512]{1,0:T(8,128)(2,1)S(1)}, bf16[256,512]{1,0:T(8,128)(2,1)S(1)}) custom-call(bf16[256,1024]{1,0:T(8,128)(2,1)} %keys_far.3, bf16[256,1024]{1,0:T(8,128)(2,1)} %values_far.3), custom_call_target="tpu_custom_call" | custom-call | tf_op jit(solution)/shard_map/pallas_call | solution.py:59
  2.0 3.3 %collective-permute-start = (f32[4,128,128]{2,1,0:T(8,128)S(1)}, f32[4,128,128]{2,1,0:T(8,128)S(1)}, u32[]{:S(2)}, u32[]{:S(2)}) collective-permute-start(f32[4,128,128]{2,1,0:T(8,128)S(1)} %get-tuple-element.55), channel_id=1, source_target_pairs={{0,4},{4,0},{1,5},{5,1},{2,6},{6,2},{3,7},{7,3},{8,12},{12,8},{9,1... | collective-permute-start | bytes 786440 | tf_op jit(solution)/shard_map/ppermute | solution.py:281
  5.4 1.4 %shard_map.76 = (f32[4,128,128]{2,1,0:T(8,128)S(1)}, bf16[256,512]{1,0:T(8,128)(2,1)S(1)}, bf16[256,512]{1,0:T(8,128)(2,1)S(1)}) custom-call(bf16[256,1024]{1,0:T(8,128)(2,1)} %keys_far.3, bf16[256,1024]{1,0:T(8,128)(2,1)} %values_far.3), custom_call_target="tpu_custom_call" | custom-call | tf_op jit(solution)/shard_map/pallas_call | solution.py:59
  7.0 2.9 %collective-permute-start.2 = (f32[128,128]{1,0:T(8,128)S(1)}, f32[128,128]{1,0:T(8,128)S(1)}, u32[]{:S(2)}, u32[]{:S(2)}) collective-permute-start(f32[128,128]{1,0:T(8,128)S(1)} %get-tuple-element.61), channel_id=1, source_target_pairs={{0,16},{8,24},{16,0},{24,8},{1,17},{9,25},{17,1},{25,9},{2,18},{10... | collective-permute-start | bytes 196616 | tf_op jit(solution)/shard_map/ppermute | solution.py:281
  9.9 0.7 collective-permute-start.3
  10.5 0.6 reshape.9.gain_far
  11.1 2.3 %shard_map.79 = (f32[256,1024]{1,0:T(8,128)S(1)}, f32[256,1024]{1,0:T(8,128)S(1)}, bf16[256,1024]{1,0:T(8,128)(2,1)S(1)}) custom-call(bf16[256,1024]{1,0:T(8,128)(2,1)} %queries_far.1, bf16[256,1024]{1,0:T(8,128)(2,1)} %grad_far.1, bf16[1,1024]{1,0:T(2,128)(2,1)} %reshape.9.gain_far, bf16[256,512]{1,0:T(8,128)(2,1)S(1)} %get-tuple-element.50.keys_0.refs_0_.keys, ...), custom_call_target="tpu_custom_call" | custom-call | tf_op jit(solution)/shard_map/pallas_call | solution.py:59
  13.4 1.4 %collective-permute-done.3.refs_3_ = f32[128,128]{1,0:T(8,128)S(1)} collective-permute-done((f32[128,128]{1,0:T(8,128)S(1)}, f32[128,128]{1,0:T(8,128)S(1)}, u32[]{:S(2)}, u32[]{:S(2)}) %collective-permute-start.3) | collective-permute-done | bytes 65568 | tf_op jit(solution)/shard_map/ppermute | solution.py:281
  14.9 5.4 %collective-permute-start.4 = (f32[128,128]{1,0:T(8,128)S(1)}, f32[128,128]{1,0:T(8,128)S(1)}, u32[]{:S(2)}, u32[]{:S(2)}) collective-permute-start(f32[128,128]{1,0:T(8,128)S(1)} %shard_map.80.refs_0_), channel_id=1, source_target_pairs={{0,48},{8,56},{16,32},{24,40},{32,16},{40,24},{48,0},{56,8},{1,49}... | collective-permute-start | bytes 196616 | tf_op jit(solution)/shard_map/ppermute | solution.py:281
  20.3 1.7 %collective-permute-done.4.refs_1_.refs_4_ = f32[128,128]{1,0:T(8,128)S(1)} collective-permute-done((f32[128,128]{1,0:T(8,128)S(1)}, f32[128,128]{1,0:T(8,128)S(1)}, u32[]{:S(2)}, u32[]{:S(2)}) %collective-permute-start.4) | collective-permute-done | bytes 65568 | tf_op jit(solution)/shard_map/ppermute | solution.py:281
  22.0 2.8 %collective-permute-start.7 = (f32[128,128]{1,0:T(8,128)S(1)}, f32[128,128]{1,0:T(8,128)S(1)}, u32[]{:S(2)}, u32[]{:S(2)}) collective-permute-start(f32[128,128]{1,0:T(8,128)S(1)} %shard_map.81), channel_id=1, source_target_pairs={{0,192},{64,128},{128,64},{192,0},{1,193},{65,129},{129,65},{193,1... | collective-permute-start | bytes 196616 | tf_op jit(solution)/shard_map/ppermute | solution.py:281
  25.5 1.0 %collective-permute-done.7.refs_7_ = f32[128,128]{1,0:T(8,128)S(1)} collective-permute-done((f32[128,128]{1,0:T(8,128)S(1)}, f32[128,128]{1,0:T(8,128)S(1)}, u32[]{:S(2)}, u32[]{:S(2)}) %collective-permute-start.7) | collective-permute-done | bytes 65568 | tf_op jit(solution)/shard_map/ppermute | solution.py:281
  26.5 3.1 %collective-permute-done.6.refs_6_ = f32[128,128]{1,0:T(8,128)S(1)} collective-permute-done((f32[128,128]{1,0:T(8,128)S(1)}, f32[128,128]{1,0:T(8,128)S(1)}, u32[]{:S(2)}, u32[]{:S(2)}) %collective-permute-start.6) | collective-permute-done | bytes 65568 | tf_op jit(solution)/shard_map/ppermute | solution.py:281
  29.7 1.9 %collective-permute-start.9 = (f32[128,128]{1,0:T(8,128)S(1)}, f32[128,128]{1,0:T(8,128)S(1)}, u32[]{:S(2)}, u32[]{:S(2)}) collective-permute-start(f32[128,128]{1,0:T(8,128)S(1)} %get-tuple-element.65), channel_id=1, source_target_pairs={{0,16},{8,24},{16,0},{24,8},{1,17},{9,25},{17,1},{25,9},{2,18},{10... | collective-permute-start | bytes 196616 | tf_op jit(solution)/shard_map/ppermute | solution.py:281
  31.6 1.7 %collective-permute-start.10 = (f32[128,128]{1,0:T(8,128)S(1)}, f32[128,128]{1,0:T(8,128)S(1)}, u32[]{:S(2)}, u32[]{:S(2)}) collective-permute-start(f32[128,128]{1,0:T(8,128)S(1)} %get-tuple-element.66), channel_id=1, source_target_pairs={{0,24},{8,16},{16,8},{24,0},{1,25},{9,17},{17,9},{25,1},{2,26},{10... | collective-permute-start | bytes 196616 | tf_op jit(solution)/shard_map/ppermute | solution.py:281
  33.3 0.6 collective-permute-done.9.refs_2_
  33.8 2.7 %collective-permute-done.10.refs_3_ = f32[128,128]{1,0:T(8,128)S(1)} collective-permute-done((f32[128,128]{1,0:T(8,128)S(1)}, f32[128,128]{1,0:T(8,128)S(1)}, u32[]{:S(2)}, u32[]{:S(2)}) %collective-permute-start.10) | collective-permute-done | bytes 65568 | tf_op jit(solution)/shard_map/ppermute | solution.py:281
  36.7 5.3 %collective-permute-start.11 = (f32[4,128,128]{2,1,0:T(8,128)S(1)}, f32[4,128,128]{2,1,0:T(8,128)S(1)}, u32[]{:S(2)}, u32[]{:S(2)}) collective-permute-start(f32[4,128,128]{2,1,0:T(8,128)S(1)} %get-tuple-element.69), channel_id=1, source_target_pairs={{0,4},{4,0},{1,5},{5,1},{2,6},{6,2},{3,7},{7,3},{8,12},{12,8},{9,1... | collective-permute-start | bytes 786440 | tf_op jit(solution)/shard_map/ppermute | solution.py:281
  42.3 0.8 collective-permute-done.11.state
  43.5 2.6 %collective-permute-start.14 = (f32[2,256]{1,0:T(2,128)S(1)}, f32[2,256]{1,0:T(2,128)S(1)}, u32[]{:S(2)}, u32[]{:S(2)}) collective-permute-start(f32[2,256]{1,0:T(2,128)S(1)} %get-tuple-element.71.sums_3), channel_id=1, source_target_pairs={{0,3},{1,2},{2,1},{3,0},{4,7},{5,6},{6,5},{7,4},{8,11},{9,10},{10,... | collective-permute-start | bytes 6152 | tf_op jit(solution)/shard_map/ppermute | solution.py:281
  46.0 0.5 collective-permute-start.13
  46.8 0.4 collective-permute-done.14.sums_2
  47.2 2.8 %collective-permute-done.13.sums_1 = f32[2,256]{1,0:T(2,128)S(1)} collective-permute-done((f32[2,256]{1,0:T(2,128)S(1)}, f32[2,256]{1,0:T(2,128)S(1)}, u32[]{:S(2)}, u32[]{:S(2)}) %collective-permute-start.13) | collective-permute-done | bytes 2080 | tf_op jit(solution)/shard_map/ppermute | solution.py:281
  50.0 0.4 shard_map.87
  50.4 1.9 %collective-permute-start.15 = (f32[4,128,128]{2,1,0:T(8,128)S(1)}, f32[4,128,128]{2,1,0:T(8,128)S(1)}, u32[]{:S(2)}, u32[]{:S(2)}) collective-permute-start(f32[4,128,128]{2,1,0:T(8,128)S(1)} %get-tuple-element.78), channel_id=1, source_target_pairs={{0,4},{4,0},{1,5},{5,1},{2,6},{6,2},{3,7},{7,3},{8,12},{12,8},{9,1... | collective-permute-start | bytes 786440 | tf_op jit(solution)/shard_map/ppermute | solution.py:281
  52.3 0.4 shard_map.86
  52.7 0.7 collective-permute-done.15.got.refs_5_
  53.5 0.6 collective-permute-start.16
  54.1 1.6 %collective-permute-start.17 = (f32[128,128]{1,0:T(8,128)S(1)}, f32[128,128]{1,0:T(8,128)S(1)}, u32[]{:S(2)}, u32[]{:S(2)}) collective-permute-start(f32[128,128]{1,0:T(8,128)S(1)} %get-tuple-element.83), channel_id=1, source_target_pairs={{0,16},{8,24},{16,0},{24,8},{1,17},{9,25},{17,1},{25,9},{2,18},{10... | collective-permute-start | bytes 196616 | tf_op jit(solution)/shard_map/ppermute | solution.py:281
  55.7 1.6 %collective-permute-start.18 = (f32[128,128]{1,0:T(8,128)S(1)}, f32[128,128]{1,0:T(8,128)S(1)}, u32[]{:S(2)}, u32[]{:S(2)}) collective-permute-start(f32[128,128]{1,0:T(8,128)S(1)} %get-tuple-element.84), channel_id=1, source_target_pairs={{0,24},{8,16},{16,8},{24,0},{1,25},{9,17},{17,9},{25,1},{2,26},{10... | collective-permute-start | bytes 196616 | tf_op jit(solution)/shard_map/ppermute | solution.py:281
  57.3 0.9 %shard_map.90 = (f32[256,512]{1,0:T(8,128)S(1)}, f32[256,512]{1,0:T(8,128)S(1)}) custom-call(bf16[256,1024]{1,0:T(8,128)(2,1)S(1)} %get-tuple-element.57.refs_6_.queries, bf16[256,512]{1,0:T(8,128)(2,1)S(1)} %get-tuple-element.51.keys_1.refs_1_.keys, bf16[256,512]{1,0:T(8,128)(2,1)S(1)} %get-tuple-element.53.values_1.refs_3_.values, ...), custom_call_target="tpu_custom_call" | custom-call | tf_op jit(solution)/shard_map/pallas_call | solution.py:59
  58.2 0.9 %shard_map.91 = (f32[256,512]{1,0:T(8,128)S(1)}, f32[256,512]{1,0:T(8,128)S(1)}) custom-call(bf16[256,1024]{1,0:T(8,128)(2,1)S(1)} %get-tuple-element.57.refs_6_.queries, bf16[256,512]{1,0:T(8,128)(2,1)S(1)} %get-tuple-element.50.keys_0.refs_0_.keys, bf16[256,512]{1,0:T(8,128)(2,1)S(1)} %get-tuple-element.52.values_0.refs_2_.values.refs_1_, ...), custom_call_target="tpu_custom_call" | custom-call | tf_op jit(solution)/shard_map/pallas_call | solution.py:59
  59.2 2.1 %shard_map.89.refs_0_ = bf16[256,1024]{1,0:T(8,128)(2,1)} custom-call(bf16[256,512]{1,0:T(8,128)(2,1)S(1)} %get-tuple-element.50.keys_0.refs_0_.keys, bf16[256,512]{1,0:T(8,128)(2,1)S(1)} %get-tuple-element.51.keys_1.refs_1_.keys, bf16[256,512]{1,0:T(8,128)(2,1)S(1)} %get-tuple-element.52.values_0.refs_2_.values.refs_1_, ...), custom_call_target="tpu_custom_call" | custom-call | tf_op jit(solution)/shard_map/pallas_call | solution.py:59
  61.3 4.1 %collective-permute-start.19 = (f32[128,128]{1,0:T(8,128)S(1)}, f32[128,128]{1,0:T(8,128)S(1)}, u32[]{:S(2)}, u32[]{:S(2)}) collective-permute-start(f32[128,128]{1,0:T(8,128)S(1)} %shard_map.92.refs_0_), channel_id=1, source_target_pairs={{0,48},{8,56},{16,32},{24,40},{32,16},{40,24},{48,0},{56,8},{1,49}... | collective-permute-start | bytes 196616 | tf_op jit(solution)/shard_map/ppermute | solution.py:281
  65.4 1.8 %collective-permute-done.19.refs_1_.refs_4_ = f32[128,128]{1,0:T(8,128)S(1)} collective-permute-done((f32[128,128]{1,0:T(8,128)S(1)}, f32[128,128]{1,0:T(8,128)S(1)}, u32[]{:S(2)}, u32[]{:S(2)}) %collective-permute-start.19) | collective-permute-done | bytes 65568 | tf_op jit(solution)/shard_map/ppermute | solution.py:281
  67.2 1.1 %collective-permute-start.22 = (f32[128,128]{1,0:T(8,128)S(1)}, f32[128,128]{1,0:T(8,128)S(1)}, u32[]{:S(2)}, u32[]{:S(2)}) collective-permute-start(f32[128,128]{1,0:T(8,128)S(1)} %shard_map.93), channel_id=1, source_target_pairs={{0,192},{64,128},{128,64},{192,0},{1,193},{65,129},{129,65},{193,1... | collective-permute-start | bytes 196616 | tf_op jit(solution)/shard_map/ppermute | solution.py:281
  68.3 0.8 collective-permute-start.21
  69.1 1.4 %collective-permute-start.20 = (f32[128,128]{1,0:T(8,128)S(1)}, f32[128,128]{1,0:T(8,128)S(1)}, u32[]{:S(2)}, u32[]{:S(2)}) collective-permute-start(f32[128,128]{1,0:T(8,128)S(1)} %shard_map.93), channel_id=1, source_target_pairs={{0,64},{64,0},{128,192},{192,128},{1,65},{65,1},{129,193},{193,129... | collective-permute-start | bytes 196616 | tf_op jit(solution)/shard_map/ppermute | solution.py:281
  70.5 1.1 %collective-permute-done.22.refs_7_ = f32[128,128]{1,0:T(8,128)S(1)} collective-permute-done((f32[128,128]{1,0:T(8,128)S(1)}, f32[128,128]{1,0:T(8,128)S(1)}, u32[]{:S(2)}, u32[]{:S(2)}) %collective-permute-start.22) | collective-permute-done | bytes 65568 | tf_op jit(solution)/shard_map/ppermute | solution.py:281
  71.6 1.3 %collective-permute-done.21.refs_6_ = f32[128,128]{1,0:T(8,128)S(1)} collective-permute-done((f32[128,128]{1,0:T(8,128)S(1)}, f32[128,128]{1,0:T(8,128)S(1)}, u32[]{:S(2)}, u32[]{:S(2)}) %collective-permute-start.21) | collective-permute-done | bytes 65568 | tf_op jit(solution)/shard_map/ppermute | solution.py:281
  73.0 1.4 %collective-permute-start.23 = (f32[128,128]{1,0:T(8,128)S(1)}, f32[128,128]{1,0:T(8,128)S(1)}, u32[]{:S(2)}, u32[]{:S(2)}) collective-permute-start(f32[128,128]{1,0:T(8,128)S(1)} %get-tuple-element.88), channel_id=1, source_target_pairs={{0,8},{8,0},{16,24},{24,16},{1,9},{9,1},{17,25},{25,17},{2,10},{10... | collective-permute-start | bytes 196616 | tf_op jit(solution)/shard_map/ppermute | solution.py:281
  74.4 0.6 collective-permute-start.24
  75.0 1.6 %collective-permute-start.25 = (f32[128,128]{1,0:T(8,128)S(1)}, f32[128,128]{1,0:T(8,128)S(1)}, u32[]{:S(2)}, u32[]{:S(2)}) collective-permute-start(f32[128,128]{1,0:T(8,128)S(1)} %get-tuple-element.90), channel_id=1, source_target_pairs={{0,24},{8,16},{16,8},{24,0},{1,25},{9,17},{17,9},{25,1},{2,26},{10... | collective-permute-start | bytes 196616 | tf_op jit(solution)/shard_map/ppermute | solution.py:281
  76.6 2.4 %collective-permute-done.24.refs_2_ = f32[128,128]{1,0:T(8,128)S(1)} collective-permute-done((f32[128,128]{1,0:T(8,128)S(1)}, f32[128,128]{1,0:T(8,128)S(1)}, u32[]{:S(2)}, u32[]{:S(2)}) %collective-permute-start.24) | collective-permute-done | bytes 65568 | tf_op jit(solution)/shard_map/ppermute | solution.py:281
  79.1 1.0 %collective-permute-done.25.refs_3_ = f32[128,128]{1,0:T(8,128)S(1)} collective-permute-done((f32[128,128]{1,0:T(8,128)S(1)}, f32[128,128]{1,0:T(8,128)S(1)}, u32[]{:S(2)}, u32[]{:S(2)}) %collective-permute-start.25) | collective-permute-done | bytes 65568 | tf_op jit(solution)/shard_map/ppermute | solution.py:281
  80.1 5.8 %collective-permute-start.26 = (f32[4,128,128]{2,1,0:T(8,128)S(1)}, f32[4,128,128]{2,1,0:T(8,128)S(1)}, u32[]{:S(2)}, u32[]{:S(2)}) collective-permute-start(f32[4,128,128]{2,1,0:T(8,128)S(1)} %get-tuple-element.91), channel_id=1, source_target_pairs={{0,4},{4,0},{1,5},{5,1},{2,6},{6,2},{3,7},{7,3},{8,12},{12,8},{9,1... | collective-permute-start | bytes 786440 | tf_op jit(solution)/shard_map/ppermute | solution.py:281
  86.2 0.9 collective-permute-done.26.state
  87.0 1.5 %shard_map.97 = (bf16[256,1024]{1,0:T(8,128)(2,1)}, bf16[256,1024]{1,0:T(8,128)(2,1)}) custom-call(bf16[256,512]{1,0:T(8,128)(2,1)S(1)} %get-tuple-element.51.keys_1.refs_1_.keys, bf16[256,512]{1,0:T(8,128)(2,1)S(1)} %get-tuple-element.53.values_1.refs_3_.values, f32[256,512]{1,0:T(8,128)S(1)} %get-tuple-element.80.refs_7_.key_inner, ...), custom_call_target="tpu_custom_call" | custom-call | tf_op jit(solution)/shard_map/pallas_call | solution.py:59
  (31 shorter events, 2.6 us)
Async XLA Ops:
  2.0 4.7 %collective-permute-start = (f32[4,128,128]{2,1,0:T(8,128)S(1)}, f32[4,128,128]{2,1,0:T(8,128)S(1)}, u32[]{:S(2)}, u32[]{:S(2)}) collective-permute-start(f32[4,128,128]{2,1,0:T(8,128)S(1)} %get-tuple-element.55), channel_id=1, source_target_pairs={{0,4},{4,0},{1,5},{5,1},{2,6},{6,2},{3,7},{7,3},{8,12},{12,8},{9,1... | collective-permute-start | bytes 786440 | tf_op jit(solution)/shard_map/ppermute | solution.py:281
  6.8 3.7 %copy-start = (bf16[1024]{0:T(1024)(128)(2,1)S(1)}, bf16[1024]{0:T(1024)(128)(2,1)}, u32[]{:S(2)}) copy-start(bf16[1024]{0:T(1024)(128)(2,1)} %param.9) | copy-start | bytes 6148
  6.9 6.6 %collective-permute-start.1 = (f32[128,128]{1,0:T(8,128)S(1)}, f32[128,128]{1,0:T(8,128)S(1)}, u32[]{:S(2)}, u32[]{:S(2)}) collective-permute-start(f32[128,128]{1,0:T(8,128)S(1)} %get-tuple-element.60), channel_id=1, source_target_pairs={{0,8},{8,0},{16,24},{24,16},{1,9},{9,1},{17,25},{25,17},{2,10},{10... | collective-permute-start | bytes 196616 | tf_op jit(solution)/shard_map/ppermute | solution.py:281
  7.0 6.5 %collective-permute-start.2 = (f32[128,128]{1,0:T(8,128)S(1)}, f32[128,128]{1,0:T(8,128)S(1)}, u32[]{:S(2)}, u32[]{:S(2)}) collective-permute-start(f32[128,128]{1,0:T(8,128)S(1)} %get-tuple-element.61), channel_id=1, source_target_pairs={{0,16},{8,24},{16,0},{24,8},{1,17},{9,25},{17,1},{25,9},{2,18},{10... | collective-permute-start | bytes 196616 | tf_op jit(solution)/shard_map/ppermute | solution.py:281
  9.9 5.0 %collective-permute-start.3 = (f32[128,128]{1,0:T(8,128)S(1)}, f32[128,128]{1,0:T(8,128)S(1)}, u32[]{:S(2)}, u32[]{:S(2)}) collective-permute-start(f32[128,128]{1,0:T(8,128)S(1)} %get-tuple-element.62), channel_id=1, source_target_pairs={{0,24},{8,16},{16,8},{24,0},{1,25},{9,17},{17,9},{25,1},{2,26},{10... | collective-permute-start | bytes 196616 | tf_op jit(solution)/shard_map/ppermute | solution.py:281
  14.9 7.1 %collective-permute-start.4 = (f32[128,128]{1,0:T(8,128)S(1)}, f32[128,128]{1,0:T(8,128)S(1)}, u32[]{:S(2)}, u32[]{:S(2)}) collective-permute-start(f32[128,128]{1,0:T(8,128)S(1)} %shard_map.80.refs_0_), channel_id=1, source_target_pairs={{0,48},{8,56},{16,32},{24,40},{32,16},{40,24},{48,0},{56,8},{1,49}... | collective-permute-start | bytes 196616 | tf_op jit(solution)/shard_map/ppermute | solution.py:281
  22.0 4.5 %collective-permute-start.7 = (f32[128,128]{1,0:T(8,128)S(1)}, f32[128,128]{1,0:T(8,128)S(1)}, u32[]{:S(2)}, u32[]{:S(2)}) collective-permute-start(f32[128,128]{1,0:T(8,128)S(1)} %shard_map.81), channel_id=1, source_target_pairs={{0,192},{64,128},{128,64},{192,0},{1,193},{65,129},{129,65},{193,1... | collective-permute-start | bytes 196616 | tf_op jit(solution)/shard_map/ppermute | solution.py:281
  24.8 4.7 %collective-permute-start.6 = (f32[128,128]{1,0:T(8,128)S(1)}, f32[128,128]{1,0:T(8,128)S(1)}, u32[]{:S(2)}, u32[]{:S(2)}) collective-permute-start(f32[128,128]{1,0:T(8,128)S(1)} %shard_map.81), channel_id=1, source_target_pairs={{0,128},{64,192},{128,0},{192,64},{1,129},{65,193},{129,1},{193,65... | collective-permute-start | bytes 196616 | tf_op jit(solution)/shard_map/ppermute | solution.py:281
  25.2 4.4 %collective-permute-start.5 = (f32[128,128]{1,0:T(8,128)S(1)}, f32[128,128]{1,0:T(8,128)S(1)}, u32[]{:S(2)}, u32[]{:S(2)}) collective-permute-start(f32[128,128]{1,0:T(8,128)S(1)} %shard_map.81), channel_id=1, source_target_pairs={{0,64},{64,0},{128,192},{192,128},{1,65},{65,1},{129,193},{193,129... | collective-permute-start | bytes 196616 | tf_op jit(solution)/shard_map/ppermute | solution.py:281
  29.6 3.6 %collective-permute-start.8 = (f32[128,128]{1,0:T(8,128)S(1)}, f32[128,128]{1,0:T(8,128)S(1)}, u32[]{:S(2)}, u32[]{:S(2)}) collective-permute-start(f32[128,128]{1,0:T(8,128)S(1)} %get-tuple-element.64), channel_id=1, source_target_pairs={{0,8},{8,0},{16,24},{24,16},{1,9},{9,1},{17,25},{25,17},{2,10},{10... | collective-permute-start | bytes 196616 | tf_op jit(solution)/shard_map/ppermute | solution.py:281
  29.7 4.1 %collective-permute-start.9 = (f32[128,128]{1,0:T(8,128)S(1)}, f32[128,128]{1,0:T(8,128)S(1)}, u32[]{:S(2)}, u32[]{:S(2)}) collective-permute-start(f32[128,128]{1,0:T(8,128)S(1)} %get-tuple-element.65), channel_id=1, source_target_pairs={{0,16},{8,24},{16,0},{24,8},{1,17},{9,25},{17,1},{25,9},{2,18},{10... | collective-permute-start | bytes 196616 | tf_op jit(solution)/shard_map/ppermute | solution.py:281
  31.6 5.0 %collective-permute-start.10 = (f32[128,128]{1,0:T(8,128)S(1)}, f32[128,128]{1,0:T(8,128)S(1)}, u32[]{:S(2)}, u32[]{:S(2)}) collective-permute-start(f32[128,128]{1,0:T(8,128)S(1)} %get-tuple-element.66), channel_id=1, source_target_pairs={{0,24},{8,16},{16,8},{24,0},{1,25},{9,17},{17,9},{25,1},{2,26},{10... | collective-permute-start | bytes 196616 | tf_op jit(solution)/shard_map/ppermute | solution.py:281
  36.7 6.4 %collective-permute-start.11 = (f32[4,128,128]{2,1,0:T(8,128)S(1)}, f32[4,128,128]{2,1,0:T(8,128)S(1)}, u32[]{:S(2)}, u32[]{:S(2)}) collective-permute-start(f32[4,128,128]{2,1,0:T(8,128)S(1)} %get-tuple-element.69), channel_id=1, source_target_pairs={{0,4},{4,0},{1,5},{5,1},{2,6},{6,2},{3,7},{7,3},{8,12},{12,8},{9,1... | collective-permute-start | bytes 786440 | tf_op jit(solution)/shard_map/ppermute | solution.py:281
  43.5 3.7 %collective-permute-start.14 = (f32[2,256]{1,0:T(2,128)S(1)}, f32[2,256]{1,0:T(2,128)S(1)}, u32[]{:S(2)}, u32[]{:S(2)}) collective-permute-start(f32[2,256]{1,0:T(2,128)S(1)} %get-tuple-element.71.sums_3), channel_id=1, source_target_pairs={{0,3},{1,2},{2,1},{3,0},{4,7},{5,6},{6,5},{7,4},{8,11},{9,10},{10,... | collective-permute-start | bytes 6152 | tf_op jit(solution)/shard_map/ppermute | solution.py:281
  46.0 3.9 %collective-permute-start.13 = (f32[2,256]{1,0:T(2,128)S(1)}, f32[2,256]{1,0:T(2,128)S(1)}, u32[]{:S(2)}, u32[]{:S(2)}) collective-permute-start(f32[2,256]{1,0:T(2,128)S(1)} %get-tuple-element.71.sums_3), channel_id=1, source_target_pairs={{0,2},{1,3},{2,0},{3,1},{4,6},{5,7},{6,4},{7,5},{8,10},{9,11},{10,... | collective-permute-start | bytes 6152 | tf_op jit(solution)/shard_map/ppermute | solution.py:281
  46.5 3.4 %collective-permute-start.12 = (f32[2,256]{1,0:T(2,128)S(1)}, f32[2,256]{1,0:T(2,128)S(1)}, u32[]{:S(2)}, u32[]{:S(2)}) collective-permute-start(f32[2,256]{1,0:T(2,128)S(1)} %get-tuple-element.71.sums_3), channel_id=1, source_target_pairs={{0,1},{1,0},{2,3},{3,2},{4,5},{5,4},{6,7},{7,6},{8,9},{9,8},{10,11... | collective-permute-start | bytes 6152 | tf_op jit(solution)/shard_map/ppermute | solution.py:281
  50.4 3.1 %collective-permute-start.15 = (f32[4,128,128]{2,1,0:T(8,128)S(1)}, f32[4,128,128]{2,1,0:T(8,128)S(1)}, u32[]{:S(2)}, u32[]{:S(2)}) collective-permute-start(f32[4,128,128]{2,1,0:T(8,128)S(1)} %get-tuple-element.78), channel_id=1, source_target_pairs={{0,4},{4,0},{1,5},{5,1},{2,6},{6,2},{3,7},{7,3},{8,12},{12,8},{9,1... | collective-permute-start | bytes 786440 | tf_op jit(solution)/shard_map/ppermute | solution.py:281
  53.5 7.8 %collective-permute-start.16 = (f32[128,128]{1,0:T(8,128)S(1)}, f32[128,128]{1,0:T(8,128)S(1)}, u32[]{:S(2)}, u32[]{:S(2)}) collective-permute-start(f32[128,128]{1,0:T(8,128)S(1)} %get-tuple-element.82), channel_id=1, source_target_pairs={{0,8},{8,0},{16,24},{24,16},{1,9},{9,1},{17,25},{25,17},{2,10},{10... | collective-permute-start | bytes 196616 | tf_op jit(solution)/shard_map/ppermute | solution.py:281
  54.1 7.2 %collective-permute-start.17 = (f32[128,128]{1,0:T(8,128)S(1)}, f32[128,128]{1,0:T(8,128)S(1)}, u32[]{:S(2)}, u32[]{:S(2)}) collective-permute-start(f32[128,128]{1,0:T(8,128)S(1)} %get-tuple-element.83), channel_id=1, source_target_pairs={{0,16},{8,24},{16,0},{24,8},{1,17},{9,25},{17,1},{25,9},{2,18},{10... | collective-permute-start | bytes 196616 | tf_op jit(solution)/shard_map/ppermute | solution.py:281
  55.7 5.6 %collective-permute-start.18 = (f32[128,128]{1,0:T(8,128)S(1)}, f32[128,128]{1,0:T(8,128)S(1)}, u32[]{:S(2)}, u32[]{:S(2)}) collective-permute-start(f32[128,128]{1,0:T(8,128)S(1)} %get-tuple-element.84), channel_id=1, source_target_pairs={{0,24},{8,16},{16,8},{24,0},{1,25},{9,17},{17,9},{25,1},{2,26},{10... | collective-permute-start | bytes 196616 | tf_op jit(solution)/shard_map/ppermute | solution.py:281
  61.3 5.8 %collective-permute-start.19 = (f32[128,128]{1,0:T(8,128)S(1)}, f32[128,128]{1,0:T(8,128)S(1)}, u32[]{:S(2)}, u32[]{:S(2)}) collective-permute-start(f32[128,128]{1,0:T(8,128)S(1)} %shard_map.92.refs_0_), channel_id=1, source_target_pairs={{0,48},{8,56},{16,32},{24,40},{32,16},{40,24},{48,0},{56,8},{1,49}... | collective-permute-start | bytes 196616 | tf_op jit(solution)/shard_map/ppermute | solution.py:281
  67.2 4.4 %collective-permute-start.22 = (f32[128,128]{1,0:T(8,128)S(1)}, f32[128,128]{1,0:T(8,128)S(1)}, u32[]{:S(2)}, u32[]{:S(2)}) collective-permute-start(f32[128,128]{1,0:T(8,128)S(1)} %shard_map.93), channel_id=1, source_target_pairs={{0,192},{64,128},{128,64},{192,0},{1,193},{65,129},{129,65},{193,1... | collective-permute-start | bytes 196616 | tf_op jit(solution)/shard_map/ppermute | solution.py:281
  68.3 4.6 %collective-permute-start.21 = (f32[128,128]{1,0:T(8,128)S(1)}, f32[128,128]{1,0:T(8,128)S(1)}, u32[]{:S(2)}, u32[]{:S(2)}) collective-permute-start(f32[128,128]{1,0:T(8,128)S(1)} %shard_map.93), channel_id=1, source_target_pairs={{0,128},{64,192},{128,0},{192,64},{1,129},{65,193},{129,1},{193,65... | collective-permute-start | bytes 196616 | tf_op jit(solution)/shard_map/ppermute | solution.py:281
  69.1 3.8 %collective-permute-start.20 = (f32[128,128]{1,0:T(8,128)S(1)}, f32[128,128]{1,0:T(8,128)S(1)}, u32[]{:S(2)}, u32[]{:S(2)}) collective-permute-start(f32[128,128]{1,0:T(8,128)S(1)} %shard_map.93), channel_id=1, source_target_pairs={{0,64},{64,0},{128,192},{192,128},{1,65},{65,1},{129,193},{193,129... | collective-permute-start | bytes 196616 | tf_op jit(solution)/shard_map/ppermute | solution.py:281
  73.0 3.6 %collective-permute-start.23 = (f32[128,128]{1,0:T(8,128)S(1)}, f32[128,128]{1,0:T(8,128)S(1)}, u32[]{:S(2)}, u32[]{:S(2)}) collective-permute-start(f32[128,128]{1,0:T(8,128)S(1)} %get-tuple-element.88), channel_id=1, source_target_pairs={{0,8},{8,0},{16,24},{24,16},{1,9},{9,1},{17,25},{25,17},{2,10},{10... | collective-permute-start | bytes 196616 | tf_op jit(solution)/shard_map/ppermute | solution.py:281
  74.4 4.7 %collective-permute-start.24 = (f32[128,128]{1,0:T(8,128)S(1)}, f32[128,128]{1,0:T(8,128)S(1)}, u32[]{:S(2)}, u32[]{:S(2)}) collective-permute-start(f32[128,128]{1,0:T(8,128)S(1)} %get-tuple-element.89), channel_id=1, source_target_pairs={{0,16},{8,24},{16,0},{24,8},{1,17},{9,25},{17,1},{25,9},{2,18},{10... | collective-permute-start | bytes 196616 | tf_op jit(solution)/shard_map/ppermute | solution.py:281
  75.0 5.0 %collective-permute-start.25 = (f32[128,128]{1,0:T(8,128)S(1)}, f32[128,128]{1,0:T(8,128)S(1)}, u32[]{:S(2)}, u32[]{:S(2)}) collective-permute-start(f32[128,128]{1,0:T(8,128)S(1)} %get-tuple-element.90), channel_id=1, source_target_pairs={{0,24},{8,16},{16,8},{24,0},{1,25},{9,17},{17,9},{25,1},{2,26},{10... | collective-permute-start | bytes 196616 | tf_op jit(solution)/shard_map/ppermute | solution.py:281
  80.1 6.9 %collective-permute-start.26 = (f32[4,128,128]{2,1,0:T(8,128)S(1)}, f32[4,128,128]{2,1,0:T(8,128)S(1)}, u32[]{:S(2)}, u32[]{:S(2)}) collective-permute-start(f32[4,128,128]{2,1,0:T(8,128)S(1)} %get-tuple-element.91), channel_id=1, source_target_pairs={{0,4},{4,0},{1,5},{5,1},{2,6},{6,2},{3,7},{7,3},{8,12},{12,8},{9,1... | collective-permute-start | bytes 786440 | tf_op jit(solution)/shard_map/ppermute | solution.py:281

commit v4 on v3

--- a/solution.py
+++ b/solution.py
@@ -10,6 +10,7 @@
 
 HEADS = 32
 HEAD_DIM = 128
+BLOCK = 128
 EPSILON = 1e-05
 FEATURES = HEADS * HEAD_DIM
 FACTOR = HEAD_DIM ** (-0.5)
@@ -34,10 +35,15 @@
     return pl.ds(head * HEAD_DIM, HEAD_DIM)
 
 
+def blocks(tokens):
+    return [slice(at, at + BLOCK) for at in range(0, tokens, BLOCK)]
+
+
 def causal(count, transposed):
     row = lax.broadcasted_iota(jnp.int32, (count, count), 0)
     col = lax.broadcasted_iota(jnp.int32, (count, count), 1)
-    return row <= col if transposed else col <= row
+    order = row <= col if transposed else col <= row
+    return order & (row // BLOCK == col // BLOCK)
 
 
 def scores(a, b, mask):
@@ -81,7 +87,7 @@
     return [pltpu.make_async_copy(there, at, sem) for there, at, sem in halves(far, near, sems)]
 
 
-def totals_kernel(part, keys_far, values_far, out, keys, values, sems):
+def totals_kernel(part, keys_far, values_far, out, sooner, keys, values, sems):
     chunks = sems.shape[1]
     rows = keys.shape[0] // chunks
     half = keys.shape[1]
@@ -98,7 +104,12 @@
         copy.wait()
     for head in range(out.shape[0]):
         at = columns(head)
-        out[head] = dot_tn(keys[:, at], values[:, at])
+        total = jnp.zeros(out.shape[1:], F32)
+        for block, rows in enumerate(blocks(keys.shape[0])):
+            if block:
+                sooner[head, block - 1] = total
+            total = total + dot_tn(keys[rows, at], values[rows, at])
+        out[head] = total
 
 
 def within_kernel(
@@ -166,7 +177,7 @@
         theirs[at] = back[step][...] + jnp.where(first, mine[at], 0.0)
 
 
-def forward_kernel(part, queries, upstream, within, state, *refs):
+def forward_kernel(part, queries, upstream, within, state, sooner, *refs):
     before_sums, (output, low, sums) = refs[:part], refs[part:]
     heads = state.shape[0]
     tokens = queries.shape[0]
@@ -174,9 +185,15 @@
     mixed = jnp.zeros((tokens, HEAD_DIM), F32)
     for head in range(heads):
         at = columns(part * heads + head)
-        state_low = state[head].astype(BF16)
-        low[head] = state_low
-        out = within[:, at] + FACTOR * dot_nn(queries[:, at], state_low)
+        carried = []
+        for block, rows in enumerate(blocks(tokens)):
+            wide = state[head]
+            if block:
+                wide = wide + sooner[head, block - 1]
+            state_low = wide.astype(BF16)
+            low[head, block] = state_low
+            carried.append(dot_nn(queries[rows, at], state_low))
+        out = within[:, at] + FACTOR * jnp.concatenate(carried)
         output[:, columns(head)] = out
         square = square + out * out
         mixed = mixed + upstream[:, at] * out
@@ -187,7 +204,7 @@
         sums[row : row + 1] = total
 
 
-def delta_kernel(part, queries, upstream, output, sums, sums_1, sums_2, sums_3, delta, back):
+def delta_kernel(part, queries, upstream, output, sums, sums_1, sums_2, sums_3, delta, back, later):
     tokens = queries.shape[0]
     heads = back.shape[0]
     total = sums[...] + sums_1[...] + sums_2[...] + sums_3[...]
@@ -200,7 +217,14 @@
         out_delta = inv_rms * upstream[:, at] - pull * output[:, columns(head)]
         out_delta = out_delta.astype(BF16)
         delta[:, columns(head)] = out_delta
-        back[head] = dot_tn(out_delta, queries[:, at])
+        total = jnp.zeros(back.shape[1:], F32)
+        parts = blocks(tokens)
+        for block in reversed(range(len(parts))):
+            rows = parts[block]
+            if block + 1 < len(parts):
+                later[head, block] = total
+            total = total + dot_tn(out_delta[rows], queries[rows, at])
+        back[head] = total
 
 
 def write(near, far, part, sem):
@@ -221,8 +245,12 @@
         for head in range(low.shape[0]):
             at = columns(head)
             out_delta = delta[:, at]
+            carried = [
+                dot_nt(delta[rows, at], low[head, block])
+                for block, rows in enumerate(blocks(keys.shape[0]))
+            ]
             delta_scores = scores(out_delta, values[:, at], mask)
-            grad = dot_nn(delta_scores, keys[:, at]) + FACTOR * dot_nt(out_delta, low[head])
+            grad = dot_nn(delta_scores, keys[:, at]) + FACTOR * jnp.concatenate(carried)
             near[:, at] = grad.astype(BF16)
         copies.append(write(near, far, part, sems.at[part]))
     for copy in copies:
@@ -240,16 +268,26 @@
         value_inner[:, at] = dot_nn(scores(keys[:, at], query, mask), out_delta)
 
 
-def key_value_grads(keys, values, key_inner, value_inner, state, key_near, value_near):
-    lows = [state[head].astype(BF16) for head in range(state.shape[0])]
-    for head, later_low in enumerate(lows):
+def key_value_grads(keys, values, key_inner, value_inner, state, later, key_near, value_near):
+    parts = blocks(keys.shape[0])
+    heads = range(state.shape[0])
+    lows = {}
+    for head in heads:
+        for block in range(len(parts)):
+            wide = state[head]
+            if block + 1 < len(parts):
+                wide = wide + later[head, block]
+            lows[head, block] = wide.astype(BF16)
+    for head in heads:
         at = columns(head)
-        grad = key_inner[:, at] + FACTOR * dot_nn(values[:, at], later_low)
+        carried = [dot_nn(values[rows, at], lows[head, n]) for n, rows in enumerate(parts)]
+        grad = key_inner[:, at] + FACTOR * jnp.concatenate(carried)
         key_near[:, at] = grad.astype(BF16)
     yield
-    for head, later_low in enumerate(lows):
+    for head in heads:
         at = columns(head)
-        grad = value_inner[:, at] + FACTOR * dot_nt(keys[:, at], later_low)
+        carried = [dot_nt(keys[rows, at], lows[head, n]) for n, rows in enumerate(parts)]
+        grad = value_inner[:, at] + FACTOR * jnp.concatenate(carried)
         value_near[:, at] = grad.astype(BF16)
     yield
 
@@ -260,14 +298,16 @@
 
 
 def last_kernel(
-    keys, values, key_inner, value_inner, state, key_0, value_0,
+    keys, values, key_inner, value_inner, state, later, key_0, value_0,
     key_far, value_far, key_1, value_1, sems,
 ):
     copies = [
         write(key_0, key_far, 0, sems.at[0]),
         write(value_0, value_far, 0, sems.at[1]),
     ]
-    steps = key_value_grads(keys, values, key_inner, value_inner, state, key_1, value_1)
+    steps = key_value_grads(
+        keys, values, key_inner, value_inner, state, later, key_1, value_1
+    )
     next(steps)
     copies.append(write(key_1, key_far, 1, sems.at[2]))
     next(steps)
@@ -327,7 +367,8 @@
     wide = near((tokens, width), BF16)
     full = near((tokens, width))
     half = near((heads // 2, HEAD_DIM, HEAD_DIM))
-    half_low = near(half.shape, BF16)
+    inner_blocks = near((heads // 2, tokens // BLOCK - 1, HEAD_DIM, HEAD_DIM))
+    half_low = near((heads // 2, tokens // BLOCK, HEAD_DIM, HEAD_DIM), BF16)
     half_wide = near((tokens, width // 2), BF16)
     half_full = near((tokens, width // 2))
     sums_shape = near((2, tokens))
@@ -335,14 +376,15 @@
     other, mine = (
         call(
             functools.partial(totals_kernel, part),
-            (half, half_wide, half_wide),
+            (half, inner_blocks, half_wide, half_wide),
             far=2,
             scratch_shapes=[pltpu.SemaphoreType.DMA((2, 4))],
         )(keys, values)
         for part in (1, 0)
     )
-    mine, *near_0 = mine
-    other, *near_1 = other
+    mine, sooner_0, *near_0 = mine
+    other, sooner_1, *near_1 = other
+    sooner = sooner_0, sooner_1
     keys, values = zip(near_0, near_1)
 
     def beside_forward(after):
@@ -358,19 +400,19 @@
     for part, state in enumerate(states):
         output, low, *sums = call(
             functools.partial(forward_kernel, part), (half_full, half_low, sums_shape)
-        )(queries, upstream, within, state, *sums)
+        )(queries, upstream, within, state, sooner[part], *sums)
         outputs.append(output)
         lows.append(low)
     sums = swaps(sums * lax.axis_size("head"), "head", (1, 3, 2)) + sums
-    deltas, backs = zip(
+    deltas, backs, later = zip(
         *(
-            call(functools.partial(delta_kernel, part), (half_wide, half))(
+            call(functools.partial(delta_kernel, part), (half_wide, half, inner_blocks))(
                 queries, upstream, outputs[part], *sums
             )
             for part in (1, 0)
         )
     )
-    deltas, backs = deltas[::-1], backs[::-1]
+    deltas, backs, later = deltas[::-1], backs[::-1], later[::-1]
 
     def beside_backward(after):
         query_grad = call(
@@ -388,13 +430,13 @@
 
     states, (query_grad, *inner) = entering(*backs, True, beside_backward)
     key_0, value_0 = call(backward_kernel, (half_wide, half_wide))(
-        keys[0], values[0], *inner[:2], states[0]
+        keys[0], values[0], *inner[:2], states[0], later[0]
     )
     key_grad, value_grad = call(
         last_kernel,
         (grads, grads),
         scratch_shapes=[half_wide, half_wide, pltpu.SemaphoreType.DMA((4,))],
-    )(keys[1], values[1], *inner[2:], states[1], key_0, value_0)
+    )(keys[1], values[1], *inner[2:], states[1], later[1], key_0, value_0)
     return query_grad, key_grad, value_grad
 
 

time: 89 us -> 89.3 us (level)
  Pallas kernels: 12.9 us -> 14 us
  starting transfers between devices: 50.6 us -> 49.6 us
    pallas_call x22, Pallas kernels: 12.9 us -> 14 us  [run(): pl.pallas_call(kernel, out_shape=out_shape, in_specs=[pl.BlockSpec(memory...]
    ppermute x27, starting transfers between devices: 50.6 us -> 49.6 us  [swap(): lax.ppermute(array, axis, [(at, at ^ distance) for at in range(count)])]
  transfers between devices with their start and end apart: 27 -> 27, of which waited for: 16 -> 16; matrix products, arithmetic and copies ran while one was open for 1% -> 1% of each run, Pallas kernels for 10% -> 11%
where the time goes in v4:
time: 89.3 us; the launch traced here: 89 us
  starting transfers between devices  49.6 us (56%)
  waiting for transfers between devices  23.8 us (27%)
  Pallas kernels  14 us (16%)
  between operations  1.01 us (1%)
    ppermute x27, starting transfers between devices, swap(): lax.ppermute(array, axis, [(at, at ^ distance) for at in range(count)])  49.6 us
    ppermute x27, waiting for transfers between devices, swap(): lax.ppermute(array, axis, [(at, at ^ distance) for at in range(count)])  23.8 us
    pallas_call x22, Pallas kernels, run(): pl.pallas_call(kernel, out_shape=out_shape, in_specs=[pl.BlockSpec(memory...  14 us
  transfers between devices with their start and end apart: 27, of which 16 were waited for; matrix products, arithmetic and copies ran while one was open for 1% of the time, Pallas kernels for 11%

profile of v4, /device:TPU:1, one launch (start us, length us, event | category | flops | bytes accessed | tf_op | source)
XLA Modules:
  0.0 89.0 jit_solution(11679870502394899352)
XLA Ops:
  0.6 1.4 %shard_map.77 = (f32[4,128,128]{2,1,0:T(8,128)S(1)}, f32[4,1,128,128]{3,2,1,0:T(8,128)S(1)}, bf16[256,512]{1,0:T(8,128)(2,1)S(1)}, bf16[256,512]{1,0:T(8,128)(2,1)S(1)}) custom-call(bf16[256,1024]{1,0:T(8,128)(2,1)} %keys_far.3, bf16[256,1024]{1,0:T(8,128)(2,1)} %values_far.3), custom_call_target="tpu_custom_call" | custom-call | tf_op jit(solution)/shard_map/pallas_call | solution.py:65
  2.0 3.3 %collective-permute-start = (f32[4,128,128]{2,1,0:T(8,128)S(1)}, f32[4,128,128]{2,1,0:T(8,128)S(1)}, u32[]{:S(2)}, u32[]{:S(2)}) collective-permute-start(f32[4,128,128]{2,1,0:T(8,128)S(1)} %get-tuple-element.59), channel_id=1, source_target_pairs={{0,4},{4,0},{1,5},{5,1},{2,6},{6,2},{3,7},{7,3},{8,12},{12,8},{9,1... | collective-permute-start | bytes 786440 | tf_op jit(solution)/shard_map/ppermute | solution.py:321
  5.4 1.4 %shard_map.76 = (f32[4,128,128]{2,1,0:T(8,128)S(1)}, f32[4,1,128,128]{3,2,1,0:T(8,128)S(1)}, bf16[256,512]{1,0:T(8,128)(2,1)S(1)}, bf16[256,512]{1,0:T(8,128)(2,1)S(1)}) custom-call(bf16[256,1024]{1,0:T(8,128)(2,1)} %keys_far.3, bf16[256,1024]{1,0:T(8,128)(2,1)} %values_far.3), custom_call_target="tpu_custom_call" | custom-call | tf_op jit(solution)/shard_map/pallas_call | solution.py:65
  6.9 2.9 %collective-permute-start.2 = (f32[128,128]{1,0:T(8,128)S(1)}, f32[128,128]{1,0:T(8,128)S(1)}, u32[]{:S(2)}, u32[]{:S(2)}) collective-permute-start(f32[128,128]{1,0:T(8,128)S(1)} %get-tuple-element.65), channel_id=1, source_target_pairs={{0,16},{8,24},{16,0},{24,8},{1,17},{9,25},{17,1},{25,9},{2,18},{10... | collective-permute-start | bytes 196616 | tf_op jit(solution)/shard_map/ppermute | solution.py:321
  9.8 0.7 collective-permute-start.3
  10.5 0.6 reshape.9.gain_far
  11.1 2.3 %shard_map.79 = (f32[256,1024]{1,0:T(8,128)S(1)}, f32[256,1024]{1,0:T(8,128)S(1)}, bf16[256,1024]{1,0:T(8,128)(2,1)S(1)}) custom-call(bf16[256,1024]{1,0:T(8,128)(2,1)} %queries_far.1, bf16[256,1024]{1,0:T(8,128)(2,1)} %grad_far.1, bf16[1,1024]{1,0:T(2,128)(2,1)} %reshape.9.gain_far, bf16[256,512]{1,0:T(8,128)(2,1)S(1)} %get-tuple-element.54.keys_0.refs_0_.keys, ...), custom_call_target="tpu_custom_call" | custom-call | tf_op jit(solution)/shard_map/pallas_call | solution.py:65
  13.4 1.4 %collective-permute-done.3.refs_3_ = f32[128,128]{1,0:T(8,128)S(1)} collective-permute-done((f32[128,128]{1,0:T(8,128)S(1)}, f32[128,128]{1,0:T(8,128)S(1)}, u32[]{:S(2)}, u32[]{:S(2)}) %collective-permute-start.3) | collective-permute-done | bytes 65568 | tf_op jit(solution)/shard_map/ppermute | solution.py:321
  14.9 5.4 %collective-permute-start.4 = (f32[128,128]{1,0:T(8,128)S(1)}, f32[128,128]{1,0:T(8,128)S(1)}, u32[]{:S(2)}, u32[]{:S(2)}) collective-permute-start(f32[128,128]{1,0:T(8,128)S(1)} %shard_map.80.refs_0_), channel_id=1, source_target_pairs={{0,48},{8,56},{16,32},{24,40},{32,16},{40,24},{48,0},{56,8},{1,49}... | collective-permute-start | bytes 196616 | tf_op jit(solution)/shard_map/ppermute | solution.py:321
  20.3 1.7 %collective-permute-done.4.refs_1_.refs_4_ = f32[128,128]{1,0:T(8,128)S(1)} collective-permute-done((f32[128,128]{1,0:T(8,128)S(1)}, f32[128,128]{1,0:T(8,128)S(1)}, u32[]{:S(2)}, u32[]{:S(2)}) %collective-permute-start.4) | collective-permute-done | bytes 65568 | tf_op jit(solution)/shard_map/ppermute | solution.py:321
  22.0 2.8 %collective-permute-start.7 = (f32[128,128]{1,0:T(8,128)S(1)}, f32[128,128]{1,0:T(8,128)S(1)}, u32[]{:S(2)}, u32[]{:S(2)}) collective-permute-start(f32[128,128]{1,0:T(8,128)S(1)} %shard_map.81), channel_id=1, source_target_pairs={{0,192},{64,128},{128,64},{192,0},{1,193},{65,129},{129,65},{193,1... | collective-permute-start | bytes 196616 | tf_op jit(solution)/shard_map/ppermute | solution.py:321
  25.5 1.0 %collective-permute-done.7.refs_7_ = f32[128,128]{1,0:T(8,128)S(1)} collective-permute-done((f32[128,128]{1,0:T(8,128)S(1)}, f32[128,128]{1,0:T(8,128)S(1)}, u32[]{:S(2)}, u32[]{:S(2)}) %collective-permute-start.7) | collective-permute-done | bytes 65568 | tf_op jit(solution)/shard_map/ppermute | solution.py:321
  26.5 3.1 %collective-permute-done.6.refs_6_ = f32[128,128]{1,0:T(8,128)S(1)} collective-permute-done((f32[128,128]{1,0:T(8,128)S(1)}, f32[128,128]{1,0:T(8,128)S(1)}, u32[]{:S(2)}, u32[]{:S(2)}) %collective-permute-start.6) | collective-permute-done | bytes 65568 | tf_op jit(solution)/shard_map/ppermute | solution.py:321
  29.7 1.9 %collective-permute-start.9 = (f32[128,128]{1,0:T(8,128)S(1)}, f32[128,128]{1,0:T(8,128)S(1)}, u32[]{:S(2)}, u32[]{:S(2)}) collective-permute-start(f32[128,128]{1,0:T(8,128)S(1)} %get-tuple-element.69), channel_id=1, source_target_pairs={{0,16},{8,24},{16,0},{24,8},{1,17},{9,25},{17,1},{25,9},{2,18},{10... | collective-permute-start | bytes 196616 | tf_op jit(solution)/shard_map/ppermute | solution.py:321
  31.6 1.7 %collective-permute-start.10 = (f32[128,128]{1,0:T(8,128)S(1)}, f32[128,128]{1,0:T(8,128)S(1)}, u32[]{:S(2)}, u32[]{:S(2)}) collective-permute-start(f32[128,128]{1,0:T(8,128)S(1)} %get-tuple-element.70), channel_id=1, source_target_pairs={{0,24},{8,16},{16,8},{24,0},{1,25},{9,17},{17,9},{25,1},{2,26},{10... | collective-permute-start | bytes 196616 | tf_op jit(solution)/shard_map/ppermute | solution.py:321
  33.2 0.6 collective-permute-done.9.refs_2_
  33.8 2.7 %collective-permute-done.10.refs_3_ = f32[128,128]{1,0:T(8,128)S(1)} collective-permute-done((f32[128,128]{1,0:T(8,128)S(1)}, f32[128,128]{1,0:T(8,128)S(1)}, u32[]{:S(2)}, u32[]{:S(2)}) %collective-permute-start.10) | collective-permute-done | bytes 65568 | tf_op jit(solution)/shard_map/ppermute | solution.py:321
  36.6 5.3 %collective-permute-start.11 = (f32[4,128,128]{2,1,0:T(8,128)S(1)}, f32[4,128,128]{2,1,0:T(8,128)S(1)}, u32[]{:S(2)}, u32[]{:S(2)}) collective-permute-start(f32[4,128,128]{2,1,0:T(8,128)S(1)} %get-tuple-element.74), channel_id=1, source_target_pairs={{0,4},{4,0},{1,5},{5,1},{2,6},{6,2},{3,7},{7,3},{8,12},{12,8},{9,1... | collective-permute-start | bytes 786440 | tf_op jit(solution)/shard_map/ppermute | solution.py:321
  42.3 0.8 collective-permute-done.11.state
  43.5 2.6 %collective-permute-start.14 = (f32[2,256]{1,0:T(2,128)S(1)}, f32[2,256]{1,0:T(2,128)S(1)}, u32[]{:S(2)}, u32[]{:S(2)}) collective-permute-start(f32[2,256]{1,0:T(2,128)S(1)} %get-tuple-element.77.sums_3), channel_id=1, source_target_pairs={{0,3},{1,2},{2,1},{3,0},{4,7},{5,6},{6,5},{7,4},{8,11},{9,10},{10,... | collective-permute-start | bytes 6152 | tf_op jit(solution)/shard_map/ppermute | solution.py:321
  46.0 0.5 collective-permute-start.13
  47.2 2.8 %collective-permute-done.13.sums_1 = f32[2,256]{1,0:T(2,128)S(1)} collective-permute-done((f32[2,256]{1,0:T(2,128)S(1)}, f32[2,256]{1,0:T(2,128)S(1)}, u32[]{:S(2)}, u32[]{:S(2)}) %collective-permute-start.13) | collective-permute-done | bytes 2080 | tf_op jit(solution)/shard_map/ppermute | solution.py:321
  50.0 0.4 shard_map.87
  50.4 1.9 %collective-permute-start.15 = (f32[4,128,128]{2,1,0:T(8,128)S(1)}, f32[4,128,128]{2,1,0:T(8,128)S(1)}, u32[]{:S(2)}, u32[]{:S(2)}) collective-permute-start(f32[4,128,128]{2,1,0:T(8,128)S(1)} %get-tuple-element.84), channel_id=1, source_target_pairs={{0,4},{4,0},{1,5},{5,1},{2,6},{6,2},{3,7},{7,3},{8,12},{12,8},{9,1... | collective-permute-start | bytes 786440 | tf_op jit(solution)/shard_map/ppermute | solution.py:321
  52.3 0.4 shard_map.86
  52.7 0.7 collective-permute-done.15.got.refs_5_
  53.5 0.6 collective-permute-start.16
  54.1 1.6 %collective-permute-start.17 = (f32[128,128]{1,0:T(8,128)S(1)}, f32[128,128]{1,0:T(8,128)S(1)}, u32[]{:S(2)}, u32[]{:S(2)}) collective-permute-start(f32[128,128]{1,0:T(8,128)S(1)} %get-tuple-element.89), channel_id=1, source_target_pairs={{0,16},{8,24},{16,0},{24,8},{1,17},{9,25},{17,1},{25,9},{2,18},{10... | collective-permute-start | bytes 196616 | tf_op jit(solution)/shard_map/ppermute | solution.py:321
  55.7 1.6 %collective-permute-start.18 = (f32[128,128]{1,0:T(8,128)S(1)}, f32[128,128]{1,0:T(8,128)S(1)}, u32[]{:S(2)}, u32[]{:S(2)}) collective-permute-start(f32[128,128]{1,0:T(8,128)S(1)} %get-tuple-element.90), channel_id=1, source_target_pairs={{0,24},{8,16},{16,8},{24,0},{1,25},{9,17},{17,9},{25,1},{2,26},{10... | collective-permute-start | bytes 196616 | tf_op jit(solution)/shard_map/ppermute | solution.py:321
  57.3 0.9 %shard_map.90 = (f32[256,512]{1,0:T(8,128)S(1)}, f32[256,512]{1,0:T(8,128)S(1)}) custom-call(bf16[256,1024]{1,0:T(8,128)(2,1)S(1)} %get-tuple-element.61.refs_6_.queries, bf16[256,512]{1,0:T(8,128)(2,1)S(1)} %get-tuple-element.55.keys_1.refs_1_.keys, bf16[256,512]{1,0:T(8,128)(2,1)S(1)} %get-tuple-element.57.values_1.refs_3_.values, ...), custom_call_target="tpu_custom_call" | custom-call | tf_op jit(solution)/shard_map/pallas_call | solution.py:65
  58.3 0.9 %shard_map.91 = (f32[256,512]{1,0:T(8,128)S(1)}, f32[256,512]{1,0:T(8,128)S(1)}) custom-call(bf16[256,1024]{1,0:T(8,128)(2,1)S(1)} %get-tuple-element.61.refs_6_.queries, bf16[256,512]{1,0:T(8,128)(2,1)S(1)} %get-tuple-element.54.keys_0.refs_0_.keys, bf16[256,512]{1,0:T(8,128)(2,1)S(1)} %get-tuple-element.56.values_0.refs_2_.values.refs_1_, ...), custom_call_target="tpu_custom_call" | custom-call | tf_op jit(solution)/shard_map/pallas_call | solution.py:65
  59.2 3.0 %shard_map.89.refs_0_ = bf16[256,1024]{1,0:T(8,128)(2,1)} custom-call(bf16[256,512]{1,0:T(8,128)(2,1)S(1)} %get-tuple-element.54.keys_0.refs_0_.keys, bf16[256,512]{1,0:T(8,128)(2,1)S(1)} %get-tuple-element.55.keys_1.refs_1_.keys, bf16[256,512]{1,0:T(8,128)(2,1)S(1)} %get-tuple-element.56.values_0.refs_2_.values.refs_1_, ...), custom_call_target="tpu_custom_call" | custom-call | tf_op jit(solution)/shard_map/pallas_call | solution.py:65
  62.2 3.2 %collective-permute-start.19 = (f32[128,128]{1,0:T(8,128)S(1)}, f32[128,128]{1,0:T(8,128)S(1)}, u32[]{:S(2)}, u32[]{:S(2)}) collective-permute-start(f32[128,128]{1,0:T(8,128)S(1)} %shard_map.92.refs_0_), channel_id=1, source_target_pairs={{0,48},{8,56},{16,32},{24,40},{32,16},{40,24},{48,0},{56,8},{1,49}... | collective-permute-start | bytes 196616 | tf_op jit(solution)/shard_map/ppermute | solution.py:321
  65.4 2.2 %collective-permute-done.19.refs_1_.refs_4_ = f32[128,128]{1,0:T(8,128)S(1)} collective-permute-done((f32[128,128]{1,0:T(8,128)S(1)}, f32[128,128]{1,0:T(8,128)S(1)}, u32[]{:S(2)}, u32[]{:S(2)}) %collective-permute-start.19) | collective-permute-done | bytes 65568 | tf_op jit(solution)/shard_map/ppermute | solution.py:321
  67.6 1.1 %collective-permute-start.22 = (f32[128,128]{1,0:T(8,128)S(1)}, f32[128,128]{1,0:T(8,128)S(1)}, u32[]{:S(2)}, u32[]{:S(2)}) collective-permute-start(f32[128,128]{1,0:T(8,128)S(1)} %shard_map.93), channel_id=1, source_target_pairs={{0,192},{64,128},{128,64},{192,0},{1,193},{65,129},{129,65},{193,1... | collective-permute-start | bytes 196616 | tf_op jit(solution)/shard_map/ppermute | solution.py:321
  68.7 0.8 collective-permute-start.21
  69.5 1.4 %collective-permute-start.20 = (f32[128,128]{1,0:T(8,128)S(1)}, f32[128,128]{1,0:T(8,128)S(1)}, u32[]{:S(2)}, u32[]{:S(2)}) collective-permute-start(f32[128,128]{1,0:T(8,128)S(1)} %shard_map.93), channel_id=1, source_target_pairs={{0,64},{64,0},{128,192},{192,128},{1,65},{65,1},{129,193},{193,129... | collective-permute-start | bytes 196616 | tf_op jit(solution)/shard_map/ppermute | solution.py:321
  71.0 1.1 %collective-permute-done.22.refs_7_ = f32[128,128]{1,0:T(8,128)S(1)} collective-permute-done((f32[128,128]{1,0:T(8,128)S(1)}, f32[128,128]{1,0:T(8,128)S(1)}, u32[]{:S(2)}, u32[]{:S(2)}) %collective-permute-start.22) | collective-permute-done | bytes 65568 | tf_op jit(solution)/shard_map/ppermute | solution.py:321
  72.0 1.3 %collective-permute-done.21.refs_6_ = f32[128,128]{1,0:T(8,128)S(1)} collective-permute-done((f32[128,128]{1,0:T(8,128)S(1)}, f32[128,128]{1,0:T(8,128)S(1)}, u32[]{:S(2)}, u32[]{:S(2)}) %collective-permute-start.21) | collective-permute-done | bytes 65568 | tf_op jit(solution)/shard_map/ppermute | solution.py:321
  73.4 0.6 collective-permute-start.23
  74.0 1.4 %collective-permute-start.24 = (f32[128,128]{1,0:T(8,128)S(1)}, f32[128,128]{1,0:T(8,128)S(1)}, u32[]{:S(2)}, u32[]{:S(2)}) collective-permute-start(f32[128,128]{1,0:T(8,128)S(1)} %get-tuple-element.95), channel_id=1, source_target_pairs={{0,16},{8,24},{16,0},{24,8},{1,17},{9,25},{17,1},{25,9},{2,18},{10... | collective-permute-start | bytes 196616 | tf_op jit(solution)/shard_map/ppermute | solution.py:321
  75.4 1.6 %collective-permute-start.25 = (f32[128,128]{1,0:T(8,128)S(1)}, f32[128,128]{1,0:T(8,128)S(1)}, u32[]{:S(2)}, u32[]{:S(2)}) collective-permute-start(f32[128,128]{1,0:T(8,128)S(1)} %get-tuple-element.96), channel_id=1, source_target_pairs={{0,24},{8,16},{16,8},{24,0},{1,25},{9,17},{17,9},{25,1},{2,26},{10... | collective-permute-start | bytes 196616 | tf_op jit(solution)/shard_map/ppermute | solution.py:321
  77.1 1.0 %collective-permute-done.24.refs_2_ = f32[128,128]{1,0:T(8,128)S(1)} collective-permute-done((f32[128,128]{1,0:T(8,128)S(1)}, f32[128,128]{1,0:T(8,128)S(1)}, u32[]{:S(2)}, u32[]{:S(2)}) %collective-permute-start.24) | collective-permute-done | bytes 65568 | tf_op jit(solution)/shard_map/ppermute | solution.py:321
  78.0 2.3 %collective-permute-done.25.refs_3_ = f32[128,128]{1,0:T(8,128)S(1)} collective-permute-done((f32[128,128]{1,0:T(8,128)S(1)}, f32[128,128]{1,0:T(8,128)S(1)}, u32[]{:S(2)}, u32[]{:S(2)}) %collective-permute-start.25) | collective-permute-done | bytes 65568 | tf_op jit(solution)/shard_map/ppermute | solution.py:321
  80.5 5.6 %collective-permute-start.26 = (f32[4,128,128]{2,1,0:T(8,128)S(1)}, f32[4,128,128]{2,1,0:T(8,128)S(1)}, u32[]{:S(2)}, u32[]{:S(2)}) collective-permute-start(f32[4,128,128]{2,1,0:T(8,128)S(1)} %get-tuple-element.97), channel_id=1, source_target_pairs={{0,4},{4,0},{1,5},{5,1},{2,6},{6,2},{3,7},{7,3},{8,12},{12,8},{9,1... | collective-permute-start | bytes 786440 | tf_op jit(solution)/shard_map/ppermute | solution.py:321
  86.1 0.4 shard_map.96
  86.5 0.7 collective-permute-done.26.state
  87.3 1.6 %shard_map.97 = (bf16[256,1024]{1,0:T(8,128)(2,1)}, bf16[256,1024]{1,0:T(8,128)(2,1)}) custom-call(bf16[256,512]{1,0:T(8,128)(2,1)S(1)} %get-tuple-element.55.keys_1.refs_1_.keys, bf16[256,512]{1,0:T(8,128)(2,1)S(1)} %get-tuple-element.57.values_1.refs_3_.values, f32[256,512]{1,0:T(8,128)S(1)} %get-tuple-element.86.refs_7_.key_inner, ...), custom_call_target="tpu_custom_call" | custom-call | tf_op jit(solution)/shard_map/pallas_call | solution.py:65
  (31 shorter events, 2.8 us)
Async XLA Ops:
  2.0 4.7 %collective-permute-start = (f32[4,128,128]{2,1,0:T(8,128)S(1)}, f32[4,128,128]{2,1,0:T(8,128)S(1)}, u32[]{:S(2)}, u32[]{:S(2)}) collective-permute-start(f32[4,128,128]{2,1,0:T(8,128)S(1)} %get-tuple-element.59), channel_id=1, source_target_pairs={{0,4},{4,0},{1,5},{5,1},{2,6},{6,2},{3,7},{7,3},{8,12},{12,8},{9,1... | collective-permute-start | bytes 786440 | tf_op jit(solution)/shard_map/ppermute | solution.py:321
  6.8 3.7 %copy-start = (bf16[1024]{0:T(1024)(128)(2,1)S(1)}, bf16[1024]{0:T(1024)(128)(2,1)}, u32[]{:S(2)}) copy-start(bf16[1024]{0:T(1024)(128)(2,1)} %param.9) | copy-start | bytes 6148
  6.8 6.6 %collective-permute-start.1 = (f32[128,128]{1,0:T(8,128)S(1)}, f32[128,128]{1,0:T(8,128)S(1)}, u32[]{:S(2)}, u32[]{:S(2)}) collective-permute-start(f32[128,128]{1,0:T(8,128)S(1)} %get-tuple-element.64), channel_id=1, source_target_pairs={{0,8},{8,0},{16,24},{24,16},{1,9},{9,1},{17,25},{25,17},{2,10},{10... | collective-permute-start | bytes 196616 | tf_op jit(solution)/shard_map/ppermute | solution.py:321
  6.9 6.5 %collective-permute-start.2 = (f32[128,128]{1,0:T(8,128)S(1)}, f32[128,128]{1,0:T(8,128)S(1)}, u32[]{:S(2)}, u32[]{:S(2)}) collective-permute-start(f32[128,128]{1,0:T(8,128)S(1)} %get-tuple-element.65), channel_id=1, source_target_pairs={{0,16},{8,24},{16,0},{24,8},{1,17},{9,25},{17,1},{25,9},{2,18},{10... | collective-permute-start | bytes 196616 | tf_op jit(solution)/shard_map/ppermute | solution.py:321
  9.8 5.0 %collective-permute-start.3 = (f32[128,128]{1,0:T(8,128)S(1)}, f32[128,128]{1,0:T(8,128)S(1)}, u32[]{:S(2)}, u32[]{:S(2)}) collective-permute-start(f32[128,128]{1,0:T(8,128)S(1)} %get-tuple-element.66), channel_id=1, source_target_pairs={{0,24},{8,16},{16,8},{24,0},{1,25},{9,17},{17,9},{25,1},{2,26},{10... | collective-permute-start | bytes 196616 | tf_op jit(solution)/shard_map/ppermute | solution.py:321
  14.9 7.1 %collective-permute-start.4 = (f32[128,128]{1,0:T(8,128)S(1)}, f32[128,128]{1,0:T(8,128)S(1)}, u32[]{:S(2)}, u32[]{:S(2)}) collective-permute-start(f32[128,128]{1,0:T(8,128)S(1)} %shard_map.80.refs_0_), channel_id=1, source_target_pairs={{0,48},{8,56},{16,32},{24,40},{32,16},{40,24},{48,0},{56,8},{1,49}... | collective-permute-start | bytes 196616 | tf_op jit(solution)/shard_map/ppermute | solution.py:321
  22.0 4.5 %collective-permute-start.7 = (f32[128,128]{1,0:T(8,128)S(1)}, f32[128,128]{1,0:T(8,128)S(1)}, u32[]{:S(2)}, u32[]{:S(2)}) collective-permute-start(f32[128,128]{1,0:T(8,128)S(1)} %shard_map.81), channel_id=1, source_target_pairs={{0,192},{64,128},{128,64},{192,0},{1,193},{65,129},{129,65},{193,1... | collective-permute-start | bytes 196616 | tf_op jit(solution)/shard_map/ppermute | solution.py:321
  24.8 4.7 %collective-permute-start.6 = (f32[128,128]{1,0:T(8,128)S(1)}, f32[128,128]{1,0:T(8,128)S(1)}, u32[]{:S(2)}, u32[]{:S(2)}) collective-permute-start(f32[128,128]{1,0:T(8,128)S(1)} %shard_map.81), channel_id=1, source_target_pairs={{0,128},{64,192},{128,0},{192,64},{1,129},{65,193},{129,1},{193,65... | collective-permute-start | bytes 196616 | tf_op jit(solution)/shard_map/ppermute | solution.py:321
  25.1 4.4 %collective-permute-start.5 = (f32[128,128]{1,0:T(8,128)S(1)}, f32[128,128]{1,0:T(8,128)S(1)}, u32[]{:S(2)}, u32[]{:S(2)}) collective-permute-start(f32[128,128]{1,0:T(8,128)S(1)} %shard_map.81), channel_id=1, source_target_pairs={{0,64},{64,0},{128,192},{192,128},{1,65},{65,1},{129,193},{193,129... | collective-permute-start | bytes 196616 | tf_op jit(solution)/shard_map/ppermute | solution.py:321
  29.6 3.6 %collective-permute-start.8 = (f32[128,128]{1,0:T(8,128)S(1)}, f32[128,128]{1,0:T(8,128)S(1)}, u32[]{:S(2)}, u32[]{:S(2)}) collective-permute-start(f32[128,128]{1,0:T(8,128)S(1)} %get-tuple-element.68), channel_id=1, source_target_pairs={{0,8},{8,0},{16,24},{24,16},{1,9},{9,1},{17,25},{25,17},{2,10},{10... | collective-permute-start | bytes 196616 | tf_op jit(solution)/shard_map/ppermute | solution.py:321
  29.7 4.1 %collective-permute-start.9 = (f32[128,128]{1,0:T(8,128)S(1)}, f32[128,128]{1,0:T(8,128)S(1)}, u32[]{:S(2)}, u32[]{:S(2)}) collective-permute-start(f32[128,128]{1,0:T(8,128)S(1)} %get-tuple-element.69), channel_id=1, source_target_pairs={{0,16},{8,24},{16,0},{24,8},{1,17},{9,25},{17,1},{25,9},{2,18},{10... | collective-permute-start | bytes 196616 | tf_op jit(solution)/shard_map/ppermute | solution.py:321
  31.6 5.0 %collective-permute-start.10 = (f32[128,128]{1,0:T(8,128)S(1)}, f32[128,128]{1,0:T(8,128)S(1)}, u32[]{:S(2)}, u32[]{:S(2)}) collective-permute-start(f32[128,128]{1,0:T(8,128)S(1)} %get-tuple-element.70), channel_id=1, source_target_pairs={{0,24},{8,16},{16,8},{24,0},{1,25},{9,17},{17,9},{25,1},{2,26},{10... | collective-permute-start | bytes 196616 | tf_op jit(solution)/shard_map/ppermute | solution.py:321
  36.6 6.4 %collective-permute-start.11 = (f32[4,128,128]{2,1,0:T(8,128)S(1)}, f32[4,128,128]{2,1,0:T(8,128)S(1)}, u32[]{:S(2)}, u32[]{:S(2)}) collective-permute-start(f32[4,128,128]{2,1,0:T(8,128)S(1)} %get-tuple-element.74), channel_id=1, source_target_pairs={{0,4},{4,0},{1,5},{5,1},{2,6},{6,2},{3,7},{7,3},{8,12},{12,8},{9,1... | collective-permute-start | bytes 786440 | tf_op jit(solution)/shard_map/ppermute | solution.py:321
  43.5 3.7 %collective-permute-start.14 = (f32[2,256]{1,0:T(2,128)S(1)}, f32[2,256]{1,0:T(2,128)S(1)}, u32[]{:S(2)}, u32[]{:S(2)}) collective-permute-start(f32[2,256]{1,0:T(2,128)S(1)} %get-tuple-element.77.sums_3), channel_id=1, source_target_pairs={{0,3},{1,2},{2,1},{3,0},{4,7},{5,6},{6,5},{7,4},{8,11},{9,10},{10,... | collective-permute-start | bytes 6152 | tf_op jit(solution)/shard_map/ppermute | solution.py:321
  46.0 3.9 %collective-permute-start.13 = (f32[2,256]{1,0:T(2,128)S(1)}, f32[2,256]{1,0:T(2,128)S(1)}, u32[]{:S(2)}, u32[]{:S(2)}) collective-permute-start(f32[2,256]{1,0:T(2,128)S(1)} %get-tuple-element.77.sums_3), channel_id=1, source_target_pairs={{0,2},{1,3},{2,0},{3,1},{4,6},{5,7},{6,4},{7,5},{8,10},{9,11},{10,... | collective-permute-start | bytes 6152 | tf_op jit(solution)/shard_map/ppermute | solution.py:321
  46.6 3.4 %collective-permute-start.12 = (f32[2,256]{1,0:T(2,128)S(1)}, f32[2,256]{1,0:T(2,128)S(1)}, u32[]{:S(2)}, u32[]{:S(2)}) collective-permute-start(f32[2,256]{1,0:T(2,128)S(1)} %get-tuple-element.77.sums_3), channel_id=1, source_target_pairs={{0,1},{1,0},{2,3},{3,2},{4,5},{5,4},{6,7},{7,6},{8,9},{9,8},{10,11... | collective-permute-start | bytes 6152 | tf_op jit(solution)/shard_map/ppermute | solution.py:321
  50.4 3.1 %collective-permute-start.15 = (f32[4,128,128]{2,1,0:T(8,128)S(1)}, f32[4,128,128]{2,1,0:T(8,128)S(1)}, u32[]{:S(2)}, u32[]{:S(2)}) collective-permute-start(f32[4,128,128]{2,1,0:T(8,128)S(1)} %get-tuple-element.84), channel_id=1, source_target_pairs={{0,4},{4,0},{1,5},{5,1},{2,6},{6,2},{3,7},{7,3},{8,12},{12,8},{9,1... | collective-permute-start | bytes 786440 | tf_op jit(solution)/shard_map/ppermute | solution.py:321
  53.5 8.7 %collective-permute-start.16 = (f32[128,128]{1,0:T(8,128)S(1)}, f32[128,128]{1,0:T(8,128)S(1)}, u32[]{:S(2)}, u32[]{:S(2)}) collective-permute-start(f32[128,128]{1,0:T(8,128)S(1)} %get-tuple-element.88), channel_id=1, source_target_pairs={{0,8},{8,0},{16,24},{24,16},{1,9},{9,1},{17,25},{25,17},{2,10},{10... | collective-permute-start | bytes 196616 | tf_op jit(solution)/shard_map/ppermute | solution.py:321
  54.1 8.1 %collective-permute-start.17 = (f32[128,128]{1,0:T(8,128)S(1)}, f32[128,128]{1,0:T(8,128)S(1)}, u32[]{:S(2)}, u32[]{:S(2)}) collective-permute-start(f32[128,128]{1,0:T(8,128)S(1)} %get-tuple-element.89), channel_id=1, source_target_pairs={{0,16},{8,24},{16,0},{24,8},{1,17},{9,25},{17,1},{25,9},{2,18},{10... | collective-permute-start | bytes 196616 | tf_op jit(solution)/shard_map/ppermute | solution.py:321
  55.7 6.5 %collective-permute-start.18 = (f32[128,128]{1,0:T(8,128)S(1)}, f32[128,128]{1,0:T(8,128)S(1)}, u32[]{:S(2)}, u32[]{:S(2)}) collective-permute-start(f32[128,128]{1,0:T(8,128)S(1)} %get-tuple-element.90), channel_id=1, source_target_pairs={{0,24},{8,16},{16,8},{24,0},{1,25},{9,17},{17,9},{25,1},{2,26},{10... | collective-permute-start | bytes 196616 | tf_op jit(solution)/shard_map/ppermute | solution.py:321
  62.2 5.4 %collective-permute-start.19 = (f32[128,128]{1,0:T(8,128)S(1)}, f32[128,128]{1,0:T(8,128)S(1)}, u32[]{:S(2)}, u32[]{:S(2)}) collective-permute-start(f32[128,128]{1,0:T(8,128)S(1)} %shard_map.92.refs_0_), channel_id=1, source_target_pairs={{0,48},{8,56},{16,32},{24,40},{32,16},{40,24},{48,0},{56,8},{1,49}... | collective-permute-start | bytes 196616 | tf_op jit(solution)/shard_map/ppermute | solution.py:321
  67.6 4.4 %collective-permute-start.22 = (f32[128,128]{1,0:T(8,128)S(1)}, f32[128,128]{1,0:T(8,128)S(1)}, u32[]{:S(2)}, u32[]{:S(2)}) collective-permute-start(f32[128,128]{1,0:T(8,128)S(1)} %shard_map.93), channel_id=1, source_target_pairs={{0,192},{64,128},{128,64},{192,0},{1,193},{65,129},{129,65},{193,1... | collective-permute-start | bytes 196616 | tf_op jit(solution)/shard_map/ppermute | solution.py:321
  68.7 4.6 %collective-permute-start.21 = (f32[128,128]{1,0:T(8,128)S(1)}, f32[128,128]{1,0:T(8,128)S(1)}, u32[]{:S(2)}, u32[]{:S(2)}) collective-permute-start(f32[128,128]{1,0:T(8,128)S(1)} %shard_map.93), channel_id=1, source_target_pairs={{0,128},{64,192},{128,0},{192,64},{1,129},{65,193},{129,1},{193,65... | collective-permute-start | bytes 196616 | tf_op jit(solution)/shard_map/ppermute | solution.py:321
  69.5 3.8 %collective-permute-start.20 = (f32[128,128]{1,0:T(8,128)S(1)}, f32[128,128]{1,0:T(8,128)S(1)}, u32[]{:S(2)}, u32[]{:S(2)}) collective-permute-start(f32[128,128]{1,0:T(8,128)S(1)} %shard_map.93), channel_id=1, source_target_pairs={{0,64},{64,0},{128,192},{192,128},{1,65},{65,1},{129,193},{193,129... | collective-permute-start | bytes 196616 | tf_op jit(solution)/shard_map/ppermute | solution.py:321
  73.4 3.6 %collective-permute-start.23 = (f32[128,128]{1,0:T(8,128)S(1)}, f32[128,128]{1,0:T(8,128)S(1)}, u32[]{:S(2)}, u32[]{:S(2)}) collective-permute-start(f32[128,128]{1,0:T(8,128)S(1)} %get-tuple-element.94), channel_id=1, source_target_pairs={{0,8},{8,0},{16,24},{24,16},{1,9},{9,1},{17,25},{25,17},{2,10},{10... | collective-permute-start | bytes 196616 | tf_op jit(solution)/shard_map/ppermute | solution.py:321
  74.0 4.0 %collective-permute-start.24 = (f32[128,128]{1,0:T(8,128)S(1)}, f32[128,128]{1,0:T(8,128)S(1)}, u32[]{:S(2)}, u32[]{:S(2)}) collective-permute-start(f32[128,128]{1,0:T(8,128)S(1)} %get-tuple-element.95), channel_id=1, source_target_pairs={{0,16},{8,24},{16,0},{24,8},{1,17},{9,25},{17,1},{25,9},{2,18},{10... | collective-permute-start | bytes 196616 | tf_op jit(solution)/shard_map/ppermute | solution.py:321
  75.4 4.9 %collective-permute-start.25 = (f32[128,128]{1,0:T(8,128)S(1)}, f32[128,128]{1,0:T(8,128)S(1)}, u32[]{:S(2)}, u32[]{:S(2)}) collective-permute-start(f32[128,128]{1,0:T(8,128)S(1)} %get-tuple-element.96), channel_id=1, source_target_pairs={{0,24},{8,16},{16,8},{24,0},{1,25},{9,17},{17,9},{25,1},{2,26},{10... | collective-permute-start | bytes 196616 | tf_op jit(solution)/shard_map/ppermute | solution.py:321
  80.5 6.8 %collective-permute-start.26 = (f32[4,128,128]{2,1,0:T(8,128)S(1)}, f32[4,128,128]{2,1,0:T(8,128)S(1)}, u32[]{:S(2)}, u32[]{:S(2)}) collective-permute-start(f32[4,128,128]{2,1,0:T(8,128)S(1)} %get-tuple-element.97), channel_id=1, source_target_pairs={{0,4},{4,0},{1,5},{5,1},{2,6},{6,2},{3,7},{7,3},{8,12},{12,8},{9,1... | collective-permute-start | bytes 786440 | tf_op jit(solution)/shard_map/ppermute | solution.py:321

commit v5 on v4

--- a/solution.py
+++ b/solution.py
@@ -17,6 +17,7 @@
 F32 = jnp.float32
 BF16 = jnp.bfloat16
 VMEM_LIMIT = 16 * 1024 * 1024
+STEPS = ((3,), (2, 1, 0))
 
 
 def dot_nn(a, b):
@@ -33,6 +34,11 @@
 
 def columns(head):
     return pl.ds(head * HEAD_DIM, HEAD_DIM)
+
+
+def columns_of(part, step, heads):
+    head = part * heads + (owner() ^ step)
+    return pl.ds(pl.multiple_of(head * HEAD_DIM, HEAD_DIM), HEAD_DIM)
 
 
 def blocks(tokens):
@@ -87,29 +93,44 @@
     return [pltpu.make_async_copy(there, at, sem) for there, at, sem in halves(far, near, sems)]
 
 
-def totals_kernel(part, keys_far, values_far, out, sooner, keys, values, sems):
-    chunks = sems.shape[1]
-    rows = keys.shape[0] // chunks
-    half = keys.shape[1]
-    core = 1 - here("core") if part else here("core")
-    there = pl.ds(pl.multiple_of(core * half, half), half)
+def key_value_states(keys, values, first, rest, sooner):
+    heads = keys.shape[1] // HEAD_DIM
+    for out, steps in zip((first, rest), STEPS):
+        for index, step in enumerate(steps):
+            at = columns_of(0, step, heads)
+            total = jnp.zeros(out.shape[1:], F32)
+            for block, rows in enumerate(blocks(keys.shape[0])):
+                if block:
+                    sooner[owner() ^ step, block - 1] = total
+                total = total + dot_tn(keys[rows, at], values[rows, at])
+            out[index] = total
+
+
+def other_totals_kernel(
+    keys_far, values_far, first, rest, sooner, keys_0, keys_1, values_0, values_1, sems
+):
+    chunks = sems.shape[2]
+    rows = keys_0.shape[0] // chunks
+    half = keys_0.shape[1]
     copies = []
-    for chunk in range(chunks):
-        at = pl.ds(chunk * rows, rows)
-        for which, (far, near) in enumerate(((keys_far, keys), (values_far, values))):
-            copy = pltpu.make_async_copy(far.at[at, there], near.at[at], sems.at[which, chunk])
-            copy.start()
-            copies.append(copy)
-    for copy in copies:
+    for part, arrays in ((1, (keys_1, values_1)), (0, (keys_0, values_0))):
+        core = 1 - here("core") if part else here("core")
+        there = pl.ds(pl.multiple_of(core * half, half), half)
+        group = []
+        for which, (far, near) in enumerate(zip((keys_far, values_far), arrays)):
+            for chunk in range(chunks):
+                at = pl.ds(chunk * rows, rows)
+                copy = pltpu.make_async_copy(
+                    far.at[at, there], near.at[at], sems.at[part, which, chunk]
+                )
+                copy.start()
+                group.append(copy)
+        copies.append(group)
+    for copy in copies[0]:
         copy.wait()
-    for head in range(out.shape[0]):
-        at = columns(head)
-        total = jnp.zeros(out.shape[1:], F32)
-        for block, rows in enumerate(blocks(keys.shape[0])):
-            if block:
-                sooner[head, block - 1] = total
-            total = total + dot_tn(keys[rows, at], values[rows, at])
-        out[head] = total
+    key_value_states(keys_1, values_1, first, rest, sooner)
+    for copy in copies[1]:
+        copy.wait()
 
 
 def within_kernel(
@@ -138,9 +159,8 @@
 
 
 def split_kernel(mine, got, *pieces):
-    for step, piece in enumerate(pieces):
-        at = owner() ^ step
-        piece[...] = mine[at] + got[at]
+    for index, piece in enumerate(pieces):
+        piece[...] = mine[index] + got[index]
 
 
 def join_kernel(skip, count, *refs):
@@ -168,13 +188,14 @@
         out[...] = result
 
 
-def merge_kernel(reverse, group, *refs):
-    back, (mine, got, own, theirs) = refs[:group], refs[group:]
+def merge_kernel(reverse, *refs):
+    *back, mine_0, mine_1, got_0, got_1, own, theirs = refs
     first = before(here("core"), 1 - here("core"), reverse)
-    for step in range(group):
-        at = owner() ^ step
-        own[at] = back[step][...] + jnp.where(first, 0.0, got[at])
-        theirs[at] = back[step][...] + jnp.where(first, mine[at], 0.0)
+    for mine, got, steps in ((mine_0, got_0, STEPS[0]), (mine_1, got_1, STEPS[1])):
+        for index, step in enumerate(steps):
+            at = owner() ^ step
+            own[at] = back[step][...] + jnp.where(first, 0.0, got[index])
+            theirs[at] = back[step][...] + jnp.where(first, mine[index], 0.0)
 
 
 def forward_kernel(part, queries, upstream, within, state, sooner, *refs):
@@ -204,27 +225,28 @@
         sums[row : row + 1] = total
 
 
-def delta_kernel(part, queries, upstream, output, sums, sums_1, sums_2, sums_3, delta, back, later):
+def delta_kernel(part, queries, upstream, output, *refs):
+    sums, (delta, first, rest, later) = refs[:4], refs[4:]
     tokens = queries.shape[0]
-    heads = back.shape[0]
-    total = sums[...] + sums_1[...] + sums_2[...] + sums_3[...]
+    heads = delta.shape[1] // HEAD_DIM
+    total = sums[0][...] + sums[1][...] + sums[2][...] + sums[3][...]
     inv_rms = lax.rsqrt(total[0:1] / FEATURES + EPSILON)
     pull = inv_rms * inv_rms * inv_rms * (total[1:2] / FEATURES)
     inv_rms = jnp.broadcast_to(inv_rms, (HEAD_DIM, tokens)).T
     pull = jnp.broadcast_to(pull, (HEAD_DIM, tokens)).T
-    for head in range(heads):
-        at = columns(part * heads + head)
-        out_delta = inv_rms * upstream[:, at] - pull * output[:, columns(head)]
-        out_delta = out_delta.astype(BF16)
-        delta[:, columns(head)] = out_delta
-        total = jnp.zeros(back.shape[1:], F32)
-        parts = blocks(tokens)
-        for block in reversed(range(len(parts))):
-            rows = parts[block]
-            if block + 1 < len(parts):
-                later[head, block] = total
-            total = total + dot_tn(out_delta[rows], queries[rows, at])
-        back[head] = total
+    for back, steps in zip((first, rest), STEPS):
+        for index, step in enumerate(steps):
+            at, near = columns_of(part, step, heads), columns_of(0, step, heads)
+            out_delta = (inv_rms * upstream[:, at] - pull * output[:, near]).astype(BF16)
+            delta[:, near] = out_delta
+            total = jnp.zeros(back.shape[1:], F32)
+            parts = blocks(tokens)
+            for block in reversed(range(len(parts))):
+                rows = parts[block]
+                if block + 1 < len(parts):
+                    later[owner() ^ step, block] = total
+                total = total + dot_tn(out_delta[rows], queries[rows, at])
+            back[index] = total
 
 
 def write(near, far, part, sem):
@@ -334,30 +356,31 @@
     return [there[step] for step in sorted(there)]
 
 
-def entering(mine, other, reverse, beside):
+def entering(mine, other, reverse, beside_first, beside_second):
     group, rows = lax.axis_size("low"), lax.axis_size("row")
     line, ring = (3, 2, 1), (1, 3, 2)
-    piece = near(mine.shape[1:])
-    got = swap(other, "core", 1)
-    parts = call(split_kernel, [piece] * group)(mine, got)
-    made = beside(parts[0])
+    piece = near(mine[0].shape[1:])
+    got = [swap(array, "core", 1) for array in other]
+    parts = {}
+    for steps, *arrays in zip(STEPS, mine, got):
+        parts.update(zip(steps, call(split_kernel, [piece] * len(steps))(*arrays)))
+    made = beside_first(parts[0])
     parts = [parts[0]] + swaps(parts, "low", line)
-    first, *ties = made
-    whole = call(functools.partial(join_kernel, int(reverse), group), piece, far=int(reverse))(
-        *((first, *parts) if reverse else (*parts, first)), *ties
-    )
+    whole = call(functools.partial(join_kernel, 0, group), piece)(*parts, *made)
+    second = beside_second(whole)
     mirror = swap(whole, ("high", "low"), group + group // 2)
-    whole = call(functools.partial(join_kernel, 0, 2), piece)(whole, mirror)
+    far = len(second)
+    whole = call(functools.partial(join_kernel, far, 2), piece, far=far)(*second, whole, mirror)
     there = swaps([whole] * rows, "row", ring)
     back = call(functools.partial(members_kernel, reverse, group, rows), [piece] * group)(
         *parts, mirror, *there
     )
     back = [back[0]] + swaps(back, "low", line)
-    half = near(mine.shape)
-    own, theirs = call(functools.partial(merge_kernel, reverse, group), (half, half))(
-        *back, mine, got
-    )
-    return (own, swap(theirs, "core", 1)), made
+    half = near((group * mine[0].shape[0], *mine[0].shape[1:]))
+    own, theirs = call(functools.partial(merge_kernel, reverse), (half, half))(
+        *back, *mine, *got
+    )
+    return (own, swap(theirs, "core", 1)), made, second
 
 
 def on_device(queries, keys, values, out_grad, gain):
@@ -373,19 +396,15 @@
     half_full = near((tokens, width // 2))
     sums_shape = near((2, tokens))
     grads = pltpu.HBM((tokens, width), BF16)
-    other, mine = (
-        call(
-            functools.partial(totals_kernel, part),
-            (half, inner_blocks, half_wide, half_wide),
-            far=2,
-            scratch_shapes=[pltpu.SemaphoreType.DMA((2, 4))],
-        )(keys, values)
-        for part in (1, 0)
-    )
-    mine, sooner_0, *near_0 = mine
-    other, sooner_1, *near_1 = other
-    sooner = sooner_0, sooner_1
-    keys, values = zip(near_0, near_1)
+    states = [near((len(steps), HEAD_DIM, HEAD_DIM)) for steps in STEPS]
+    *other, sooner_1, keys_0, keys_1, values_0, values_1 = call(
+        other_totals_kernel,
+        (*states, inner_blocks, *[half_wide] * 4),
+        far=2,
+        scratch_shapes=[pltpu.SemaphoreType.DMA((2, 2, 4))],
+    )(keys, values)
+    *mine, sooner_0 = call(key_value_states, (*states, inner_blocks))(keys_0, values_0)
+    sooner, keys, values = (sooner_0, sooner_1), (keys_0, keys_1), (values_0, values_1)
 
     def beside_forward(after):
         return call(
@@ -395,48 +414,54 @@
             scratch_shapes=[wide, near((1, width), BF16), pltpu.SemaphoreType.DMA((3, 2))],
         )(queries, out_grad, gain, *keys, *values, after)
 
-    states, (within, upstream, queries) = entering(mine, other, False, beside_forward)
+    entered, (within, upstream, queries), _ = entering(
+        mine, other, False, beside_forward, lambda after: ()
+    )
     outputs, lows, sums = [], [], []
-    for part, state in enumerate(states):
+    for part, state in enumerate(entered):
         output, low, *sums = call(
             functools.partial(forward_kernel, part), (half_full, half_low, sums_shape)
         )(queries, upstream, within, state, sooner[part], *sums)
         outputs.append(output)
         lows.append(low)
     sums = swaps(sums * lax.axis_size("head"), "head", (1, 3, 2)) + sums
-    deltas, backs, later = zip(
-        *(
-            call(functools.partial(delta_kernel, part), (half_wide, half, inner_blocks))(
-                queries, upstream, outputs[part], *sums
-            )
-            for part in (1, 0)
+    results = [
+        call(functools.partial(delta_kernel, part), (half_wide, *states, inner_blocks))(
+            queries, upstream, outputs[part], *sums
         )
-    )
-    deltas, backs, later = deltas[::-1], backs[::-1], later[::-1]
-
-    def beside_backward(after):
-        query_grad = call(
-            query_kernel,
-            grads,
-            scratch_shapes=[half_wide, half_wide, pltpu.SemaphoreType.DMA((2,))],
-        )(*keys, *values, *deltas, *lows, after)
-        inner = [
-            call(functools.partial(inner_kernel, part), (half_full, half_full))(
+        for part in (1, 0)
+    ][::-1]
+    deltas = [result[0] for result in results]
+    later = [result[3] for result in results]
+
+    def inner_grads(after):
+        made = []
+        for part in range(2):
+            made += call(functools.partial(inner_kernel, part), (half_full, half_full))(
                 queries, keys[part], values[part], deltas[part], after
             )
-            for part in range(2)
-        ]
-        return query_grad, *inner[0], *inner[1]
-
-    states, (query_grad, *inner) = entering(*backs, True, beside_backward)
+        return made
+
+    def query_grads(after):
+        return (
+            call(
+                query_kernel,
+                grads,
+                scratch_shapes=[half_wide, half_wide, pltpu.SemaphoreType.DMA((2,))],
+            )(*keys, *values, *deltas, *lows, after),
+        )
+
+    entered, inner, (query_grad,) = entering(
+        results[0][1:3], results[1][1:3], True, inner_grads, query_grads
+    )
     key_0, value_0 = call(backward_kernel, (half_wide, half_wide))(
-        keys[0], values[0], *inner[:2], states[0], later[0]
+        keys[0], values[0], *inner[:2], entered[0], later[0]
     )
     key_grad, value_grad = call(
         last_kernel,
         (grads, grads),
         scratch_shapes=[half_wide, half_wide, pltpu.SemaphoreType.DMA((4,))],
-    )(keys[1], values[1], *inner[2:], states[1], later[1], key_0, value_0)
+    )(keys[1], values[1], *inner[2:], entered[1], later[1], key_0, value_0)
     return query_grad, key_grad, value_grad
 
 

time: 89.3 us -> 88.3 us (0.989)
  waiting for transfers between devices: 23.8 us -> 25.8 us
  starting transfers between devices: 49.6 us -> 47.7 us
  Pallas kernels: 14 us -> 13.1 us
    ppermute x27 -> x29, waiting for transfers between devices: 23.8 us -> 25.8 us  [swap(): lax.ppermute(array, axis, [(at, at ^ distance) for at in range(count)])]
    ppermute x27 -> x29, starting transfers between devices: 49.6 us -> 47.7 us  [swap(): lax.ppermute(array, axis, [(at, at ^ distance) for at in range(count)])]
    pallas_call x22 -> x24, Pallas kernels: 14 us -> 13.1 us  [run(): pl.pallas_call(kernel, out_shape=out_shape, in_specs=[pl.BlockSpec(memory...]
  transfers between devices with their start and end apart: 27 -> 29, of which waited for: 16 -> 17; matrix products, arithmetic and copies ran while one was open for 1% -> 1% of each run, Pallas kernels for 11% -> 10%
where the time goes in v5:
time: 88.3 us; the launch traced here: 88.1 us
  starting transfers between devices  47.7 us (54%)
  waiting for transfers between devices  25.8 us (29%)
  Pallas kernels  13.1 us (15%)
  between operations  0.99 us (1%)
    ppermute x29, starting transfers between devices, swap(): lax.ppermute(array, axis, [(at, at ^ distance) for at in range(count)])  47.7 us
    ppermute x29, waiting for transfers between devices, swap(): lax.ppermute(array, axis, [(at, at ^ distance) for at in range(count)])  25.8 us
    pallas_call x24, Pallas kernels, run(): pl.pallas_call(kernel, out_shape=out_shape, in_specs=[pl.BlockSpec(memory...  13.1 us
  transfers between devices with their start and end apart: 29, of which 17 were waited for; matrix products, arithmetic and copies ran while one was open for 1% of the time, Pallas kernels for 10%

profile of v5, /device:TPU:1, one launch (start us, length us, event | category | flops | bytes accessed | tf_op | source)
XLA Modules:
  0.0 88.1 jit_solution(18406315374806880990)
XLA Ops:
  0.6 1.5 %shard_map.76 = (f32[1,128,128]{2,1,0:T(8,128)S(1)}, f32[3,128,128]{2,1,0:T(8,128)S(1)}, f32[4,1,128,128]{3,2,1,0:T(8,128)S(1)}, bf16[256,512]{1,0:T(8,128)(2,1)...) custom-call(bf16[256,1024]{1,0:T(8,128)(2,1)} %keys_far.1, ...), custom_call_target="tpu_custom_call" | custom-call | tf_op jit(solution)/shard_map/pallas_call | solution.py:71
  2.1 3.3 %collective-permute-start = (f32[3,128,128]{2,1,0:T(8,128)S(1)}, f32[3,128,128]{2,1,0:T(8,128)S(1)}, u32[]{:S(2)}, u32[]{:S(2)}) collective-permute-start(f32[3,128,128]{2,1,0:T(8,128)S(1)} %get-tuple-element.61), channel_id=1, source_target_pairs={{0,4},{4,0},{1,5},{5,1},{2,6},{6,2},{3,7},{7,3},{8,12},{12,8},{9,1... | collective-permute-start | bytes 589832 | tf_op jit(solution)/shard_map/ppermute | solution.py:343
  5.8 0.9 %collective-permute-done.3.got.refs_6_ = f32[1,128,128]{2,1,0:T(8,128)S(1)} collective-permute-done((f32[1,128,128]{2,1,0:T(8,128)S(1)}, f32[1,128,128]{2,1,0:T(8,128)S(1)}, u32[]{:S(2)}, u32[]{:S(2)}) %collective-permute-start.3) | collective-permute-done | bytes 65568 | tf_op jit(solution)/shard_map/ppermute | solution.py:343
  6.7 2.7 %collective-permute-start.4 = (f32[128,128]{1,0:T(8,128)S(1)}, f32[128,128]{1,0:T(8,128)S(1)}, u32[]{:S(2)}, u32[]{:S(2)}) collective-permute-start(f32[128,128]{1,0:T(8,128)S(1)} %shard_map.80), channel_id=1, source_target_pairs={{0,24},{8,16},{16,8},{24,0},{1,25},{9,17},{17,9},{25,1},{2,26},{10... | collective-permute-start | bytes 196616 | tf_op jit(solution)/shard_map/ppermute | solution.py:343
  9.6 0.9 %collective-permute-start.2 = (f32[128,128]{1,0:T(8,128)S(1)}, f32[128,128]{1,0:T(8,128)S(1)}, u32[]{:S(2)}, u32[]{:S(2)}) collective-permute-start(f32[128,128]{1,0:T(8,128)S(1)} %get-tuple-element.67), channel_id=1, source_target_pairs={{0,16},{8,24},{16,0},{24,8},{1,17},{9,25},{17,1},{25,9},{2,18},{10... | collective-permute-start | bytes 196616 | tf_op jit(solution)/shard_map/ppermute | solution.py:343
  10.5 0.6 reshape.9.gain_far
  11.1 2.3 %shard_map.79 = (f32[256,1024]{1,0:T(8,128)S(1)}, f32[256,1024]{1,0:T(8,128)S(1)}, bf16[256,1024]{1,0:T(8,128)(2,1)S(1)}) custom-call(bf16[256,1024]{1,0:T(8,128)(2,1)} %queries_far.1, bf16[256,1024]{1,0:T(8,128)(2,1)} %grad_far.1, bf16[1,1024]{1,0:T(2,128)(2,1)} %reshape.9.gain_far, bf16[256,512]{1,0:T(8,128)(2,1)S(1)} %get-tuple-element.56.keys.keys_0.refs_0_, ...), custom_call_target="tpu_custom_call" | custom-call | tf_op jit(solution)/shard_map/pallas_call | solution.py:71
  13.4 1.2 %collective-permute-done.1.refs_1_ = f32[128,128]{1,0:T(8,128)S(1)} collective-permute-done((f32[128,128]{1,0:T(8,128)S(1)}, f32[128,128]{1,0:T(8,128)S(1)}, u32[]{:S(2)}, u32[]{:S(2)}) %collective-permute-start.1) | collective-permute-done | bytes 65568 | tf_op jit(solution)/shard_map/ppermute | solution.py:343
  14.6 3.9 %collective-permute-start.5 = (f32[128,128]{1,0:T(8,128)S(1)}, f32[128,128]{1,0:T(8,128)S(1)}, u32[]{:S(2)}, u32[]{:S(2)}) collective-permute-start(f32[128,128]{1,0:T(8,128)S(1)} %shard_map.81.refs_0_), channel_id=1, source_target_pairs={{0,48},{8,56},{16,32},{24,40},{32,16},{40,24},{48,0},{56,8},{1,49}... | collective-permute-start | bytes 196616 | tf_op jit(solution)/shard_map/ppermute | solution.py:343
  18.5 1.7 %collective-permute-done.5.refs_1_.refs_4_ = f32[128,128]{1,0:T(8,128)S(1)} collective-permute-done((f32[128,128]{1,0:T(8,128)S(1)}, f32[128,128]{1,0:T(8,128)S(1)}, u32[]{:S(2)}, u32[]{:S(2)}) %collective-permute-start.5) | collective-permute-done | bytes 65568 | tf_op jit(solution)/shard_map/ppermute | solution.py:343
  20.2 2.8 %collective-permute-start.8 = (f32[128,128]{1,0:T(8,128)S(1)}, f32[128,128]{1,0:T(8,128)S(1)}, u32[]{:S(2)}, u32[]{:S(2)}) collective-permute-start(f32[128,128]{1,0:T(8,128)S(1)} %shard_map.82), channel_id=1, source_target_pairs={{0,192},{64,128},{128,64},{192,0},{1,193},{65,129},{129,65},{193,1... | collective-permute-start | bytes 196616 | tf_op jit(solution)/shard_map/ppermute | solution.py:343
  23.7 1.0 %collective-permute-done.8.refs_7_ = f32[128,128]{1,0:T(8,128)S(1)} collective-permute-done((f32[128,128]{1,0:T(8,128)S(1)}, f32[128,128]{1,0:T(8,128)S(1)}, u32[]{:S(2)}, u32[]{:S(2)}) %collective-permute-start.8) | collective-permute-done | bytes 65568 | tf_op jit(solution)/shard_map/ppermute | solution.py:343
  24.6 3.1 %collective-permute-done.7.refs_6_ = f32[128,128]{1,0:T(8,128)S(1)} collective-permute-done((f32[128,128]{1,0:T(8,128)S(1)}, f32[128,128]{1,0:T(8,128)S(1)}, u32[]{:S(2)}, u32[]{:S(2)}) %collective-permute-start.7) | collective-permute-done | bytes 65568 | tf_op jit(solution)/shard_map/ppermute | solution.py:343
  27.8 2.0 %collective-permute-start.9 = (f32[128,128]{1,0:T(8,128)S(1)}, f32[128,128]{1,0:T(8,128)S(1)}, u32[]{:S(2)}, u32[]{:S(2)}) collective-permute-start(f32[128,128]{1,0:T(8,128)S(1)} %get-tuple-element.71), channel_id=1, source_target_pairs={{0,8},{8,0},{16,24},{24,16},{1,9},{9,1},{17,25},{25,17},{2,10},{10... | collective-permute-start | bytes 196616 | tf_op jit(solution)/shard_map/ppermute | solution.py:343
  29.8 0.7 collective-permute-start.10
  30.5 1.4 %collective-permute-start.11 = (f32[128,128]{1,0:T(8,128)S(1)}, f32[128,128]{1,0:T(8,128)S(1)}, u32[]{:S(2)}, u32[]{:S(2)}) collective-permute-start(f32[128,128]{1,0:T(8,128)S(1)} %get-tuple-element.73), channel_id=1, source_target_pairs={{0,24},{8,16},{16,8},{24,0},{1,25},{9,17},{17,9},{25,1},{2,26},{10... | collective-permute-start | bytes 196616 | tf_op jit(solution)/shard_map/ppermute | solution.py:343
  31.9 2.5 %collective-permute-done.10.refs_2_ = f32[128,128]{1,0:T(8,128)S(1)} collective-permute-done((f32[128,128]{1,0:T(8,128)S(1)}, f32[128,128]{1,0:T(8,128)S(1)}, u32[]{:S(2)}, u32[]{:S(2)}) %collective-permute-start.10) | collective-permute-done | bytes 65568 | tf_op jit(solution)/shard_map/ppermute | solution.py:343
  34.5 1.1 %collective-permute-done.11.refs_3_ = f32[128,128]{1,0:T(8,128)S(1)} collective-permute-done((f32[128,128]{1,0:T(8,128)S(1)}, f32[128,128]{1,0:T(8,128)S(1)}, u32[]{:S(2)}, u32[]{:S(2)}) %collective-permute-start.11) | collective-permute-done | bytes 65568 | tf_op jit(solution)/shard_map/ppermute | solution.py:343
  35.6 5.0 %collective-permute-start.12 = (f32[4,128,128]{2,1,0:T(8,128)S(1)}, f32[4,128,128]{2,1,0:T(8,128)S(1)}, u32[]{:S(2)}, u32[]{:S(2)}) collective-permute-start(f32[4,128,128]{2,1,0:T(8,128)S(1)} %get-tuple-element.77), channel_id=1, source_target_pairs={{0,4},{4,0},{1,5},{5,1},{2,6},{6,2},{3,7},{7,3},{8,12},{12,8},{9,1... | collective-permute-start | bytes 786440 | tf_op jit(solution)/shard_map/ppermute | solution.py:343
  41.0 0.8 collective-permute-done.12.state
  42.2 2.6 %collective-permute-start.15 = (f32[2,256]{1,0:T(2,128)S(1)}, f32[2,256]{1,0:T(2,128)S(1)}, u32[]{:S(2)}, u32[]{:S(2)}) collective-permute-start(f32[2,256]{1,0:T(2,128)S(1)} %get-tuple-element.80.refs_3_), channel_id=1, source_target_pairs={{0,3},{1,2},{2,1},{3,0},{4,7},{5,6},{6,5},{7,4},{8,11},{9,10},{10,... | collective-permute-start | bytes 6152 | tf_op jit(solution)/shard_map/ppermute | solution.py:343
  44.7 0.5 collective-permute-start.14
  45.9 2.8 %collective-permute-done.14.refs_1_ = f32[2,256]{1,0:T(2,128)S(1)} collective-permute-done((f32[2,256]{1,0:T(2,128)S(1)}, f32[2,256]{1,0:T(2,128)S(1)}, u32[]{:S(2)}, u32[]{:S(2)}) %collective-permute-start.14) | collective-permute-done | bytes 2080 | tf_op jit(solution)/shard_map/ppermute | solution.py:343
  48.7 0.5 shard_map.88
  49.2 2.1 %collective-permute-start.16 = (f32[3,128,128]{2,1,0:T(8,128)S(1)}, f32[3,128,128]{2,1,0:T(8,128)S(1)}, u32[]{:S(2)}, u32[]{:S(2)}) collective-permute-start(f32[3,128,128]{2,1,0:T(8,128)S(1)} %get-tuple-element.87), channel_id=1, source_target_pairs={{0,4},{4,0},{1,5},{5,1},{2,6},{6,2},{3,7},{7,3},{8,12},{12,8},{9,1... | collective-permute-start | bytes 589832 | tf_op jit(solution)/shard_map/ppermute | solution.py:343
  51.3 0.5 shard_map.87
  51.8 0.7 collective-permute-done.19.got.refs_6_
  52.5 1.7 %collective-permute-start.20 = (f32[128,128]{1,0:T(8,128)S(1)}, f32[128,128]{1,0:T(8,128)S(1)}, u32[]{:S(2)}, u32[]{:S(2)}) collective-permute-start(f32[128,128]{1,0:T(8,128)S(1)} %shard_map.90), channel_id=1, source_target_pairs={{0,24},{8,16},{16,8},{24,0},{1,25},{9,17},{17,9},{25,1},{2,26},{10... | collective-permute-start | bytes 196616 | tf_op jit(solution)/shard_map/ppermute | solution.py:343
  54.4 1.9 %collective-permute-start.18 = (f32[128,128]{1,0:T(8,128)S(1)}, f32[128,128]{1,0:T(8,128)S(1)}, u32[]{:S(2)}, u32[]{:S(2)}) collective-permute-start(f32[128,128]{1,0:T(8,128)S(1)} %get-tuple-element.90), channel_id=1, source_target_pairs={{0,16},{8,24},{16,0},{24,8},{1,17},{9,25},{17,1},{25,9},{2,18},{10... | collective-permute-start | bytes 196616 | tf_op jit(solution)/shard_map/ppermute | solution.py:343
  56.3 0.9 %shard_map.92 = (f32[256,512]{1,0:T(8,128)S(1)}, f32[256,512]{1,0:T(8,128)S(1)}) custom-call(bf16[256,1024]{1,0:T(8,128)(2,1)S(1)} %get-tuple-element.63.refs_6_.queries, bf16[256,512]{1,0:T(8,128)(2,1)S(1)} %get-tuple-element.57.keys_1.keys.refs_1_, bf16[256,512]{1,0:T(8,128)(2,1)S(1)} %get-tuple-element.59.values_1.values.refs_3_, ...), custom_call_target="tpu_custom_call" | custom-call | tf_op jit(solution)/shard_map/pallas_call | solution.py:71
  57.2 0.9 %shard_map.91 = (f32[256,512]{1,0:T(8,128)S(1)}, f32[256,512]{1,0:T(8,128)S(1)}) custom-call(bf16[256,1024]{1,0:T(8,128)(2,1)S(1)} %get-tuple-element.63.refs_6_.queries, bf16[256,512]{1,0:T(8,128)(2,1)S(1)} %get-tuple-element.56.keys.keys_0.refs_0_, bf16[256,512]{1,0:T(8,128)(2,1)S(1)} %get-tuple-element.58.values.values_0.refs_2_.refs_1_, ...), custom_call_target="tpu_custom_call" | custom-call | tf_op jit(solution)/shard_map/pallas_call | solution.py:71
  58.1 2.9 %collective-permute-done.17.refs_1_ = f32[128,128]{1,0:T(8,128)S(1)} collective-permute-done((f32[128,128]{1,0:T(8,128)S(1)}, f32[128,128]{1,0:T(8,128)S(1)}, u32[]{:S(2)}, u32[]{:S(2)}) %collective-permute-start.17) | collective-permute-done | bytes 65568 | tf_op jit(solution)/shard_map/ppermute | solution.py:343
  61.1 3.0 %collective-permute-start.21 = (f32[128,128]{1,0:T(8,128)S(1)}, f32[128,128]{1,0:T(8,128)S(1)}, u32[]{:S(2)}, u32[]{:S(2)}) collective-permute-start(f32[128,128]{1,0:T(8,128)S(1)} %shard_map.93.refs_8_.refs_1_), channel_id=1, source_target_pairs={{0,48},{8,56},{16,32},{24,40},{32,16},{40,24},{48,0},{56,8},{1,49}... | collective-permute-start | bytes 196616 | tf_op jit(solution)/shard_map/ppermute | solution.py:343
  64.0 3.0 %shard_map.94.refs_0_ = bf16[256,1024]{1,0:T(8,128)(2,1)} custom-call(bf16[256,512]{1,0:T(8,128)(2,1)S(1)} %get-tuple-element.56.keys.keys_0.refs_0_, bf16[256,512]{1,0:T(8,128)(2,1)S(1)} %get-tuple-element.57.keys_1.keys.refs_1_, bf16[256,512]{1,0:T(8,128)(2,1)S(1)} %get-tuple-element.58.values.values_0.refs_2_.refs_1_, ...), custom_call_target="tpu_custom_call" | custom-call | tf_op jit(solution)/shard_map/pallas_call | solution.py:71
  67.1 1.1 %collective-permute-start.24 = (f32[128,128]{1,0:T(8,128)S(1)}, f32[128,128]{1,0:T(8,128)S(1)}, u32[]{:S(2)}, u32[]{:S(2)}) collective-permute-start(f32[128,128]{1,0:T(8,128)S(1)} %shard_map.95), channel_id=1, source_target_pairs={{0,192},{64,128},{128,64},{192,0},{1,193},{65,129},{129,65},{193,1... | collective-permute-start | bytes 196616 | tf_op jit(solution)/shard_map/ppermute | solution.py:343
  68.2 0.8 collective-permute-start.23
  69.0 1.4 %collective-permute-start.22 = (f32[128,128]{1,0:T(8,128)S(1)}, f32[128,128]{1,0:T(8,128)S(1)}, u32[]{:S(2)}, u32[]{:S(2)}) collective-permute-start(f32[128,128]{1,0:T(8,128)S(1)} %shard_map.95), channel_id=1, source_target_pairs={{0,64},{64,0},{128,192},{192,128},{1,65},{65,1},{129,193},{193,129... | collective-permute-start | bytes 196616 | tf_op jit(solution)/shard_map/ppermute | solution.py:343
  70.4 1.1 %collective-permute-done.24.refs_7_ = f32[128,128]{1,0:T(8,128)S(1)} collective-permute-done((f32[128,128]{1,0:T(8,128)S(1)}, f32[128,128]{1,0:T(8,128)S(1)}, u32[]{:S(2)}, u32[]{:S(2)}) %collective-permute-start.24) | collective-permute-done | bytes 65568 | tf_op jit(solution)/shard_map/ppermute | solution.py:343
  71.5 1.3 %collective-permute-done.23.refs_6_ = f32[128,128]{1,0:T(8,128)S(1)} collective-permute-done((f32[128,128]{1,0:T(8,128)S(1)}, f32[128,128]{1,0:T(8,128)S(1)}, u32[]{:S(2)}, u32[]{:S(2)}) %collective-permute-start.23) | collective-permute-done | bytes 65568 | tf_op jit(solution)/shard_map/ppermute | solution.py:343
  72.9 3.0 %collective-permute-start.25 = (f32[128,128]{1,0:T(8,128)S(1)}, f32[128,128]{1,0:T(8,128)S(1)}, u32[]{:S(2)}, u32[]{:S(2)}) collective-permute-start(f32[128,128]{1,0:T(8,128)S(1)} %get-tuple-element.98), channel_id=1, source_target_pairs={{0,8},{8,0},{16,24},{24,16},{1,9},{9,1},{17,25},{25,17},{2,10},{10... | collective-permute-start | bytes 196616 | tf_op jit(solution)/shard_map/ppermute | solution.py:343
  75.9 0.6 collective-permute-start.26
  76.4 1.6 %collective-permute-start.27 = (f32[128,128]{1,0:T(8,128)S(1)}, f32[128,128]{1,0:T(8,128)S(1)}, u32[]{:S(2)}, u32[]{:S(2)}) collective-permute-start(f32[128,128]{1,0:T(8,128)S(1)} %get-tuple-element.100), channel_id=1, source_target_pairs={{0,24},{8,16},{16,8},{24,0},{1,25},{9,17},{17,9},{25,1},{2,26},{10... | collective-permute-start | bytes 196616 | tf_op jit(solution)/shard_map/ppermute | solution.py:343
  78.0 2.5 %collective-permute-done.26.refs_2_ = f32[128,128]{1,0:T(8,128)S(1)} collective-permute-done((f32[128,128]{1,0:T(8,128)S(1)}, f32[128,128]{1,0:T(8,128)S(1)}, u32[]{:S(2)}, u32[]{:S(2)}) %collective-permute-start.26) | collective-permute-done | bytes 65568 | tf_op jit(solution)/shard_map/ppermute | solution.py:343
  80.6 1.1 %collective-permute-done.27.refs_3_ = f32[128,128]{1,0:T(8,128)S(1)} collective-permute-done((f32[128,128]{1,0:T(8,128)S(1)}, f32[128,128]{1,0:T(8,128)S(1)}, u32[]{:S(2)}, u32[]{:S(2)}) %collective-permute-start.27) | collective-permute-done | bytes 65568 | tf_op jit(solution)/shard_map/ppermute | solution.py:343
  81.8 3.4 %collective-permute-start.28 = (f32[4,128,128]{2,1,0:T(8,128)S(1)}, f32[4,128,128]{2,1,0:T(8,128)S(1)}, u32[]{:S(2)}, u32[]{:S(2)}) collective-permute-start(f32[4,128,128]{2,1,0:T(8,128)S(1)} %get-tuple-element.101), channel_id=1, source_target_pairs={{0,4},{4,0},{1,5},{5,1},{2,6},{6,2},{3,7},{7,3},{8,12},{12,8},{9,1... | collective-permute-start | bytes 786440 | tf_op jit(solution)/shard_map/ppermute | solution.py:343
  85.2 0.4 shard_map.98
  85.6 0.7 collective-permute-done.28.state
  86.3 1.6 %shard_map.99 = (bf16[256,1024]{1,0:T(8,128)(2,1)}, bf16[256,1024]{1,0:T(8,128)(2,1)}) custom-call(bf16[256,512]{1,0:T(8,128)(2,1)S(1)} %get-tuple-element.57.keys_1.keys.refs_1_, bf16[256,512]{1,0:T(8,128)(2,1)S(1)} %get-tuple-element.59.values_1.values.refs_3_, f32[256,512]{1,0:T(8,128)S(1)} %get-tuple-element.95.refs_6_.key_inner, ...), custom_call_target="tpu_custom_call" | custom-call | tf_op jit(solution)/shard_map/pallas_call | solution.py:71
  (37 shorter events, 3.2 us)
Async XLA Ops:
  2.1 7.3 %collective-permute-start = (f32[3,128,128]{2,1,0:T(8,128)S(1)}, f32[3,128,128]{2,1,0:T(8,128)S(1)}, u32[]{:S(2)}, u32[]{:S(2)}) collective-permute-start(f32[3,128,128]{2,1,0:T(8,128)S(1)} %get-tuple-element.61), channel_id=1, source_target_pairs={{0,4},{4,0},{1,5},{5,1},{2,6},{6,2},{3,7},{7,3},{8,12},{12,8},{9,1... | collective-permute-start | bytes 589832 | tf_op jit(solution)/shard_map/ppermute | solution.py:343
  5.5 1.3 %collective-permute-start.3 = (f32[1,128,128]{2,1,0:T(8,128)S(1)}, f32[1,128,128]{2,1,0:T(8,128)S(1)}, u32[]{:S(2)}, u32[]{:S(2)}) collective-permute-start(f32[1,128,128]{2,1,0:T(8,128)S(1)} %get-tuple-element.69), channel_id=1, source_target_pairs={{0,4},{4,0},{1,5},{5,1},{2,6},{6,2},{3,7},{7,3},{8,12},{12,8},{9,1... | collective-permute-start | bytes 196616 | tf_op jit(solution)/shard_map/ppermute | solution.py:343
  6.7 6.7 %collective-permute-start.4 = (f32[128,128]{1,0:T(8,128)S(1)}, f32[128,128]{1,0:T(8,128)S(1)}, u32[]{:S(2)}, u32[]{:S(2)}) collective-permute-start(f32[128,128]{1,0:T(8,128)S(1)} %shard_map.80), channel_id=1, source_target_pairs={{0,24},{8,16},{16,8},{24,0},{1,25},{9,17},{17,9},{25,1},{2,26},{10... | collective-permute-start | bytes 196616 | tf_op jit(solution)/shard_map/ppermute | solution.py:343
  9.4 1.0 %copy-start = (bf16[1024]{0:T(1024)(128)(2,1)S(1)}, bf16[1024]{0:T(1024)(128)(2,1)}, u32[]{:S(2)}) copy-start(bf16[1024]{0:T(1024)(128)(2,1)} %param.9) | copy-start | bytes 6148
  9.5 5.1 %collective-permute-start.1 = (f32[128,128]{1,0:T(8,128)S(1)}, f32[128,128]{1,0:T(8,128)S(1)}, u32[]{:S(2)}, u32[]{:S(2)}) collective-permute-start(f32[128,128]{1,0:T(8,128)S(1)} %get-tuple-element.66), channel_id=1, source_target_pairs={{0,8},{8,0},{16,24},{24,16},{1,9},{9,1},{17,25},{25,17},{2,10},{10... | collective-permute-start | bytes 196616 | tf_op jit(solution)/shard_map/ppermute | solution.py:343
  9.6 5.0 %collective-permute-start.2 = (f32[128,128]{1,0:T(8,128)S(1)}, f32[128,128]{1,0:T(8,128)S(1)}, u32[]{:S(2)}, u32[]{:S(2)}) collective-permute-start(f32[128,128]{1,0:T(8,128)S(1)} %get-tuple-element.67), channel_id=1, source_target_pairs={{0,16},{8,24},{16,0},{24,8},{1,17},{9,25},{17,1},{25,9},{2,18},{10... | collective-permute-start | bytes 196616 | tf_op jit(solution)/shard_map/ppermute | solution.py:343
  14.6 5.5 %collective-permute-start.5 = (f32[128,128]{1,0:T(8,128)S(1)}, f32[128,128]{1,0:T(8,128)S(1)}, u32[]{:S(2)}, u32[]{:S(2)}) collective-permute-start(f32[128,128]{1,0:T(8,128)S(1)} %shard_map.81.refs_0_), channel_id=1, source_target_pairs={{0,48},{8,56},{16,32},{24,40},{32,16},{40,24},{48,0},{56,8},{1,49}... | collective-permute-start | bytes 196616 | tf_op jit(solution)/shard_map/ppermute | solution.py:343
  20.2 4.5 %collective-permute-start.8 = (f32[128,128]{1,0:T(8,128)S(1)}, f32[128,128]{1,0:T(8,128)S(1)}, u32[]{:S(2)}, u32[]{:S(2)}) collective-permute-start(f32[128,128]{1,0:T(8,128)S(1)} %shard_map.82), channel_id=1, source_target_pairs={{0,192},{64,128},{128,64},{192,0},{1,193},{65,129},{129,65},{193,1... | collective-permute-start | bytes 196616 | tf_op jit(solution)/shard_map/ppermute | solution.py:343
  23.0 4.7 %collective-permute-start.7 = (f32[128,128]{1,0:T(8,128)S(1)}, f32[128,128]{1,0:T(8,128)S(1)}, u32[]{:S(2)}, u32[]{:S(2)}) collective-permute-start(f32[128,128]{1,0:T(8,128)S(1)} %shard_map.82), channel_id=1, source_target_pairs={{0,128},{64,192},{128,0},{192,64},{1,129},{65,193},{129,1},{193,65... | collective-permute-start | bytes 196616 | tf_op jit(solution)/shard_map/ppermute | solution.py:343
  23.3 4.4 %collective-permute-start.6 = (f32[128,128]{1,0:T(8,128)S(1)}, f32[128,128]{1,0:T(8,128)S(1)}, u32[]{:S(2)}, u32[]{:S(2)}) collective-permute-start(f32[128,128]{1,0:T(8,128)S(1)} %shard_map.82), channel_id=1, source_target_pairs={{0,64},{64,0},{128,192},{192,128},{1,65},{65,1},{129,193},{193,129... | collective-permute-start | bytes 196616 | tf_op jit(solution)/shard_map/ppermute | solution.py:343
  27.8 4.2 %collective-permute-start.9 = (f32[128,128]{1,0:T(8,128)S(1)}, f32[128,128]{1,0:T(8,128)S(1)}, u32[]{:S(2)}, u32[]{:S(2)}) collective-permute-start(f32[128,128]{1,0:T(8,128)S(1)} %get-tuple-element.71), channel_id=1, source_target_pairs={{0,8},{8,0},{16,24},{24,16},{1,9},{9,1},{17,25},{25,17},{2,10},{10... | collective-permute-start | bytes 196616 | tf_op jit(solution)/shard_map/ppermute | solution.py:343
  29.8 4.7 %collective-permute-start.10 = (f32[128,128]{1,0:T(8,128)S(1)}, f32[128,128]{1,0:T(8,128)S(1)}, u32[]{:S(2)}, u32[]{:S(2)}) collective-permute-start(f32[128,128]{1,0:T(8,128)S(1)} %get-tuple-element.72), channel_id=1, source_target_pairs={{0,16},{8,24},{16,0},{24,8},{1,17},{9,25},{17,1},{25,9},{2,18},{10... | collective-permute-start | bytes 196616 | tf_op jit(solution)/shard_map/ppermute | solution.py:343
  30.5 5.1 %collective-permute-start.11 = (f32[128,128]{1,0:T(8,128)S(1)}, f32[128,128]{1,0:T(8,128)S(1)}, u32[]{:S(2)}, u32[]{:S(2)}) collective-permute-start(f32[128,128]{1,0:T(8,128)S(1)} %get-tuple-element.73), channel_id=1, source_target_pairs={{0,24},{8,16},{16,8},{24,0},{1,25},{9,17},{17,9},{25,1},{2,26},{10... | collective-permute-start | bytes 196616 | tf_op jit(solution)/shard_map/ppermute | solution.py:343
  35.6 6.1 %collective-permute-start.12 = (f32[4,128,128]{2,1,0:T(8,128)S(1)}, f32[4,128,128]{2,1,0:T(8,128)S(1)}, u32[]{:S(2)}, u32[]{:S(2)}) collective-permute-start(f32[4,128,128]{2,1,0:T(8,128)S(1)} %get-tuple-element.77), channel_id=1, source_target_pairs={{0,4},{4,0},{1,5},{5,1},{2,6},{6,2},{3,7},{7,3},{8,12},{12,8},{9,1... | collective-permute-start | bytes 786440 | tf_op jit(solution)/shard_map/ppermute | solution.py:343
  42.2 3.7 %collective-permute-start.15 = (f32[2,256]{1,0:T(2,128)S(1)}, f32[2,256]{1,0:T(2,128)S(1)}, u32[]{:S(2)}, u32[]{:S(2)}) collective-permute-start(f32[2,256]{1,0:T(2,128)S(1)} %get-tuple-element.80.refs_3_), channel_id=1, source_target_pairs={{0,3},{1,2},{2,1},{3,0},{4,7},{5,6},{6,5},{7,4},{8,11},{9,10},{10,... | collective-permute-start | bytes 6152 | tf_op jit(solution)/shard_map/ppermute | solution.py:343
  44.7 3.9 %collective-permute-start.14 = (f32[2,256]{1,0:T(2,128)S(1)}, f32[2,256]{1,0:T(2,128)S(1)}, u32[]{:S(2)}, u32[]{:S(2)}) collective-permute-start(f32[2,256]{1,0:T(2,128)S(1)} %get-tuple-element.80.refs_3_), channel_id=1, source_target_pairs={{0,2},{1,3},{2,0},{3,1},{4,6},{5,7},{6,4},{7,5},{8,10},{9,11},{10,... | collective-permute-start | bytes 6152 | tf_op jit(solution)/shard_map/ppermute | solution.py:343
  45.3 3.4 %collective-permute-start.13 = (f32[2,256]{1,0:T(2,128)S(1)}, f32[2,256]{1,0:T(2,128)S(1)}, u32[]{:S(2)}, u32[]{:S(2)}) collective-permute-start(f32[2,256]{1,0:T(2,128)S(1)} %get-tuple-element.80.refs_3_), channel_id=1, source_target_pairs={{0,1},{1,0},{2,3},{3,2},{4,5},{5,4},{6,7},{7,6},{8,9},{9,8},{10,11... | collective-permute-start | bytes 6152 | tf_op jit(solution)/shard_map/ppermute | solution.py:343
  49.2 5.1 %collective-permute-start.16 = (f32[3,128,128]{2,1,0:T(8,128)S(1)}, f32[3,128,128]{2,1,0:T(8,128)S(1)}, u32[]{:S(2)}, u32[]{:S(2)}) collective-permute-start(f32[3,128,128]{2,1,0:T(8,128)S(1)} %get-tuple-element.87), channel_id=1, source_target_pairs={{0,4},{4,0},{1,5},{5,1},{2,6},{6,2},{3,7},{7,3},{8,12},{12,8},{9,1... | collective-permute-start | bytes 589832 | tf_op jit(solution)/shard_map/ppermute | solution.py:343
  51.2 1.3 %collective-permute-start.19 = (f32[1,128,128]{2,1,0:T(8,128)S(1)}, f32[1,128,128]{2,1,0:T(8,128)S(1)}, u32[]{:S(2)}, u32[]{:S(2)}) collective-permute-start(f32[1,128,128]{2,1,0:T(8,128)S(1)} %get-tuple-element.92), channel_id=1, source_target_pairs={{0,4},{4,0},{1,5},{5,1},{2,6},{6,2},{3,7},{7,3},{8,12},{12,8},{9,1... | collective-permute-start | bytes 196616 | tf_op jit(solution)/shard_map/ppermute | solution.py:343
  52.5 5.6 %collective-permute-start.20 = (f32[128,128]{1,0:T(8,128)S(1)}, f32[128,128]{1,0:T(8,128)S(1)}, u32[]{:S(2)}, u32[]{:S(2)}) collective-permute-start(f32[128,128]{1,0:T(8,128)S(1)} %shard_map.90), channel_id=1, source_target_pairs={{0,24},{8,16},{16,8},{24,0},{1,25},{9,17},{17,9},{25,1},{2,26},{10... | collective-permute-start | bytes 196616 | tf_op jit(solution)/shard_map/ppermute | solution.py:343
  54.2 6.8 %collective-permute-start.17 = (f32[128,128]{1,0:T(8,128)S(1)}, f32[128,128]{1,0:T(8,128)S(1)}, u32[]{:S(2)}, u32[]{:S(2)}) collective-permute-start(f32[128,128]{1,0:T(8,128)S(1)} %get-tuple-element.89), channel_id=1, source_target_pairs={{0,8},{8,0},{16,24},{24,16},{1,9},{9,1},{17,25},{25,17},{2,10},{10... | collective-permute-start | bytes 196616 | tf_op jit(solution)/shard_map/ppermute | solution.py:343
  54.4 6.7 %collective-permute-start.18 = (f32[128,128]{1,0:T(8,128)S(1)}, f32[128,128]{1,0:T(8,128)S(1)}, u32[]{:S(2)}, u32[]{:S(2)}) collective-permute-start(f32[128,128]{1,0:T(8,128)S(1)} %get-tuple-element.90), channel_id=1, source_target_pairs={{0,16},{8,24},{16,0},{24,8},{1,17},{9,25},{17,1},{25,9},{2,18},{10... | collective-permute-start | bytes 196616 | tf_op jit(solution)/shard_map/ppermute | solution.py:343
  61.1 6.0 %collective-permute-start.21 = (f32[128,128]{1,0:T(8,128)S(1)}, f32[128,128]{1,0:T(8,128)S(1)}, u32[]{:S(2)}, u32[]{:S(2)}) collective-permute-start(f32[128,128]{1,0:T(8,128)S(1)} %shard_map.93.refs_8_.refs_1_), channel_id=1, source_target_pairs={{0,48},{8,56},{16,32},{24,40},{32,16},{40,24},{48,0},{56,8},{1,49}... | collective-permute-start | bytes 196616 | tf_op jit(solution)/shard_map/ppermute | solution.py:343
  67.1 4.4 %collective-permute-start.24 = (f32[128,128]{1,0:T(8,128)S(1)}, f32[128,128]{1,0:T(8,128)S(1)}, u32[]{:S(2)}, u32[]{:S(2)}) collective-permute-start(f32[128,128]{1,0:T(8,128)S(1)} %shard_map.95), channel_id=1, source_target_pairs={{0,192},{64,128},{128,64},{192,0},{1,193},{65,129},{129,65},{193,1... | collective-permute-start | bytes 196616 | tf_op jit(solution)/shard_map/ppermute | solution.py:343
  68.2 4.6 %collective-permute-start.23 = (f32[128,128]{1,0:T(8,128)S(1)}, f32[128,128]{1,0:T(8,128)S(1)}, u32[]{:S(2)}, u32[]{:S(2)}) collective-permute-start(f32[128,128]{1,0:T(8,128)S(1)} %shard_map.95), channel_id=1, source_target_pairs={{0,128},{64,192},{128,0},{192,64},{1,129},{65,193},{129,1},{193,65... | collective-permute-start | bytes 196616 | tf_op jit(solution)/shard_map/ppermute | solution.py:343
  69.0 3.8 %collective-permute-start.22 = (f32[128,128]{1,0:T(8,128)S(1)}, f32[128,128]{1,0:T(8,128)S(1)}, u32[]{:S(2)}, u32[]{:S(2)}) collective-permute-start(f32[128,128]{1,0:T(8,128)S(1)} %shard_map.95), channel_id=1, source_target_pairs={{0,64},{64,0},{128,192},{192,128},{1,65},{65,1},{129,193},{193,129... | collective-permute-start | bytes 196616 | tf_op jit(solution)/shard_map/ppermute | solution.py:343
  72.9 5.1 %collective-permute-start.25 = (f32[128,128]{1,0:T(8,128)S(1)}, f32[128,128]{1,0:T(8,128)S(1)}, u32[]{:S(2)}, u32[]{:S(2)}) collective-permute-start(f32[128,128]{1,0:T(8,128)S(1)} %get-tuple-element.98), channel_id=1, source_target_pairs={{0,8},{8,0},{16,24},{24,16},{1,9},{9,1},{17,25},{25,17},{2,10},{10... | collective-permute-start | bytes 196616 | tf_op jit(solution)/shard_map/ppermute | solution.py:343
  75.9 4.7 %collective-permute-start.26 = (f32[128,128]{1,0:T(8,128)S(1)}, f32[128,128]{1,0:T(8,128)S(1)}, u32[]{:S(2)}, u32[]{:S(2)}) collective-permute-start(f32[128,128]{1,0:T(8,128)S(1)} %get-tuple-element.99), channel_id=1, source_target_pairs={{0,16},{8,24},{16,0},{24,8},{1,17},{9,25},{17,1},{25,9},{2,18},{10... | collective-permute-start | bytes 196616 | tf_op jit(solution)/shard_map/ppermute | solution.py:343
  76.4 5.3 %collective-permute-start.27 = (f32[128,128]{1,0:T(8,128)S(1)}, f32[128,128]{1,0:T(8,128)S(1)}, u32[]{:S(2)}, u32[]{:S(2)}) collective-permute-start(f32[128,128]{1,0:T(8,128)S(1)} %get-tuple-element.100), channel_id=1, source_target_pairs={{0,24},{8,16},{16,8},{24,0},{1,25},{9,17},{17,9},{25,1},{2,26},{10... | collective-permute-start | bytes 196616 | tf_op jit(solution)/shard_map/ppermute | solution.py:343
  81.8 4.6 %collective-permute-start.28 = (f32[4,128,128]{2,1,0:T(8,128)S(1)}, f32[4,128,128]{2,1,0:T(8,128)S(1)}, u32[]{:S(2)}, u32[]{:S(2)}) collective-permute-start(f32[4,128,128]{2,1,0:T(8,128)S(1)} %get-tuple-element.101), channel_id=1, source_target_pairs={{0,4},{4,0},{1,5},{5,1},{2,6},{6,2},{3,7},{7,3},{8,12},{12,8},{9,1... | collective-permute-start | bytes 786440 | tf_op jit(solution)/shard_map/ppermute | solution.py:343

commit v6 on v5

--- a/solution.py
+++ b/solution.py
@@ -17,7 +17,9 @@
 F32 = jnp.float32
 BF16 = jnp.bfloat16
 VMEM_LIMIT = 16 * 1024 * 1024
+COST = pl.CostEstimate(flops=10**9, bytes_accessed=2**21, transcendentals=0)
 STEPS = ((3,), (2, 1, 0))
+BACK = ((0, 3, 2), (1,))
 
 
 def dot_nn(a, b):
@@ -73,6 +75,7 @@
             out_shape=out_shape,
             in_specs=[pl.BlockSpec(memory_space=space) for space in spaces],
             compiler_params=pltpu.CompilerParams(vmem_limit_bytes=VMEM_LIMIT),
+            cost_estimate=COST,
             **kwargs,
         )(*map(pltpu.with_memory_space_constraint, operands, spaces))
 
@@ -188,44 +191,48 @@
         out[...] = result
 
 
-def merge_kernel(reverse, *refs):
-    *back, mine_0, mine_1, got_0, got_1, own, theirs = refs
+def merge_kernel(reverse, steps, *refs):
+    back, refs = refs[: len(steps)], refs[len(steps) :]
+    mine, got, (own, theirs) = refs[:2], refs[2:4], refs[4:]
     first = before(here("core"), 1 - here("core"), reverse)
-    for mine, got, steps in ((mine_0, got_0, STEPS[0]), (mine_1, got_1, STEPS[1])):
-        for index, step in enumerate(steps):
-            at = owner() ^ step
-            own[at] = back[step][...] + jnp.where(first, 0.0, got[index])
-            theirs[at] = back[step][...] + jnp.where(first, mine[index], 0.0)
-
-
-def forward_kernel(part, queries, upstream, within, state, sooner, *refs):
-    before_sums, (output, low, sums) = refs[:part], refs[part:]
-    heads = state.shape[0]
+    for index, step in enumerate(steps):
+        which = int(step not in STEPS[0])
+        at = STEPS[which].index(step)
+        own[index] = back[index][...] + jnp.where(first, 0.0, got[which][at])
+        theirs[index] = back[index][...] + jnp.where(first, mine[which][at], 0.0)
+
+
+def forward_kernel(part, steps, last, queries, upstream, within, state, sooner, *refs):
+    outputs = 3 if last else 4
+    earlier, (output, low, *sums) = refs[:-outputs], refs[-outputs:]
+    heads = sooner.shape[0]
     tokens = queries.shape[0]
-    square = jnp.zeros((tokens, HEAD_DIM), F32)
-    mixed = jnp.zeros((tokens, HEAD_DIM), F32)
-    for head in range(heads):
-        at = columns(part * heads + head)
+    if earlier:
+        square, mixed = (ref[...] for ref in earlier)
+    else:
+        square = mixed = jnp.zeros((tokens, HEAD_DIM), F32)
+    for index, step in enumerate(steps):
+        at = columns_of(part, step, heads)
         carried = []
         for block, rows in enumerate(blocks(tokens)):
-            wide = state[head]
+            wide = state[index]
             if block:
-                wide = wide + sooner[head, block - 1]
+                wide = wide + sooner[owner() ^ step, block - 1]
             state_low = wide.astype(BF16)
-            low[head, block] = state_low
+            low[index, block] = state_low
             carried.append(dot_nn(queries[rows, at], state_low))
         out = within[:, at] + FACTOR * jnp.concatenate(carried)
-        output[:, columns(head)] = out
+        output[:, columns(index)] = out
         square = square + out * out
         mixed = mixed + upstream[:, at] * out
     for row, array in enumerate((square, mixed)):
-        total = jnp.sum(array.T, axis=0, keepdims=True)
-        for ref in before_sums:
-            total = total + ref[row : row + 1]
-        sums[row : row + 1] = total
-
-
-def delta_kernel(part, queries, upstream, output, *refs):
+        if last:
+            sums[0][row : row + 1] = jnp.sum(array.T, axis=0, keepdims=True)
+        else:
+            sums[row][...] = array
+
+
+def delta_kernel(part, queries, upstream, output_a, output_b, *refs):
     sums, (delta, first, rest, later) = refs[:4], refs[4:]
     tokens = queries.shape[0]
     heads = delta.shape[1] // HEAD_DIM
@@ -236,9 +243,11 @@
     pull = jnp.broadcast_to(pull, (HEAD_DIM, tokens)).T
     for back, steps in zip((first, rest), STEPS):
         for index, step in enumerate(steps):
-            at, near = columns_of(part, step, heads), columns_of(0, step, heads)
-            out_delta = (inv_rms * upstream[:, at] - pull * output[:, near]).astype(BF16)
-            delta[:, near] = out_delta
+            which = int(step not in BACK[0])
+            output = (output_a, output_b)[which][:, columns(BACK[which].index(step))]
+            at = columns_of(part, step, heads)
+            out_delta = (inv_rms * upstream[:, at] - pull * output).astype(BF16)
+            delta[:, columns_of(0, step, heads)] = out_delta
             total = jnp.zeros(back.shape[1:], F32)
             parts = blocks(tokens)
             for block in reversed(range(len(parts))):
@@ -263,17 +272,19 @@
     mask = causal(operands[0].shape[0], False)
     copies = []
     for part, near in enumerate((near_0, near_1)):
-        keys, values, delta, low = operands[part::2]
-        for head in range(low.shape[0]):
-            at = columns(head)
-            out_delta = delta[:, at]
-            carried = [
-                dot_nt(delta[rows, at], low[head, block])
-                for block, rows in enumerate(blocks(keys.shape[0]))
-            ]
-            delta_scores = scores(out_delta, values[:, at], mask)
-            grad = dot_nn(delta_scores, keys[:, at]) + FACTOR * jnp.concatenate(carried)
-            near[:, at] = grad.astype(BF16)
+        keys, values, delta, *lows = operands[part::2]
+        heads = near.shape[1] // HEAD_DIM
+        for low, steps in zip(lows, BACK):
+            for index, step in enumerate(steps):
+                at = columns_of(0, step, heads)
+                out_delta = delta[:, at]
+                carried = [
+                    dot_nt(out_delta[rows], low[index, block])
+                    for block, rows in enumerate(blocks(keys.shape[0]))
+                ]
+                delta_scores = scores(out_delta, values[:, at], mask)
+                grad = dot_nn(delta_scores, keys[:, at]) + FACTOR * jnp.concatenate(carried)
+                near[:, at] = grad.astype(BF16)
         copies.append(write(near, far, part, sems.at[part]))
     for copy in copies:
         copy.wait()
@@ -290,50 +301,48 @@
         value_inner[:, at] = dot_nn(scores(keys[:, at], query, mask), out_delta)
 
 
-def key_value_grads(keys, values, key_inner, value_inner, state, later, key_near, value_near):
+def backward_kernel(
+    steps, keys, values, key_inner, value_inner, state, later, key_near, value_near
+):
     parts = blocks(keys.shape[0])
-    heads = range(state.shape[0])
-    lows = {}
-    for head in heads:
+    heads = later.shape[0]
+    for index, step in enumerate(steps):
+        at = columns_of(0, step, heads)
+        lows = []
         for block in range(len(parts)):
-            wide = state[head]
+            wide = state[index]
             if block + 1 < len(parts):
-                wide = wide + later[head, block]
-            lows[head, block] = wide.astype(BF16)
-    for head in heads:
-        at = columns(head)
-        carried = [dot_nn(values[rows, at], lows[head, n]) for n, rows in enumerate(parts)]
+                wide = wide + later[owner() ^ step, block]
+            lows.append(wide.astype(BF16))
+        carried = [dot_nn(values[rows, at], lows[n]) for n, rows in enumerate(parts)]
         grad = key_inner[:, at] + FACTOR * jnp.concatenate(carried)
-        key_near[:, at] = grad.astype(BF16)
-    yield
-    for head in heads:
-        at = columns(head)
-        carried = [dot_nt(keys[rows, at], lows[head, n]) for n, rows in enumerate(parts)]
+        key_near[:, columns(index)] = grad.astype(BF16)
+        carried = [dot_nt(keys[rows, at], lows[n]) for n, rows in enumerate(parts)]
         grad = value_inner[:, at] + FACTOR * jnp.concatenate(carried)
-        value_near[:, at] = grad.astype(BF16)
-    yield
-
-
-def backward_kernel(*refs):
-    for _ in key_value_grads(*refs):
-        pass
-
-
-def last_kernel(
-    keys, values, key_inner, value_inner, state, later, key_0, value_0,
-    key_far, value_far, key_1, value_1, sems,
-):
-    copies = [
-        write(key_0, key_far, 0, sems.at[0]),
-        write(value_0, value_far, 0, sems.at[1]),
-    ]
-    steps = key_value_grads(
-        keys, values, key_inner, value_inner, state, later, key_1, value_1
-    )
-    next(steps)
-    copies.append(write(key_1, key_far, 1, sems.at[2]))
-    next(steps)
-    copies.append(write(value_1, value_far, 1, sems.at[3]))
+        value_near[:, columns(index)] = grad.astype(BF16)
+
+
+def last_kernel(*refs):
+    operands, ready, refs = refs[:6], refs[6:12], refs[12:]
+    (key_far, value_far), (key_last, value_last, sems) = refs[:2], refs[2:]
+    heads = operands[5].shape[0]
+    copies = []
+
+    def send(part, steps, pair):
+        core = 1 - here("core") if part else here("core")
+        for near, far in zip(pair, (key_far, value_far)):
+            for index, step in enumerate(steps):
+                there = columns_of(core, step, heads)
+                copy = pltpu.make_async_copy(
+                    near.at[:, columns(index)], far.at[:, there], sems.at[len(copies)]
+                )
+                copy.start()
+                copies.append(copy)
+
+    for turn, (part, steps) in enumerate(((0, BACK[0]), (0, BACK[1]), (1, BACK[0]))):
+        send(part, steps, ready[2 * turn : 2 * turn + 2])
+    backward_kernel(BACK[1], *operands, key_last, value_last)
+    send(1, BACK[1], (key_last, value_last))
     for copy in copies:
         copy.wait()
 
@@ -356,7 +365,7 @@
     return [there[step] for step in sorted(there)]
 
 
-def entering(mine, other, reverse, beside_first, beside_second):
+def entering(mine, other, reverse, beside):
     group, rows = lax.axis_size("low"), lax.axis_size("row")
     line, ring = (3, 2, 1), (1, 3, 2)
     piece = near(mine[0].shape[1:])
@@ -364,23 +373,27 @@
     parts = {}
     for steps, *arrays in zip(STEPS, mine, got):
         parts.update(zip(steps, call(split_kernel, [piece] * len(steps))(*arrays)))
-    made = beside_first(parts[0])
+    made = beside(parts[0])
     parts = [parts[0]] + swaps(parts, "low", line)
-    whole = call(functools.partial(join_kernel, 0, group), piece)(*parts, *made)
-    second = beside_second(whole)
+    first, *ties = made
+    whole = call(functools.partial(join_kernel, int(reverse), group), piece, far=int(reverse))(
+        *((first, *parts) if reverse else (*parts, first)), *ties
+    )
     mirror = swap(whole, ("high", "low"), group + group // 2)
-    far = len(second)
-    whole = call(functools.partial(join_kernel, far, 2), piece, far=far)(*second, whole, mirror)
+    whole = call(functools.partial(join_kernel, 0, 2), piece)(whole, mirror)
     there = swaps([whole] * rows, "row", ring)
     back = call(functools.partial(members_kernel, reverse, group, rows), [piece] * group)(
         *parts, mirror, *there
     )
     back = [back[0]] + swaps(back, "low", line)
-    half = near((group * mine[0].shape[0], *mine[0].shape[1:]))
-    own, theirs = call(functools.partial(merge_kernel, reverse), (half, half))(
-        *back, *mine, *got
-    )
-    return (own, swap(theirs, "core", 1)), made, second
+    states = []
+    for steps in BACK:
+        shape = near((len(steps), *mine[0].shape[1:]))
+        own, theirs = call(functools.partial(merge_kernel, reverse, steps), (shape, shape))(
+            *(back[step] for step in steps), *mine, *got
+        )
+        states.append((own, swap(theirs, "core", 1)))
+    return list(zip(*states)), made
 
 
 def on_device(queries, keys, values, out_grad, gain):
@@ -389,14 +402,13 @@
     gain = gain.reshape(1, width)
     wide = near((tokens, width), BF16)
     full = near((tokens, width))
-    half = near((heads // 2, HEAD_DIM, HEAD_DIM))
-    inner_blocks = near((heads // 2, tokens // BLOCK - 1, HEAD_DIM, HEAD_DIM))
-    half_low = near((heads // 2, tokens // BLOCK, HEAD_DIM, HEAD_DIM), BF16)
+    count = heads // 2
+    states = [near((len(steps), HEAD_DIM, HEAD_DIM)) for steps in STEPS]
+    inner_blocks = near((count, tokens // BLOCK - 1, HEAD_DIM, HEAD_DIM))
     half_wide = near((tokens, width // 2), BF16)
     half_full = near((tokens, width // 2))
-    sums_shape = near((2, tokens))
+    lane_full = near((tokens, HEAD_DIM))
     grads = pltpu.HBM((tokens, width), BF16)
-    states = [near((len(steps), HEAD_DIM, HEAD_DIM)) for steps in STEPS]
     *other, sooner_1, keys_0, keys_1, values_0, values_1 = call(
         other_totals_kernel,
         (*states, inner_blocks, *[half_wide] * 4),
@@ -414,54 +426,65 @@
             scratch_shapes=[wide, near((1, width), BF16), pltpu.SemaphoreType.DMA((3, 2))],
         )(queries, out_grad, gain, *keys, *values, after)
 
-    entered, (within, upstream, queries), _ = entering(
-        mine, other, False, beside_forward, lambda after: ()
-    )
+    entered, (within, upstream, queries) = entering(mine, other, False, beside_forward)
     outputs, lows, sums = [], [], []
-    for part, state in enumerate(entered):
-        output, low, *sums = call(
-            functools.partial(forward_kernel, part), (half_full, half_low, sums_shape)
-        )(queries, upstream, within, state, sooner[part], *sums)
-        outputs.append(output)
-        lows.append(low)
+    for part in range(2):
+        for turn, steps in enumerate(BACK):
+            last = bool(part and turn)
+            output, low, *sums = call(
+                functools.partial(forward_kernel, part, steps, last),
+                (
+                    near((tokens, len(steps) * HEAD_DIM)),
+                    near((len(steps), tokens // BLOCK, HEAD_DIM, HEAD_DIM), BF16),
+                    *([near((2, tokens))] if last else [lane_full] * 2),
+                ),
+            )(queries, upstream, within, entered[part][turn], sooner[part], *sums)
+            outputs.append(output)
+            lows.append(low)
     sums = swaps(sums * lax.axis_size("head"), "head", (1, 3, 2)) + sums
     results = [
-        call(functools.partial(delta_kernel, part), (half_wide, *states, inner_blocks))(
-            queries, upstream, outputs[part], *sums
-        )
+        call(
+            functools.partial(delta_kernel, part), (half_wide, *states, inner_blocks)
+        )(queries, upstream, *outputs[2 * part : 2 * part + 2], *sums)
         for part in (1, 0)
     ][::-1]
     deltas = [result[0] for result in results]
     later = [result[3] for result in results]
 
-    def inner_grads(after):
-        made = []
-        for part in range(2):
-            made += call(functools.partial(inner_kernel, part), (half_full, half_full))(
+    def beside_backward(after):
+        query_grad = call(
+            query_kernel,
+            grads,
+            scratch_shapes=[half_wide, half_wide, pltpu.SemaphoreType.DMA((2,))],
+        )(*keys, *values, *deltas, *lows[::2], *lows[1::2], after)
+        inner = [
+            call(functools.partial(inner_kernel, part), (half_full, half_full))(
                 queries, keys[part], values[part], deltas[part], after
             )
-        return made
-
-    def query_grads(after):
-        return (
-            call(
-                query_kernel,
-                grads,
-                scratch_shapes=[half_wide, half_wide, pltpu.SemaphoreType.DMA((2,))],
-            )(*keys, *values, *deltas, *lows, after),
-        )
-
-    entered, inner, (query_grad,) = entering(
-        results[0][1:3], results[1][1:3], True, inner_grads, query_grads
+            for part in range(2)
+        ]
+        return query_grad, *inner[0], *inner[1]
+
+    entered, (query_grad, *inner) = entering(
+        results[0][1:3], results[1][1:3], True, beside_backward
     )
-    key_0, value_0 = call(backward_kernel, (half_wide, half_wide))(
-        keys[0], values[0], *inner[:2], entered[0], later[0]
-    )
+    ready = []
+    for part in range(2):
+        for turn, steps in enumerate(BACK):
+            operands = (
+                keys[part], values[part], *inner[2 * part : 2 * part + 2],
+                entered[part][turn], later[part],
+            )
+            shape = near((tokens, len(steps) * HEAD_DIM), BF16)
+            if not (part and turn):
+                ready += call(functools.partial(backward_kernel, steps), (shape, shape))(
+                    *operands
+                )
     key_grad, value_grad = call(
         last_kernel,
         (grads, grads),
-        scratch_shapes=[half_wide, half_wide, pltpu.SemaphoreType.DMA((4,))],
-    )(keys[1], values[1], *inner[2:], entered[1], later[1], key_0, value_0)
+        scratch_shapes=[shape, shape, pltpu.SemaphoreType.DMA((2 * heads,))],
+    )(*operands, *ready)
     return query_grad, key_grad, value_grad
 
 

time: 88.3 us -> 86.4 us (0.978)
  waiting for transfers between devices: 25.8 us -> 23.3 us
    ppermute x29 -> x31, waiting for transfers between devices: 25.8 us -> 23.3 us  [swap(): lax.ppermute(array, axis, [(at, at ^ distance) for at in range(count)])]
    pallas_call x24 -> x30, Pallas kernels: 13.1 us -> 13.7 us  [run(): pl.pallas_call(kernel, out_shape=out_shape, in_specs=[pl.BlockSpec(memory...]
    ppermute x29 -> x31, starting transfers between devices: 47.7 us -> 47.7 us  [swap(): lax.ppermute(array, axis, [(at, at ^ distance) for at in range(count)])]
  transfers between devices with their start and end apart: 29 -> 31, of which waited for: 17 -> 17; matrix products, arithmetic and copies ran while one was open for 1% -> 1% of each run, Pallas kernels for 10% -> 11%
where the time goes in v6:
time: 86.4 us; the launch traced here: 86.3 us
  starting transfers between devices  47.7 us (55%)
  waiting for transfers between devices  23.3 us (27%)
  Pallas kernels  13.7 us (16%)
  between operations  1.05 us (1%)
    ppermute x31, starting transfers between devices, swap(): lax.ppermute(array, axis, [(at, at ^ distance) for at in range(count)])  47.7 us
    ppermute x31, waiting for transfers between devices, swap(): lax.ppermute(array, axis, [(at, at ^ distance) for at in range(count)])  23.3 us
    pallas_call x30, Pallas kernels, run(): pl.pallas_call(kernel, out_shape=out_shape, in_specs=[pl.BlockSpec(memory...  13.7 us
  transfers between devices with their start and end apart: 31, of which 17 were waited for; matrix products, arithmetic and copies ran while one was open for 1% of the time, Pallas kernels for 11%

profile of v6, /device:TPU:1, one launch (start us, length us, event | category | flops | bytes accessed | tf_op | source)
XLA Modules:
  0.0 86.3 jit_solution(11526655602652469827)
XLA Ops:
  0.6 1.5 %shard_map.76 = (f32[1,128,128]{2,1,0:T(8,128)S(1)}, f32[3,128,128]{2,1,0:T(8,128)S(1)}, f32[4,1,128,128]{3,2,1,0:T(8,128)S(1)}, bf16[256,512]{1,0:T(8,128)(2,1)...) custom-call(bf16[256,1024]{1,0:T(8,128)(2,1)} %keys_far.1, ...), custom_call_target="tpu_custom_call" | custom-call | flops 1000000000 | bytes 2097152 | tf_op jit(solution)/shard_map/pallas_call | solution.py:73
  2.1 3.3 %collective-permute-start = (f32[3,128,128]{2,1,0:T(8,128)S(1)}, f32[3,128,128]{2,1,0:T(8,128)S(1)}, u32[]{:S(2)}, u32[]{:S(2)}) collective-permute-start(f32[3,128,128]{2,1,0:T(8,128)S(1)} %get-tuple-element.78), channel_id=1, source_target_pairs={{0,4},{4,0},{1,5},{5,1},{2,6},{6,2},{3,7},{7,3},{8,12},{12,8},{9,1... | collective-permute-start | bytes 589832 | tf_op jit(solution)/shard_map/ppermute | solution.py:352
  5.6 0.6 reshape.9.gain_far
  6.7 2.7 %collective-permute-start.4 = (f32[128,128]{1,0:T(8,128)S(1)}, f32[128,128]{1,0:T(8,128)S(1)}, u32[]{:S(2)}, u32[]{:S(2)}) collective-permute-start(f32[128,128]{1,0:T(8,128)S(1)} %shard_map.80), channel_id=1, source_target_pairs={{0,24},{8,16},{16,8},{24,0},{1,25},{9,17},{17,9},{25,1},{2,26},{10... | collective-permute-start | bytes 196616 | tf_op jit(solution)/shard_map/ppermute | solution.py:352
  9.6 0.9 %collective-permute-start.2 = (f32[128,128]{1,0:T(8,128)S(1)}, f32[128,128]{1,0:T(8,128)S(1)}, u32[]{:S(2)}, u32[]{:S(2)}) collective-permute-start(f32[128,128]{1,0:T(8,128)S(1)} %get-tuple-element.84), channel_id=1, source_target_pairs={{0,16},{8,24},{16,0},{24,8},{1,17},{9,25},{17,1},{25,9},{2,18},{10... | collective-permute-start | bytes 196616 | tf_op jit(solution)/shard_map/ppermute | solution.py:352
  10.5 2.3 %shard_map.79 = (f32[256,1024]{1,0:T(8,128)S(1)}, f32[256,1024]{1,0:T(8,128)S(1)}, bf16[256,1024]{1,0:T(8,128)(2,1)S(1)}) custom-call(bf16[256,1024]{1,0:T(8,128)(2,1)} %queries_far.1, bf16[256,1024]{1,0:T(8,128)(2,1)} %grad_far.1, bf16[1,1024]{1,0:T(2,128)(2,1)} %reshape.9.gain_far, bf16[256,512]{1,0:T(8,128)(2,1)S(1)} %get-tuple-element.73.keys.keys_0.refs_0_, ...), custom_call_target="tpu_custom_call" | custom-call | flops 1000000000 | bytes 2097152 | tf_op jit(solution)/shard_map/pallas_call | solution.py:73
  12.8 1.8 %collective-permute-done.1.refs_1_ = f32[128,128]{1,0:T(8,128)S(1)} collective-permute-done((f32[128,128]{1,0:T(8,128)S(1)}, f32[128,128]{1,0:T(8,128)S(1)}, u32[]{:S(2)}, u32[]{:S(2)}) %collective-permute-start.1) | collective-permute-done | bytes 65568 | tf_op jit(solution)/shard_map/ppermute | solution.py:352
  14.6 3.9 %collective-permute-start.5 = (f32[128,128]{1,0:T(8,128)S(1)}, f32[128,128]{1,0:T(8,128)S(1)}, u32[]{:S(2)}, u32[]{:S(2)}) collective-permute-start(f32[128,128]{1,0:T(8,128)S(1)} %shard_map.81.refs_0_), channel_id=1, source_target_pairs={{0,48},{8,56},{16,32},{24,40},{32,16},{40,24},{48,0},{56,8},{1,49}... | collective-permute-start | bytes 196616 | tf_op jit(solution)/shard_map/ppermute | solution.py:352
  18.5 1.7 %collective-permute-done.5.refs_1_.refs_4_ = f32[128,128]{1,0:T(8,128)S(1)} collective-permute-done((f32[128,128]{1,0:T(8,128)S(1)}, f32[128,128]{1,0:T(8,128)S(1)}, u32[]{:S(2)}, u32[]{:S(2)}) %collective-permute-start.5) | collective-permute-done | bytes 65568 | tf_op jit(solution)/shard_map/ppermute | solution.py:352
  20.2 2.8 %collective-permute-start.8 = (f32[128,128]{1,0:T(8,128)S(1)}, f32[128,128]{1,0:T(8,128)S(1)}, u32[]{:S(2)}, u32[]{:S(2)}) collective-permute-start(f32[128,128]{1,0:T(8,128)S(1)} %shard_map.82), channel_id=1, source_target_pairs={{0,192},{64,128},{128,64},{192,0},{1,193},{65,129},{129,65},{193,1... | collective-permute-start | bytes 196616 | tf_op jit(solution)/shard_map/ppermute | solution.py:352
  23.0 0.4 collective-permute-start.7
  23.7 1.0 %collective-permute-done.8.refs_7_ = f32[128,128]{1,0:T(8,128)S(1)} collective-permute-done((f32[128,128]{1,0:T(8,128)S(1)}, f32[128,128]{1,0:T(8,128)S(1)}, u32[]{:S(2)}, u32[]{:S(2)}) %collective-permute-start.8) | collective-permute-done | bytes 65568 | tf_op jit(solution)/shard_map/ppermute | solution.py:352
  24.6 3.1 %collective-permute-done.7.refs_6_ = f32[128,128]{1,0:T(8,128)S(1)} collective-permute-done((f32[128,128]{1,0:T(8,128)S(1)}, f32[128,128]{1,0:T(8,128)S(1)}, u32[]{:S(2)}, u32[]{:S(2)}) %collective-permute-start.7) | collective-permute-done | bytes 65568 | tf_op jit(solution)/shard_map/ppermute | solution.py:352
  27.8 1.9 %collective-permute-start.9 = (f32[128,128]{1,0:T(8,128)S(1)}, f32[128,128]{1,0:T(8,128)S(1)}, u32[]{:S(2)}, u32[]{:S(2)}) collective-permute-start(f32[128,128]{1,0:T(8,128)S(1)} %get-tuple-element.88), channel_id=1, source_target_pairs={{0,24},{8,16},{16,8},{24,0},{1,25},{9,17},{17,9},{25,1},{2,26},{10... | collective-permute-start | bytes 196616 | tf_op jit(solution)/shard_map/ppermute | solution.py:352
  29.7 1.2 %collective-permute-start.10 = (f32[128,128]{1,0:T(8,128)S(1)}, f32[128,128]{1,0:T(8,128)S(1)}, u32[]{:S(2)}, u32[]{:S(2)}) collective-permute-start(f32[128,128]{1,0:T(8,128)S(1)} %get-tuple-element.89), channel_id=1, source_target_pairs={{0,16},{8,24},{16,0},{24,8},{1,17},{9,25},{17,1},{25,9},{2,18},{10... | collective-permute-start | bytes 196616 | tf_op jit(solution)/shard_map/ppermute | solution.py:352
  30.9 0.5 collective-permute-start.11
  31.4 1.5 %collective-permute-done.9.refs_1_ = f32[128,128]{1,0:T(8,128)S(1)} collective-permute-done((f32[128,128]{1,0:T(8,128)S(1)}, f32[128,128]{1,0:T(8,128)S(1)}, u32[]{:S(2)}, u32[]{:S(2)}) %collective-permute-start.9) | collective-permute-done | bytes 65568 | tf_op jit(solution)/shard_map/ppermute | solution.py:352
  32.9 1.8 %collective-permute-done.10.refs_2_ = f32[128,128]{1,0:T(8,128)S(1)} collective-permute-done((f32[128,128]{1,0:T(8,128)S(1)}, f32[128,128]{1,0:T(8,128)S(1)}, u32[]{:S(2)}, u32[]{:S(2)}) %collective-permute-start.10) | collective-permute-done | bytes 65568 | tf_op jit(solution)/shard_map/ppermute | solution.py:352
  34.8 4.9 %collective-permute-start.13 = (f32[3,128,128]{2,1,0:T(8,128)S(1)}, f32[3,128,128]{2,1,0:T(8,128)S(1)}, u32[]{:S(2)}, u32[]{:S(2)}) collective-permute-start(f32[3,128,128]{2,1,0:T(8,128)S(1)} %get-tuple-element.100), channel_id=1, source_target_pairs={{0,4},{4,0},{1,5},{5,1},{2,6},{6,2},{3,7},{7,3},{8,12},{12,8},{9,1... | collective-permute-start | bytes 589832 | tf_op jit(solution)/shard_map/ppermute | solution.py:352
  40.3 0.5 collective-permute-done.13.state
  41.4 2.6 %collective-permute-start.16 = (f32[2,256]{1,0:T(2,128)S(1)}, f32[2,256]{1,0:T(2,128)S(1)}, u32[]{:S(2)}, u32[]{:S(2)}) collective-permute-start(f32[2,256]{1,0:T(2,128)S(1)} %get-tuple-element.105.refs_3_), channel_id=1, source_target_pairs={{0,3},{1,2},{2,1},{3,0},{4,7},{5,6},{6,5},{7,4},{8,11},{9,10},{10,... | collective-permute-start | bytes 6152 | tf_op jit(solution)/shard_map/ppermute | solution.py:352
  43.9 0.5 collective-permute-start.15
  44.7 0.4 collective-permute-done.16.refs_2_
  45.1 2.8 %collective-permute-done.15.refs_1_ = f32[2,256]{1,0:T(2,128)S(1)} collective-permute-done((f32[2,256]{1,0:T(2,128)S(1)}, f32[2,256]{1,0:T(2,128)S(1)}, u32[]{:S(2)}, u32[]{:S(2)}) %collective-permute-start.15) | collective-permute-done | bytes 2080 | tf_op jit(solution)/shard_map/ppermute | solution.py:352
  47.9 0.4 shard_map.91
  48.3 1.9 %collective-permute-start.17 = (f32[3,128,128]{2,1,0:T(8,128)S(1)}, f32[3,128,128]{2,1,0:T(8,128)S(1)}, u32[]{:S(2)}, u32[]{:S(2)}) collective-permute-start(f32[3,128,128]{2,1,0:T(8,128)S(1)} %get-tuple-element.115), channel_id=1, source_target_pairs={{0,4},{4,0},{1,5},{5,1},{2,6},{6,2},{3,7},{7,3},{8,12},{12,8},{9,1... | collective-permute-start | bytes 589832 | tf_op jit(solution)/shard_map/ppermute | solution.py:352
  50.3 0.4 shard_map.90
  50.8 0.7 collective-permute-done.20.got.refs_3_.refs_5_
  51.5 1.7 %collective-permute-start.21 = (f32[128,128]{1,0:T(8,128)S(1)}, f32[128,128]{1,0:T(8,128)S(1)}, u32[]{:S(2)}, u32[]{:S(2)}) collective-permute-start(f32[128,128]{1,0:T(8,128)S(1)} %shard_map.95), channel_id=1, source_target_pairs={{0,24},{8,16},{16,8},{24,0},{1,25},{9,17},{17,9},{25,1},{2,26},{10... | collective-permute-start | bytes 196616 | tf_op jit(solution)/shard_map/ppermute | solution.py:352
  53.3 1.9 %collective-permute-start.19 = (f32[128,128]{1,0:T(8,128)S(1)}, f32[128,128]{1,0:T(8,128)S(1)}, u32[]{:S(2)}, u32[]{:S(2)}) collective-permute-start(f32[128,128]{1,0:T(8,128)S(1)} %get-tuple-element.120), channel_id=1, source_target_pairs={{0,16},{8,24},{16,0},{24,8},{1,17},{9,25},{17,1},{25,9},{2,18},{10... | collective-permute-start | bytes 196616 | tf_op jit(solution)/shard_map/ppermute | solution.py:352
  55.2 0.9 %shard_map.94 = (f32[256,512]{1,0:T(8,128)S(1)}, f32[256,512]{1,0:T(8,128)S(1)}) custom-call(bf16[256,1024]{1,0:T(8,128)(2,1)S(1)} %get-tuple-element.80.refs_6_.queries, bf16[256,512]{1,0:T(8,128)(2,1)S(1)} %get-tuple-element.74.keys_1.refs_1_.keys.refs_0_, bf16[256,512]{1,0:T(8,128)(2,1)S(1)} %get-tuple-element.76.values_1.refs_3_.values.refs_1_, ...), custom_call_target="tpu_custom_call" | custom-call | flops 1000000000 | bytes 2097152 | tf_op jit(solution)/shard_map/pallas_call | solution.py:73
  56.2 0.9 %shard_map.96 = (f32[256,512]{1,0:T(8,128)S(1)}, f32[256,512]{1,0:T(8,128)S(1)}) custom-call(bf16[256,1024]{1,0:T(8,128)(2,1)S(1)} %get-tuple-element.80.refs_6_.queries, bf16[256,512]{1,0:T(8,128)(2,1)S(1)} %get-tuple-element.73.keys.keys_0.refs_0_, bf16[256,512]{1,0:T(8,128)(2,1)S(1)} %get-tuple-element.75.values.values_0.refs_2_, ...), custom_call_target="tpu_custom_call" | custom-call | flops 1000000000 | bytes 2097152 | tf_op jit(solution)/shard_map/pallas_call | solution.py:73
  57.1 3.0 %shard_map.93.refs_0_ = bf16[256,1024]{1,0:T(8,128)(2,1)} custom-call(bf16[256,512]{1,0:T(8,128)(2,1)S(1)} %get-tuple-element.73.keys.keys_0.refs_0_, bf16[256,512]{1,0:T(8,128)(2,1)S(1)} %get-tuple-element.74.keys_1.refs_1_.keys.refs_0_, bf16[256,512]{1,0:T(8,128)(2,1)S(1)} %get-tuple-element.75.values.values_0.refs_2_, ...), custom_call_target="tpu_custom_call" | custom-call | flops 1000000000 | bytes 2097152 | tf_op jit(solution)/shard_map/pallas_call | solution.py:73
  60.2 3.6 %collective-permute-start.22 = (f32[128,128]{1,0:T(8,128)S(1)}, f32[128,128]{1,0:T(8,128)S(1)}, u32[]{:S(2)}, u32[]{:S(2)}) collective-permute-start(f32[128,128]{1,0:T(8,128)S(1)} %shard_map.97.refs_0_), channel_id=1, source_target_pairs={{0,48},{8,56},{16,32},{24,40},{32,16},{40,24},{48,0},{56,8},{1,49}... | collective-permute-start | bytes 196616 | tf_op jit(solution)/shard_map/ppermute | solution.py:352
  63.7 1.8 %collective-permute-done.22.refs_1_.refs_4_ = f32[128,128]{1,0:T(8,128)S(1)} collective-permute-done((f32[128,128]{1,0:T(8,128)S(1)}, f32[128,128]{1,0:T(8,128)S(1)}, u32[]{:S(2)}, u32[]{:S(2)}) %collective-permute-start.22) | collective-permute-done | bytes 65568 | tf_op jit(solution)/shard_map/ppermute | solution.py:352
  65.6 1.1 %collective-permute-start.25 = (f32[128,128]{1,0:T(8,128)S(1)}, f32[128,128]{1,0:T(8,128)S(1)}, u32[]{:S(2)}, u32[]{:S(2)}) collective-permute-start(f32[128,128]{1,0:T(8,128)S(1)} %shard_map.98), channel_id=1, source_target_pairs={{0,192},{64,128},{128,64},{192,0},{1,193},{65,129},{129,65},{193,1... | collective-permute-start | bytes 196616 | tf_op jit(solution)/shard_map/ppermute | solution.py:352
  66.7 0.8 collective-permute-start.24
  67.5 1.4 %collective-permute-start.23 = (f32[128,128]{1,0:T(8,128)S(1)}, f32[128,128]{1,0:T(8,128)S(1)}, u32[]{:S(2)}, u32[]{:S(2)}) collective-permute-start(f32[128,128]{1,0:T(8,128)S(1)} %shard_map.98), channel_id=1, source_target_pairs={{0,64},{64,0},{128,192},{192,128},{1,65},{65,1},{129,193},{193,129... | collective-permute-start | bytes 196616 | tf_op jit(solution)/shard_map/ppermute | solution.py:352
  68.9 1.1 %collective-permute-done.25.refs_7_ = f32[128,128]{1,0:T(8,128)S(1)} collective-permute-done((f32[128,128]{1,0:T(8,128)S(1)}, f32[128,128]{1,0:T(8,128)S(1)}, u32[]{:S(2)}, u32[]{:S(2)}) %collective-permute-start.25) | collective-permute-done | bytes 65568 | tf_op jit(solution)/shard_map/ppermute | solution.py:352
  70.0 1.3 %collective-permute-done.24.refs_6_ = f32[128,128]{1,0:T(8,128)S(1)} collective-permute-done((f32[128,128]{1,0:T(8,128)S(1)}, f32[128,128]{1,0:T(8,128)S(1)}, u32[]{:S(2)}, u32[]{:S(2)}) %collective-permute-start.24) | collective-permute-done | bytes 65568 | tf_op jit(solution)/shard_map/ppermute | solution.py:352
  71.4 1.7 %collective-permute-start.28 = (f32[128,128]{1,0:T(8,128)S(1)}, f32[128,128]{1,0:T(8,128)S(1)}, u32[]{:S(2)}, u32[]{:S(2)}) collective-permute-start(f32[128,128]{1,0:T(8,128)S(1)} %get-tuple-element.129), channel_id=1, source_target_pairs={{0,24},{8,16},{16,8},{24,0},{1,25},{9,17},{17,9},{25,1},{2,26},{10... | collective-permute-start | bytes 196616 | tf_op jit(solution)/shard_map/ppermute | solution.py:352
  73.1 1.4 %collective-permute-start.29 = (f32[128,128]{1,0:T(8,128)S(1)}, f32[128,128]{1,0:T(8,128)S(1)}, u32[]{:S(2)}, u32[]{:S(2)}) collective-permute-start(f32[128,128]{1,0:T(8,128)S(1)} %get-tuple-element.130), channel_id=1, source_target_pairs={{0,16},{8,24},{16,0},{24,8},{1,17},{9,25},{17,1},{25,9},{2,18},{10... | collective-permute-start | bytes 196616 | tf_op jit(solution)/shard_map/ppermute | solution.py:352
  74.5 0.5 collective-permute-start.26
  75.0 1.5 %collective-permute-done.28.refs_1_ = f32[128,128]{1,0:T(8,128)S(1)} collective-permute-done((f32[128,128]{1,0:T(8,128)S(1)}, f32[128,128]{1,0:T(8,128)S(1)}, u32[]{:S(2)}, u32[]{:S(2)}) %collective-permute-start.28) | collective-permute-done | bytes 65568 | tf_op jit(solution)/shard_map/ppermute | solution.py:352
  76.5 1.7 %collective-permute-done.29.refs_2_ = f32[128,128]{1,0:T(8,128)S(1)} collective-permute-done((f32[128,128]{1,0:T(8,128)S(1)}, f32[128,128]{1,0:T(8,128)S(1)}, u32[]{:S(2)}, u32[]{:S(2)}) %collective-permute-start.29) | collective-permute-done | bytes 65568 | tf_op jit(solution)/shard_map/ppermute | solution.py:352
  78.3 4.8 %collective-permute-start.30 = (f32[3,128,128]{2,1,0:T(8,128)S(1)}, f32[3,128,128]{2,1,0:T(8,128)S(1)}, u32[]{:S(2)}, u32[]{:S(2)}) collective-permute-start(f32[3,128,128]{2,1,0:T(8,128)S(1)} %get-tuple-element.138), channel_id=1, source_target_pairs={{0,4},{4,0},{1,5},{5,1},{2,6},{6,2},{3,7},{7,3},{8,12},{12,8},{9,1... | collective-permute-start | bytes 589832 | tf_op jit(solution)/shard_map/ppermute | solution.py:352
  83.7 0.4 collective-permute-done.30.state
  84.5 1.6 %shard_map.105 = (bf16[256,1024]{1,0:T(8,128)(2,1)}, bf16[256,1024]{1,0:T(8,128)(2,1)}) custom-call(bf16[256,512]{1,0:T(8,128)(2,1)S(1)} %get-tuple-element.74.keys_1.refs_1_.keys.refs_0_, bf16[256,512]{1,0:T(8,128)(2,1)S(1)} %get-tuple-element.76.values_1.refs_3_.values.refs_1_, f32[256,512]{1,0:T(8,128)S(1)} %get-tuple-element.117.refs_7_.key_inner.refs_2_, ...), custom_call_target="tpu_custom_call" | custom-call | flops 1000000000 | bytes 2097152 | tf_op jit(solution)/shard_map/pallas_call | solution.py:73
  (47 shorter events, 4.1 us)
Async XLA Ops:
  2.1 3.4 %copy-start = (bf16[1024]{0:T(1024)(128)(2,1)S(1)}, bf16[1024]{0:T(1024)(128)(2,1)}, u32[]{:S(2)}) copy-start(bf16[1024]{0:T(1024)(128)(2,1)} %param.9) | copy-start | bytes 6148
  2.1 7.3 %collective-permute-start = (f32[3,128,128]{2,1,0:T(8,128)S(1)}, f32[3,128,128]{2,1,0:T(8,128)S(1)}, u32[]{:S(2)}, u32[]{:S(2)}) collective-permute-start(f32[3,128,128]{2,1,0:T(8,128)S(1)} %get-tuple-element.78), channel_id=1, source_target_pairs={{0,4},{4,0},{1,5},{5,1},{2,6},{6,2},{3,7},{7,3},{8,12},{12,8},{9,1... | collective-permute-start | bytes 589832 | tf_op jit(solution)/shard_map/ppermute | solution.py:352
  5.5 1.3 %collective-permute-start.3 = (f32[1,128,128]{2,1,0:T(8,128)S(1)}, f32[1,128,128]{2,1,0:T(8,128)S(1)}, u32[]{:S(2)}, u32[]{:S(2)}) collective-permute-start(f32[1,128,128]{2,1,0:T(8,128)S(1)} %get-tuple-element.86), channel_id=1, source_target_pairs={{0,4},{4,0},{1,5},{5,1},{2,6},{6,2},{3,7},{7,3},{8,12},{12,8},{9,1... | collective-permute-start | bytes 196616 | tf_op jit(solution)/shard_map/ppermute | solution.py:352
  6.7 6.1 %collective-permute-start.4 = (f32[128,128]{1,0:T(8,128)S(1)}, f32[128,128]{1,0:T(8,128)S(1)}, u32[]{:S(2)}, u32[]{:S(2)}) collective-permute-start(f32[128,128]{1,0:T(8,128)S(1)} %shard_map.80), channel_id=1, source_target_pairs={{0,24},{8,16},{16,8},{24,0},{1,25},{9,17},{17,9},{25,1},{2,26},{10... | collective-permute-start | bytes 196616 | tf_op jit(solution)/shard_map/ppermute | solution.py:352
  9.5 5.1 %collective-permute-start.1 = (f32[128,128]{1,0:T(8,128)S(1)}, f32[128,128]{1,0:T(8,128)S(1)}, u32[]{:S(2)}, u32[]{:S(2)}) collective-permute-start(f32[128,128]{1,0:T(8,128)S(1)} %get-tuple-element.83), channel_id=1, source_target_pairs={{0,8},{8,0},{16,24},{24,16},{1,9},{9,1},{17,25},{25,17},{2,10},{10... | collective-permute-start | bytes 196616 | tf_op jit(solution)/shard_map/ppermute | solution.py:352
  9.6 5.0 %collective-permute-start.2 = (f32[128,128]{1,0:T(8,128)S(1)}, f32[128,128]{1,0:T(8,128)S(1)}, u32[]{:S(2)}, u32[]{:S(2)}) collective-permute-start(f32[128,128]{1,0:T(8,128)S(1)} %get-tuple-element.84), channel_id=1, source_target_pairs={{0,16},{8,24},{16,0},{24,8},{1,17},{9,25},{17,1},{25,9},{2,18},{10... | collective-permute-start | bytes 196616 | tf_op jit(solution)/shard_map/ppermute | solution.py:352
  14.6 5.5 %collective-permute-start.5 = (f32[128,128]{1,0:T(8,128)S(1)}, f32[128,128]{1,0:T(8,128)S(1)}, u32[]{:S(2)}, u32[]{:S(2)}) collective-permute-start(f32[128,128]{1,0:T(8,128)S(1)} %shard_map.81.refs_0_), channel_id=1, source_target_pairs={{0,48},{8,56},{16,32},{24,40},{32,16},{40,24},{48,0},{56,8},{1,49}... | collective-permute-start | bytes 196616 | tf_op jit(solution)/shard_map/ppermute | solution.py:352
  20.2 4.5 %collective-permute-start.8 = (f32[128,128]{1,0:T(8,128)S(1)}, f32[128,128]{1,0:T(8,128)S(1)}, u32[]{:S(2)}, u32[]{:S(2)}) collective-permute-start(f32[128,128]{1,0:T(8,128)S(1)} %shard_map.82), channel_id=1, source_target_pairs={{0,192},{64,128},{128,64},{192,0},{1,193},{65,129},{129,65},{193,1... | collective-permute-start | bytes 196616 | tf_op jit(solution)/shard_map/ppermute | solution.py:352
  23.0 4.7 %collective-permute-start.7 = (f32[128,128]{1,0:T(8,128)S(1)}, f32[128,128]{1,0:T(8,128)S(1)}, u32[]{:S(2)}, u32[]{:S(2)}) collective-permute-start(f32[128,128]{1,0:T(8,128)S(1)} %shard_map.82), channel_id=1, source_target_pairs={{0,128},{64,192},{128,0},{192,64},{1,129},{65,193},{129,1},{193,65... | collective-permute-start | bytes 196616 | tf_op jit(solution)/shard_map/ppermute | solution.py:352
  23.3 4.4 %collective-permute-start.6 = (f32[128,128]{1,0:T(8,128)S(1)}, f32[128,128]{1,0:T(8,128)S(1)}, u32[]{:S(2)}, u32[]{:S(2)}) collective-permute-start(f32[128,128]{1,0:T(8,128)S(1)} %shard_map.82), channel_id=1, source_target_pairs={{0,64},{64,0},{128,192},{192,128},{1,65},{65,1},{129,193},{193,129... | collective-permute-start | bytes 196616 | tf_op jit(solution)/shard_map/ppermute | solution.py:352
  27.8 5.1 %collective-permute-start.9 = (f32[128,128]{1,0:T(8,128)S(1)}, f32[128,128]{1,0:T(8,128)S(1)}, u32[]{:S(2)}, u32[]{:S(2)}) collective-permute-start(f32[128,128]{1,0:T(8,128)S(1)} %get-tuple-element.88), channel_id=1, source_target_pairs={{0,24},{8,16},{16,8},{24,0},{1,25},{9,17},{17,9},{25,1},{2,26},{10... | collective-permute-start | bytes 196616 | tf_op jit(solution)/shard_map/ppermute | solution.py:352
  29.7 5.0 %collective-permute-start.10 = (f32[128,128]{1,0:T(8,128)S(1)}, f32[128,128]{1,0:T(8,128)S(1)}, u32[]{:S(2)}, u32[]{:S(2)}) collective-permute-start(f32[128,128]{1,0:T(8,128)S(1)} %get-tuple-element.89), channel_id=1, source_target_pairs={{0,16},{8,24},{16,0},{24,8},{1,17},{9,25},{17,1},{25,9},{2,18},{10... | collective-permute-start | bytes 196616 | tf_op jit(solution)/shard_map/ppermute | solution.py:352
  30.9 8.8 %collective-permute-start.11 = (f32[128,128]{1,0:T(8,128)S(1)}, f32[128,128]{1,0:T(8,128)S(1)}, u32[]{:S(2)}, u32[]{:S(2)}) collective-permute-start(f32[128,128]{1,0:T(8,128)S(1)} %get-tuple-element.93), channel_id=1, source_target_pairs={{0,8},{8,0},{16,24},{24,16},{1,9},{9,1},{17,25},{25,17},{2,10},{10... | collective-permute-start | bytes 196616 | tf_op jit(solution)/shard_map/ppermute | solution.py:352
  34.8 6.0 %collective-permute-start.13 = (f32[3,128,128]{2,1,0:T(8,128)S(1)}, f32[3,128,128]{2,1,0:T(8,128)S(1)}, u32[]{:S(2)}, u32[]{:S(2)}) collective-permute-start(f32[3,128,128]{2,1,0:T(8,128)S(1)} %get-tuple-element.100), channel_id=1, source_target_pairs={{0,4},{4,0},{1,5},{5,1},{2,6},{6,2},{3,7},{7,3},{8,12},{12,8},{9,1... | collective-permute-start | bytes 589832 | tf_op jit(solution)/shard_map/ppermute | solution.py:352
  39.7 1.3 %collective-permute-start.12 = (f32[1,128,128]{2,1,0:T(8,128)S(1)}, f32[1,128,128]{2,1,0:T(8,128)S(1)}, u32[]{:S(2)}, u32[]{:S(2)}) collective-permute-start(f32[1,128,128]{2,1,0:T(8,128)S(1)} %get-tuple-element.98), channel_id=1, source_target_pairs={{0,4},{4,0},{1,5},{5,1},{2,6},{6,2},{3,7},{7,3},{8,12},{12,8},{9,1... | collective-permute-start | bytes 196616 | tf_op jit(solution)/shard_map/ppermute | solution.py:352
  41.4 3.7 %collective-permute-start.16 = (f32[2,256]{1,0:T(2,128)S(1)}, f32[2,256]{1,0:T(2,128)S(1)}, u32[]{:S(2)}, u32[]{:S(2)}) collective-permute-start(f32[2,256]{1,0:T(2,128)S(1)} %get-tuple-element.105.refs_3_), channel_id=1, source_target_pairs={{0,3},{1,2},{2,1},{3,0},{4,7},{5,6},{6,5},{7,4},{8,11},{9,10},{10,... | collective-permute-start | bytes 6152 | tf_op jit(solution)/shard_map/ppermute | solution.py:352
  43.9 3.9 %collective-permute-start.15 = (f32[2,256]{1,0:T(2,128)S(1)}, f32[2,256]{1,0:T(2,128)S(1)}, u32[]{:S(2)}, u32[]{:S(2)}) collective-permute-start(f32[2,256]{1,0:T(2,128)S(1)} %get-tuple-element.105.refs_3_), channel_id=1, source_target_pairs={{0,2},{1,3},{2,0},{3,1},{4,6},{5,7},{6,4},{7,5},{8,10},{9,11},{10,... | collective-permute-start | bytes 6152 | tf_op jit(solution)/shard_map/ppermute | solution.py:352
  44.5 3.4 %collective-permute-start.14 = (f32[2,256]{1,0:T(2,128)S(1)}, f32[2,256]{1,0:T(2,128)S(1)}, u32[]{:S(2)}, u32[]{:S(2)}) collective-permute-start(f32[2,256]{1,0:T(2,128)S(1)} %get-tuple-element.105.refs_3_), channel_id=1, source_target_pairs={{0,1},{1,0},{2,3},{3,2},{4,5},{5,4},{6,7},{7,6},{8,9},{9,8},{10,11... | collective-permute-start | bytes 6152 | tf_op jit(solution)/shard_map/ppermute | solution.py:352
  48.3 4.9 %collective-permute-start.17 = (f32[3,128,128]{2,1,0:T(8,128)S(1)}, f32[3,128,128]{2,1,0:T(8,128)S(1)}, u32[]{:S(2)}, u32[]{:S(2)}) collective-permute-start(f32[3,128,128]{2,1,0:T(8,128)S(1)} %get-tuple-element.115), channel_id=1, source_target_pairs={{0,4},{4,0},{1,5},{5,1},{2,6},{6,2},{3,7},{7,3},{8,12},{12,8},{9,1... | collective-permute-start | bytes 589832 | tf_op jit(solution)/shard_map/ppermute | solution.py:352
  50.2 1.3 %collective-permute-start.20 = (f32[1,128,128]{2,1,0:T(8,128)S(1)}, f32[1,128,128]{2,1,0:T(8,128)S(1)}, u32[]{:S(2)}, u32[]{:S(2)}) collective-permute-start(f32[1,128,128]{2,1,0:T(8,128)S(1)} %get-tuple-element.122), channel_id=1, source_target_pairs={{0,4},{4,0},{1,5},{5,1},{2,6},{6,2},{3,7},{7,3},{8,12},{12,8},{9,1... | collective-permute-start | bytes 196616 | tf_op jit(solution)/shard_map/ppermute | solution.py:352
  51.5 8.6 %collective-permute-start.21 = (f32[128,128]{1,0:T(8,128)S(1)}, f32[128,128]{1,0:T(8,128)S(1)}, u32[]{:S(2)}, u32[]{:S(2)}) collective-permute-start(f32[128,128]{1,0:T(8,128)S(1)} %shard_map.95), channel_id=1, source_target_pairs={{0,24},{8,16},{16,8},{24,0},{1,25},{9,17},{17,9},{25,1},{2,26},{10... | collective-permute-start | bytes 196616 | tf_op jit(solution)/shard_map/ppermute | solution.py:352
  53.2 6.9 %collective-permute-start.18 = (f32[128,128]{1,0:T(8,128)S(1)}, f32[128,128]{1,0:T(8,128)S(1)}, u32[]{:S(2)}, u32[]{:S(2)}) collective-permute-start(f32[128,128]{1,0:T(8,128)S(1)} %get-tuple-element.119), channel_id=1, source_target_pairs={{0,8},{8,0},{16,24},{24,16},{1,9},{9,1},{17,25},{25,17},{2,10},{10... | collective-permute-start | bytes 196616 | tf_op jit(solution)/shard_map/ppermute | solution.py:352
  53.3 6.8 %collective-permute-start.19 = (f32[128,128]{1,0:T(8,128)S(1)}, f32[128,128]{1,0:T(8,128)S(1)}, u32[]{:S(2)}, u32[]{:S(2)}) collective-permute-start(f32[128,128]{1,0:T(8,128)S(1)} %get-tuple-element.120), channel_id=1, source_target_pairs={{0,16},{8,24},{16,0},{24,8},{1,17},{9,25},{17,1},{25,9},{2,18},{10... | collective-permute-start | bytes 196616 | tf_op jit(solution)/shard_map/ppermute | solution.py:352
  60.2 5.4 %collective-permute-start.22 = (f32[128,128]{1,0:T(8,128)S(1)}, f32[128,128]{1,0:T(8,128)S(1)}, u32[]{:S(2)}, u32[]{:S(2)}) collective-permute-start(f32[128,128]{1,0:T(8,128)S(1)} %shard_map.97.refs_0_), channel_id=1, source_target_pairs={{0,48},{8,56},{16,32},{24,40},{32,16},{40,24},{48,0},{56,8},{1,49}... | collective-permute-start | bytes 196616 | tf_op jit(solution)/shard_map/ppermute | solution.py:352
  65.6 4.4 %collective-permute-start.25 = (f32[128,128]{1,0:T(8,128)S(1)}, f32[128,128]{1,0:T(8,128)S(1)}, u32[]{:S(2)}, u32[]{:S(2)}) collective-permute-start(f32[128,128]{1,0:T(8,128)S(1)} %shard_map.98), channel_id=1, source_target_pairs={{0,192},{64,128},{128,64},{192,0},{1,193},{65,129},{129,65},{193,1... | collective-permute-start | bytes 196616 | tf_op jit(solution)/shard_map/ppermute | solution.py:352
  66.7 4.6 %collective-permute-start.24 = (f32[128,128]{1,0:T(8,128)S(1)}, f32[128,128]{1,0:T(8,128)S(1)}, u32[]{:S(2)}, u32[]{:S(2)}) collective-permute-start(f32[128,128]{1,0:T(8,128)S(1)} %shard_map.98), channel_id=1, source_target_pairs={{0,128},{64,192},{128,0},{192,64},{1,129},{65,193},{129,1},{193,65... | collective-permute-start | bytes 196616 | tf_op jit(solution)/shard_map/ppermute | solution.py:352
  67.5 3.8 %collective-permute-start.23 = (f32[128,128]{1,0:T(8,128)S(1)}, f32[128,128]{1,0:T(8,128)S(1)}, u32[]{:S(2)}, u32[]{:S(2)}) collective-permute-start(f32[128,128]{1,0:T(8,128)S(1)} %shard_map.98), channel_id=1, source_target_pairs={{0,64},{64,0},{128,192},{192,128},{1,65},{65,1},{129,193},{193,129... | collective-permute-start | bytes 196616 | tf_op jit(solution)/shard_map/ppermute | solution.py:352
  71.4 5.1 %collective-permute-start.28 = (f32[128,128]{1,0:T(8,128)S(1)}, f32[128,128]{1,0:T(8,128)S(1)}, u32[]{:S(2)}, u32[]{:S(2)}) collective-permute-start(f32[128,128]{1,0:T(8,128)S(1)} %get-tuple-element.129), channel_id=1, source_target_pairs={{0,24},{8,16},{16,8},{24,0},{1,25},{9,17},{17,9},{25,1},{2,26},{10... | collective-permute-start | bytes 196616 | tf_op jit(solution)/shard_map/ppermute | solution.py:352
  73.1 5.1 %collective-permute-start.29 = (f32[128,128]{1,0:T(8,128)S(1)}, f32[128,128]{1,0:T(8,128)S(1)}, u32[]{:S(2)}, u32[]{:S(2)}) collective-permute-start(f32[128,128]{1,0:T(8,128)S(1)} %get-tuple-element.130), channel_id=1, source_target_pairs={{0,16},{8,24},{16,0},{24,8},{1,17},{9,25},{17,1},{25,9},{2,18},{10... | collective-permute-start | bytes 196616 | tf_op jit(solution)/shard_map/ppermute | solution.py:352
  74.5 8.6 %collective-permute-start.26 = (f32[128,128]{1,0:T(8,128)S(1)}, f32[128,128]{1,0:T(8,128)S(1)}, u32[]{:S(2)}, u32[]{:S(2)}) collective-permute-start(f32[128,128]{1,0:T(8,128)S(1)} %get-tuple-element.125), channel_id=1, source_target_pairs={{0,8},{8,0},{16,24},{24,16},{1,9},{9,1},{17,25},{25,17},{2,10},{10... | collective-permute-start | bytes 196616 | tf_op jit(solution)/shard_map/ppermute | solution.py:352
  78.3 5.8 %collective-permute-start.30 = (f32[3,128,128]{2,1,0:T(8,128)S(1)}, f32[3,128,128]{2,1,0:T(8,128)S(1)}, u32[]{:S(2)}, u32[]{:S(2)}) collective-permute-start(f32[3,128,128]{2,1,0:T(8,128)S(1)} %get-tuple-element.138), channel_id=1, source_target_pairs={{0,4},{4,0},{1,5},{5,1},{2,6},{6,2},{3,7},{7,3},{8,12},{12,8},{9,1... | collective-permute-start | bytes 589832 | tf_op jit(solution)/shard_map/ppermute | solution.py:352
  83.1 1.4 %collective-permute-start.27 = (f32[1,128,128]{2,1,0:T(8,128)S(1)}, f32[1,128,128]{2,1,0:T(8,128)S(1)}, u32[]{:S(2)}, u32[]{:S(2)}) collective-permute-start(f32[1,128,128]{2,1,0:T(8,128)S(1)} %get-tuple-element.126), channel_id=1, source_target_pairs={{0,4},{4,0},{1,5},{5,1},{2,6},{6,2},{3,7},{7,3},{8,12},{12,8},{9,1... | collective-permute-start | bytes 196616 | tf_op jit(solution)/shard_map/ppermute | solution.py:352

commit v7 on v6

--- a/solution.py
+++ b/solution.py
@@ -301,48 +301,60 @@
         value_inner[:, at] = dot_nn(scores(keys[:, at], query, mask), out_delta)
 
 
-def backward_kernel(
-    steps, keys, values, key_inner, value_inner, state, later, key_near, value_near
-):
+def head_grads(step, operands, state, key_near, value_near, near_at):
+    keys, values, key_inner, value_inner, later = operands
     parts = blocks(keys.shape[0])
-    heads = later.shape[0]
+    at = columns_of(0, step, later.shape[0])
+    lows = []
+    for block in range(len(parts)):
+        wide = state
+        if block + 1 < len(parts):
+            wide = wide + later[owner() ^ step, block]
+        lows.append(wide.astype(BF16))
+    carried = [dot_nn(values[rows, at], lows[n]) for n, rows in enumerate(parts)]
+    grad = key_inner[:, at] + FACTOR * jnp.concatenate(carried)
+    key_near[:, near_at] = grad.astype(BF16)
+    carried = [dot_nt(keys[rows, at], lows[n]) for n, rows in enumerate(parts)]
+    grad = value_inner[:, at] + FACTOR * jnp.concatenate(carried)
+    value_near[:, near_at] = grad.astype(BF16)
+
+
+def own_kernel(*refs):
+    operands, states, nears = refs[:5], refs[5:7], refs[7:]
+    for state, steps in zip(states, BACK):
+        for index, step in enumerate(steps):
+            at = columns_of(0, step, operands[4].shape[0])
+            head_grads(step, operands, state[index], *nears, at)
+
+
+def backward_kernel(steps, *refs):
+    operands, state, nears = refs[:5], refs[5], refs[6:]
     for index, step in enumerate(steps):
-        at = columns_of(0, step, heads)
-        lows = []
-        for block in range(len(parts)):
-            wide = state[index]
-            if block + 1 < len(parts):
-                wide = wide + later[owner() ^ step, block]
-            lows.append(wide.astype(BF16))
-        carried = [dot_nn(values[rows, at], lows[n]) for n, rows in enumerate(parts)]
-        grad = key_inner[:, at] + FACTOR * jnp.concatenate(carried)
-        key_near[:, columns(index)] = grad.astype(BF16)
-        carried = [dot_nt(keys[rows, at], lows[n]) for n, rows in enumerate(parts)]
-        grad = value_inner[:, at] + FACTOR * jnp.concatenate(carried)
-        value_near[:, columns(index)] = grad.astype(BF16)
+        head_grads(step, operands, state[index], *nears, columns(index))
 
 
 def last_kernel(*refs):
-    operands, ready, refs = refs[:6], refs[6:12], refs[12:]
+    operands, (key_0, value_0, key_1, value_1), refs = refs[:6], refs[6:10], refs[10:]
     (key_far, value_far), (key_last, value_last, sems) = refs[:2], refs[2:]
-    heads = operands[5].shape[0]
-    copies = []
-
-    def send(part, steps, pair):
-        core = 1 - here("core") if part else here("core")
+    heads = operands[4].shape[0]
+    copies = [
+        write(key_0, key_far, 0, sems.at[0]),
+        write(value_0, value_far, 0, sems.at[1]),
+    ]
+
+    def send(steps, pair):
         for near, far in zip(pair, (key_far, value_far)):
             for index, step in enumerate(steps):
-                there = columns_of(core, step, heads)
+                there = columns_of(1 - here("core"), step, heads)
                 copy = pltpu.make_async_copy(
                     near.at[:, columns(index)], far.at[:, there], sems.at[len(copies)]
                 )
                 copy.start()
                 copies.append(copy)
 
-    for turn, (part, steps) in enumerate(((0, BACK[0]), (0, BACK[1]), (1, BACK[0]))):
-        send(part, steps, ready[2 * turn : 2 * turn + 2])
+    send(BACK[0], (key_1, value_1))
     backward_kernel(BACK[1], *operands, key_last, value_last)
-    send(1, BACK[1], (key_last, value_last))
+    send(BACK[1], (key_last, value_last))
     for copy in copies:
         copy.wait()
 
@@ -468,23 +480,20 @@
     entered, (query_grad, *inner) = entering(
         results[0][1:3], results[1][1:3], True, beside_backward
     )
-    ready = []
-    for part in range(2):
-        for turn, steps in enumerate(BACK):
-            operands = (
-                keys[part], values[part], *inner[2 * part : 2 * part + 2],
-                entered[part][turn], later[part],
-            )
-            shape = near((tokens, len(steps) * HEAD_DIM), BF16)
-            if not (part and turn):
-                ready += call(functools.partial(backward_kernel, steps), (shape, shape))(
-                    *operands
-                )
+    own, theirs = (
+        (keys[part], values[part], *inner[2 * part : 2 * part + 2], later[part])
+        for part in range(2)
+    )
+    ready = list(call(own_kernel, (half_wide, half_wide))(*own, *entered[0]))
+    shapes = [near((tokens, len(steps) * HEAD_DIM), BF16) for steps in BACK]
+    ready += call(functools.partial(backward_kernel, BACK[0]), (shapes[0], shapes[0]))(
+        *theirs, entered[1][0]
+    )
     key_grad, value_grad = call(
         last_kernel,
         (grads, grads),
-        scratch_shapes=[shape, shape, pltpu.SemaphoreType.DMA((2 * heads,))],
-    )(*operands, *ready)
+        scratch_shapes=[shapes[1], shapes[1], pltpu.SemaphoreType.DMA((2 + heads,))],
+    )(*theirs, entered[1][1], *ready)
     return query_grad, key_grad, value_grad
 
 

time: 86.4 us -> 86.3 us (level)
    pallas_call x30 -> x29, Pallas kernels: 13.7 us -> 13.4 us  [run(): pl.pallas_call(kernel, out_shape=out_shape, in_specs=[pl.BlockSpec(memory...]
where the time goes in v7:
time: 86.3 us; the launch traced here: 86.1 us
  starting transfers between devices  47.7 us (55%)
  waiting for transfers between devices  23.4 us (27%)
  Pallas kernels  13.4 us (16%)
  between operations  1.04 us (1%)
    ppermute x31, starting transfers between devices, swap(): lax.ppermute(array, axis, [(at, at ^ distance) for at in range(count)])  47.7 us
    ppermute x31, waiting for transfers between devices, swap(): lax.ppermute(array, axis, [(at, at ^ distance) for at in range(count)])  23.4 us
    pallas_call x29, Pallas kernels, run(): pl.pallas_call(kernel, out_shape=out_shape, in_specs=[pl.BlockSpec(memory...  13.4 us
  transfers between devices with their start and end apart: 31, of which 17 were waited for; matrix products, arithmetic and copies ran while one was open for 1% of the time, Pallas kernels for 11%

profile of v7, /device:TPU:1, one launch (start us, length us, event | category | flops | bytes accessed | tf_op | source)
XLA Modules:
  0.0 86.1 jit_solution(11947324995067096536)
XLA Ops:
  0.6 1.5 %shard_map.76 = (f32[1,128,128]{2,1,0:T(8,128)S(1)}, f32[3,128,128]{2,1,0:T(8,128)S(1)}, f32[4,1,128,128]{3,2,1,0:T(8,128)S(1)}, bf16[256,512]{1,0:T(8,128)(2,1)...) custom-call(bf16[256,1024]{1,0:T(8,128)(2,1)} %keys_far.1, ...), custom_call_target="tpu_custom_call" | custom-call | flops 1000000000 | bytes 2097152 | tf_op jit(solution)/shard_map/pallas_call | solution.py:73
  2.1 3.3 %collective-permute-start = (f32[3,128,128]{2,1,0:T(8,128)S(1)}, f32[3,128,128]{2,1,0:T(8,128)S(1)}, u32[]{:S(2)}, u32[]{:S(2)}) collective-permute-start(f32[3,128,128]{2,1,0:T(8,128)S(1)} %get-tuple-element.76), channel_id=1, source_target_pairs={{0,4},{4,0},{1,5},{5,1},{2,6},{6,2},{3,7},{7,3},{8,12},{12,8},{9,1... | collective-permute-start | bytes 589832 | tf_op jit(solution)/shard_map/ppermute | solution.py:364
  5.6 0.6 reshape.9.gain_far
  6.7 2.7 %collective-permute-start.4 = (f32[128,128]{1,0:T(8,128)S(1)}, f32[128,128]{1,0:T(8,128)S(1)}, u32[]{:S(2)}, u32[]{:S(2)}) collective-permute-start(f32[128,128]{1,0:T(8,128)S(1)} %shard_map.80), channel_id=1, source_target_pairs={{0,24},{8,16},{16,8},{24,0},{1,25},{9,17},{17,9},{25,1},{2,26},{10... | collective-permute-start | bytes 196616 | tf_op jit(solution)/shard_map/ppermute | solution.py:364
  9.6 0.9 %collective-permute-start.2 = (f32[128,128]{1,0:T(8,128)S(1)}, f32[128,128]{1,0:T(8,128)S(1)}, u32[]{:S(2)}, u32[]{:S(2)}) collective-permute-start(f32[128,128]{1,0:T(8,128)S(1)} %get-tuple-element.82), channel_id=1, source_target_pairs={{0,16},{8,24},{16,0},{24,8},{1,17},{9,25},{17,1},{25,9},{2,18},{10... | collective-permute-start | bytes 196616 | tf_op jit(solution)/shard_map/ppermute | solution.py:364
  10.5 2.3 %shard_map.79 = (f32[256,1024]{1,0:T(8,128)S(1)}, f32[256,1024]{1,0:T(8,128)S(1)}, bf16[256,1024]{1,0:T(8,128)(2,1)S(1)}) custom-call(bf16[256,1024]{1,0:T(8,128)(2,1)} %queries_far.1, bf16[256,1024]{1,0:T(8,128)(2,1)} %grad_far.1, bf16[1,1024]{1,0:T(2,128)(2,1)} %reshape.9.gain_far, bf16[256,512]{1,0:T(8,128)(2,1)S(1)} %get-tuple-element.71.keys.keys_0.refs_0_, ...), custom_call_target="tpu_custom_call" | custom-call | flops 1000000000 | bytes 2097152 | tf_op jit(solution)/shard_map/pallas_call | solution.py:73
  12.8 1.8 %collective-permute-done.1.refs_1_ = f32[128,128]{1,0:T(8,128)S(1)} collective-permute-done((f32[128,128]{1,0:T(8,128)S(1)}, f32[128,128]{1,0:T(8,128)S(1)}, u32[]{:S(2)}, u32[]{:S(2)}) %collective-permute-start.1) | collective-permute-done | bytes 65568 | tf_op jit(solution)/shard_map/ppermute | solution.py:364
  14.6 3.9 %collective-permute-start.5 = (f32[128,128]{1,0:T(8,128)S(1)}, f32[128,128]{1,0:T(8,128)S(1)}, u32[]{:S(2)}, u32[]{:S(2)}) collective-permute-start(f32[128,128]{1,0:T(8,128)S(1)} %shard_map.81.refs_0_), channel_id=1, source_target_pairs={{0,48},{8,56},{16,32},{24,40},{32,16},{40,24},{48,0},{56,8},{1,49}... | collective-permute-start | bytes 196616 | tf_op jit(solution)/shard_map/ppermute | solution.py:364
  18.5 1.7 %collective-permute-done.5.refs_1_.refs_4_ = f32[128,128]{1,0:T(8,128)S(1)} collective-permute-done((f32[128,128]{1,0:T(8,128)S(1)}, f32[128,128]{1,0:T(8,128)S(1)}, u32[]{:S(2)}, u32[]{:S(2)}) %collective-permute-start.5) | collective-permute-done | bytes 65568 | tf_op jit(solution)/shard_map/ppermute | solution.py:364
  20.2 2.8 %collective-permute-start.8 = (f32[128,128]{1,0:T(8,128)S(1)}, f32[128,128]{1,0:T(8,128)S(1)}, u32[]{:S(2)}, u32[]{:S(2)}) collective-permute-start(f32[128,128]{1,0:T(8,128)S(1)} %shard_map.82), channel_id=1, source_target_pairs={{0,192},{64,128},{128,64},{192,0},{1,193},{65,129},{129,65},{193,1... | collective-permute-start | bytes 196616 | tf_op jit(solution)/shard_map/ppermute | solution.py:364
  23.7 1.0 %collective-permute-done.8.refs_7_ = f32[128,128]{1,0:T(8,128)S(1)} collective-permute-done((f32[128,128]{1,0:T(8,128)S(1)}, f32[128,128]{1,0:T(8,128)S(1)}, u32[]{:S(2)}, u32[]{:S(2)}) %collective-permute-start.8) | collective-permute-done | bytes 65568 | tf_op jit(solution)/shard_map/ppermute | solution.py:364
  24.6 3.1 %collective-permute-done.7.refs_6_ = f32[128,128]{1,0:T(8,128)S(1)} collective-permute-done((f32[128,128]{1,0:T(8,128)S(1)}, f32[128,128]{1,0:T(8,128)S(1)}, u32[]{:S(2)}, u32[]{:S(2)}) %collective-permute-start.7) | collective-permute-done | bytes 65568 | tf_op jit(solution)/shard_map/ppermute | solution.py:364
  27.8 1.9 %collective-permute-start.9 = (f32[128,128]{1,0:T(8,128)S(1)}, f32[128,128]{1,0:T(8,128)S(1)}, u32[]{:S(2)}, u32[]{:S(2)}) collective-permute-start(f32[128,128]{1,0:T(8,128)S(1)} %get-tuple-element.86), channel_id=1, source_target_pairs={{0,24},{8,16},{16,8},{24,0},{1,25},{9,17},{17,9},{25,1},{2,26},{10... | collective-permute-start | bytes 196616 | tf_op jit(solution)/shard_map/ppermute | solution.py:364
  29.7 1.2 %collective-permute-start.10 = (f32[128,128]{1,0:T(8,128)S(1)}, f32[128,128]{1,0:T(8,128)S(1)}, u32[]{:S(2)}, u32[]{:S(2)}) collective-permute-start(f32[128,128]{1,0:T(8,128)S(1)} %get-tuple-element.87), channel_id=1, source_target_pairs={{0,16},{8,24},{16,0},{24,8},{1,17},{9,25},{17,1},{25,9},{2,18},{10... | collective-permute-start | bytes 196616 | tf_op jit(solution)/shard_map/ppermute | solution.py:364
  30.9 0.5 collective-permute-start.11
  31.4 1.5 %collective-permute-done.9.refs_1_ = f32[128,128]{1,0:T(8,128)S(1)} collective-permute-done((f32[128,128]{1,0:T(8,128)S(1)}, f32[128,128]{1,0:T(8,128)S(1)}, u32[]{:S(2)}, u32[]{:S(2)}) %collective-permute-start.9) | collective-permute-done | bytes 65568 | tf_op jit(solution)/shard_map/ppermute | solution.py:364
  32.9 1.8 %collective-permute-done.10.refs_2_ = f32[128,128]{1,0:T(8,128)S(1)} collective-permute-done((f32[128,128]{1,0:T(8,128)S(1)}, f32[128,128]{1,0:T(8,128)S(1)}, u32[]{:S(2)}, u32[]{:S(2)}) %collective-permute-start.10) | collective-permute-done | bytes 65568 | tf_op jit(solution)/shard_map/ppermute | solution.py:364
  34.8 4.9 %collective-permute-start.13 = (f32[3,128,128]{2,1,0:T(8,128)S(1)}, f32[3,128,128]{2,1,0:T(8,128)S(1)}, u32[]{:S(2)}, u32[]{:S(2)}) collective-permute-start(f32[3,128,128]{2,1,0:T(8,128)S(1)} %get-tuple-element.98), channel_id=1, source_target_pairs={{0,4},{4,0},{1,5},{5,1},{2,6},{6,2},{3,7},{7,3},{8,12},{12,8},{9,1... | collective-permute-start | bytes 589832 | tf_op jit(solution)/shard_map/ppermute | solution.py:364
  40.3 0.5 collective-permute-done.13.state
  41.4 2.6 %collective-permute-start.16 = (f32[2,256]{1,0:T(2,128)S(1)}, f32[2,256]{1,0:T(2,128)S(1)}, u32[]{:S(2)}, u32[]{:S(2)}) collective-permute-start(f32[2,256]{1,0:T(2,128)S(1)} %get-tuple-element.103.refs_3_), channel_id=1, source_target_pairs={{0,3},{1,2},{2,1},{3,0},{4,7},{5,6},{6,5},{7,4},{8,11},{9,10},{10,... | collective-permute-start | bytes 6152 | tf_op jit(solution)/shard_map/ppermute | solution.py:364
  43.9 0.5 collective-permute-start.15
  44.7 0.4 collective-permute-done.16.refs_2_
  45.1 2.8 %collective-permute-done.15.refs_1_ = f32[2,256]{1,0:T(2,128)S(1)} collective-permute-done((f32[2,256]{1,0:T(2,128)S(1)}, f32[2,256]{1,0:T(2,128)S(1)}, u32[]{:S(2)}, u32[]{:S(2)}) %collective-permute-start.15) | collective-permute-done | bytes 2080 | tf_op jit(solution)/shard_map/ppermute | solution.py:364
  47.9 0.4 shard_map.91
  48.3 1.9 %collective-permute-start.17 = (f32[3,128,128]{2,1,0:T(8,128)S(1)}, f32[3,128,128]{2,1,0:T(8,128)S(1)}, u32[]{:S(2)}, u32[]{:S(2)}) collective-permute-start(f32[3,128,128]{2,1,0:T(8,128)S(1)} %get-tuple-element.113), channel_id=1, source_target_pairs={{0,4},{4,0},{1,5},{5,1},{2,6},{6,2},{3,7},{7,3},{8,12},{12,8},{9,1... | collective-permute-start | bytes 589832 | tf_op jit(solution)/shard_map/ppermute | solution.py:364
  50.3 0.4 shard_map.90
  50.8 0.7 collective-permute-done.20.got.refs_3_.refs_5_
  51.5 1.7 %collective-permute-start.21 = (f32[128,128]{1,0:T(8,128)S(1)}, f32[128,128]{1,0:T(8,128)S(1)}, u32[]{:S(2)}, u32[]{:S(2)}) collective-permute-start(f32[128,128]{1,0:T(8,128)S(1)} %shard_map.95), channel_id=1, source_target_pairs={{0,24},{8,16},{16,8},{24,0},{1,25},{9,17},{17,9},{25,1},{2,26},{10... | collective-permute-start | bytes 196616 | tf_op jit(solution)/shard_map/ppermute | solution.py:364
  53.3 1.9 %collective-permute-start.19 = (f32[128,128]{1,0:T(8,128)S(1)}, f32[128,128]{1,0:T(8,128)S(1)}, u32[]{:S(2)}, u32[]{:S(2)}) collective-permute-start(f32[128,128]{1,0:T(8,128)S(1)} %get-tuple-element.119), channel_id=1, source_target_pairs={{0,16},{8,24},{16,0},{24,8},{1,17},{9,25},{17,1},{25,9},{2,18},{10... | collective-permute-start | bytes 196616 | tf_op jit(solution)/shard_map/ppermute | solution.py:364
  55.2 0.9 %shard_map.94 = (f32[256,512]{1,0:T(8,128)S(1)}, f32[256,512]{1,0:T(8,128)S(1)}) custom-call(bf16[256,1024]{1,0:T(8,128)(2,1)S(1)} %get-tuple-element.78.refs_6_.queries, bf16[256,512]{1,0:T(8,128)(2,1)S(1)} %get-tuple-element.72.keys_1.refs_1_.keys.refs_0_, bf16[256,512]{1,0:T(8,128)(2,1)S(1)} %get-tuple-element.74.values_1.refs_3_.values.refs_1_, ...), custom_call_target="tpu_custom_call" | custom-call | flops 1000000000 | bytes 2097152 | tf_op jit(solution)/shard_map/pallas_call | solution.py:73
  56.2 0.9 %shard_map.96 = (f32[256,512]{1,0:T(8,128)S(1)}, f32[256,512]{1,0:T(8,128)S(1)}) custom-call(bf16[256,1024]{1,0:T(8,128)(2,1)S(1)} %get-tuple-element.78.refs_6_.queries, bf16[256,512]{1,0:T(8,128)(2,1)S(1)} %get-tuple-element.71.keys.keys_0.refs_0_, bf16[256,512]{1,0:T(8,128)(2,1)S(1)} %get-tuple-element.73.values.values_0.refs_2_.refs_1_, ...), custom_call_target="tpu_custom_call" | custom-call | flops 1000000000 | bytes 2097152 | tf_op jit(solution)/shard_map/pallas_call | solution.py:73
  57.1 3.0 %shard_map.93.refs_0_ = bf16[256,1024]{1,0:T(8,128)(2,1)} custom-call(bf16[256,512]{1,0:T(8,128)(2,1)S(1)} %get-tuple-element.71.keys.keys_0.refs_0_, bf16[256,512]{1,0:T(8,128)(2,1)S(1)} %get-tuple-element.72.keys_1.refs_1_.keys.refs_0_, bf16[256,512]{1,0:T(8,128)(2,1)S(1)} %get-tuple-element.73.values.values_0.refs_2_.refs_1_, ...), custom_call_target="tpu_custom_call" | custom-call | flops 1000000000 | bytes 2097152 | tf_op jit(solution)/shard_map/pallas_call | solution.py:73
  60.2 3.6 %collective-permute-start.22 = (f32[128,128]{1,0:T(8,128)S(1)}, f32[128,128]{1,0:T(8,128)S(1)}, u32[]{:S(2)}, u32[]{:S(2)}) collective-permute-start(f32[128,128]{1,0:T(8,128)S(1)} %shard_map.97.refs_0_), channel_id=1, source_target_pairs={{0,48},{8,56},{16,32},{24,40},{32,16},{40,24},{48,0},{56,8},{1,49}... | collective-permute-start | bytes 196616 | tf_op jit(solution)/shard_map/ppermute | solution.py:364
  63.7 1.8 %collective-permute-done.22.refs_1_.refs_4_ = f32[128,128]{1,0:T(8,128)S(1)} collective-permute-done((f32[128,128]{1,0:T(8,128)S(1)}, f32[128,128]{1,0:T(8,128)S(1)}, u32[]{:S(2)}, u32[]{:S(2)}) %collective-permute-start.22) | collective-permute-done | bytes 65568 | tf_op jit(solution)/shard_map/ppermute | solution.py:364
  65.6 1.1 %collective-permute-start.25 = (f32[128,128]{1,0:T(8,128)S(1)}, f32[128,128]{1,0:T(8,128)S(1)}, u32[]{:S(2)}, u32[]{:S(2)}) collective-permute-start(f32[128,128]{1,0:T(8,128)S(1)} %shard_map.98), channel_id=1, source_target_pairs={{0,192},{64,128},{128,64},{192,0},{1,193},{65,129},{129,65},{193,1... | collective-permute-start | bytes 196616 | tf_op jit(solution)/shard_map/ppermute | solution.py:364
  66.7 0.8 collective-permute-start.24
  67.5 1.4 %collective-permute-start.23 = (f32[128,128]{1,0:T(8,128)S(1)}, f32[128,128]{1,0:T(8,128)S(1)}, u32[]{:S(2)}, u32[]{:S(2)}) collective-permute-start(f32[128,128]{1,0:T(8,128)S(1)} %shard_map.98), channel_id=1, source_target_pairs={{0,64},{64,0},{128,192},{192,128},{1,65},{65,1},{129,193},{193,129... | collective-permute-start | bytes 196616 | tf_op jit(solution)/shard_map/ppermute | solution.py:364
  68.9 1.1 %collective-permute-done.25.refs_7_ = f32[128,128]{1,0:T(8,128)S(1)} collective-permute-done((f32[128,128]{1,0:T(8,128)S(1)}, f32[128,128]{1,0:T(8,128)S(1)}, u32[]{:S(2)}, u32[]{:S(2)}) %collective-permute-start.25) | collective-permute-done | bytes 65568 | tf_op jit(solution)/shard_map/ppermute | solution.py:364
  70.0 1.3 %collective-permute-done.24.refs_6_ = f32[128,128]{1,0:T(8,128)S(1)} collective-permute-done((f32[128,128]{1,0:T(8,128)S(1)}, f32[128,128]{1,0:T(8,128)S(1)}, u32[]{:S(2)}, u32[]{:S(2)}) %collective-permute-start.24) | collective-permute-done | bytes 65568 | tf_op jit(solution)/shard_map/ppermute | solution.py:364
  71.4 1.7 %collective-permute-start.28 = (f32[128,128]{1,0:T(8,128)S(1)}, f32[128,128]{1,0:T(8,128)S(1)}, u32[]{:S(2)}, u32[]{:S(2)}) collective-permute-start(f32[128,128]{1,0:T(8,128)S(1)} %get-tuple-element.128), channel_id=1, source_target_pairs={{0,24},{8,16},{16,8},{24,0},{1,25},{9,17},{17,9},{25,1},{2,26},{10... | collective-permute-start | bytes 196616 | tf_op jit(solution)/shard_map/ppermute | solution.py:364
  73.1 1.4 %collective-permute-start.29 = (f32[128,128]{1,0:T(8,128)S(1)}, f32[128,128]{1,0:T(8,128)S(1)}, u32[]{:S(2)}, u32[]{:S(2)}) collective-permute-start(f32[128,128]{1,0:T(8,128)S(1)} %get-tuple-element.129), channel_id=1, source_target_pairs={{0,16},{8,24},{16,0},{24,8},{1,17},{9,25},{17,1},{25,9},{2,18},{10... | collective-permute-start | bytes 196616 | tf_op jit(solution)/shard_map/ppermute | solution.py:364
  74.5 0.5 collective-permute-start.26
  75.0 1.5 %collective-permute-done.28.refs_1_ = f32[128,128]{1,0:T(8,128)S(1)} collective-permute-done((f32[128,128]{1,0:T(8,128)S(1)}, f32[128,128]{1,0:T(8,128)S(1)}, u32[]{:S(2)}, u32[]{:S(2)}) %collective-permute-start.28) | collective-permute-done | bytes 65568 | tf_op jit(solution)/shard_map/ppermute | solution.py:364
  76.5 1.7 %collective-permute-done.29.refs_2_ = f32[128,128]{1,0:T(8,128)S(1)} collective-permute-done((f32[128,128]{1,0:T(8,128)S(1)}, f32[128,128]{1,0:T(8,128)S(1)}, u32[]{:S(2)}, u32[]{:S(2)}) %collective-permute-start.29) | collective-permute-done | bytes 65568 | tf_op jit(solution)/shard_map/ppermute | solution.py:364
  78.3 4.8 %collective-permute-start.30 = (f32[3,128,128]{2,1,0:T(8,128)S(1)}, f32[3,128,128]{2,1,0:T(8,128)S(1)}, u32[]{:S(2)}, u32[]{:S(2)}) collective-permute-start(f32[3,128,128]{2,1,0:T(8,128)S(1)} %get-tuple-element.134), channel_id=1, source_target_pairs={{0,4},{4,0},{1,5},{5,1},{2,6},{6,2},{3,7},{7,3},{8,12},{12,8},{9,1... | collective-permute-start | bytes 589832 | tf_op jit(solution)/shard_map/ppermute | solution.py:364
  83.2 0.4 shard_map.102
  83.6 0.5 collective-permute-done.30.refs_5_
  84.5 1.5 %shard_map.104 = (bf16[256,1024]{1,0:T(8,128)(2,1)}, bf16[256,1024]{1,0:T(8,128)(2,1)}) custom-call(bf16[256,512]{1,0:T(8,128)(2,1)S(1)} %get-tuple-element.72.keys_1.refs_1_.keys.refs_0_, bf16[256,512]{1,0:T(8,128)(2,1)S(1)} %get-tuple-element.74.values_1.refs_3_.values.refs_1_, f32[256,512]{1,0:T(8,128)S(1)} %get-tuple-element.115.refs_7_.refs_2_, ...), custom_call_target="tpu_custom_call" | custom-call | flops 1000000000 | bytes 2097152 | tf_op jit(solution)/shard_map/pallas_call | solution.py:73
  (46 shorter events, 3.9 us)
Async XLA Ops:
  2.1 3.4 %copy-start = (bf16[1024]{0:T(1024)(128)(2,1)S(1)}, bf16[1024]{0:T(1024)(128)(2,1)}, u32[]{:S(2)}) copy-start(bf16[1024]{0:T(1024)(128)(2,1)} %param.9) | copy-start | bytes 6148
  2.1 7.3 %collective-permute-start = (f32[3,128,128]{2,1,0:T(8,128)S(1)}, f32[3,128,128]{2,1,0:T(8,128)S(1)}, u32[]{:S(2)}, u32[]{:S(2)}) collective-permute-start(f32[3,128,128]{2,1,0:T(8,128)S(1)} %get-tuple-element.76), channel_id=1, source_target_pairs={{0,4},{4,0},{1,5},{5,1},{2,6},{6,2},{3,7},{7,3},{8,12},{12,8},{9,1... | collective-permute-start | bytes 589832 | tf_op jit(solution)/shard_map/ppermute | solution.py:364
  5.5 1.3 %collective-permute-start.3 = (f32[1,128,128]{2,1,0:T(8,128)S(1)}, f32[1,128,128]{2,1,0:T(8,128)S(1)}, u32[]{:S(2)}, u32[]{:S(2)}) collective-permute-start(f32[1,128,128]{2,1,0:T(8,128)S(1)} %get-tuple-element.84), channel_id=1, source_target_pairs={{0,4},{4,0},{1,5},{5,1},{2,6},{6,2},{3,7},{7,3},{8,12},{12,8},{9,1... | collective-permute-start | bytes 196616 | tf_op jit(solution)/shard_map/ppermute | solution.py:364
  6.7 6.1 %collective-permute-start.4 = (f32[128,128]{1,0:T(8,128)S(1)}, f32[128,128]{1,0:T(8,128)S(1)}, u32[]{:S(2)}, u32[]{:S(2)}) collective-permute-start(f32[128,128]{1,0:T(8,128)S(1)} %shard_map.80), channel_id=1, source_target_pairs={{0,24},{8,16},{16,8},{24,0},{1,25},{9,17},{17,9},{25,1},{2,26},{10... | collective-permute-start | bytes 196616 | tf_op jit(solution)/shard_map/ppermute | solution.py:364
  9.5 5.1 %collective-permute-start.1 = (f32[128,128]{1,0:T(8,128)S(1)}, f32[128,128]{1,0:T(8,128)S(1)}, u32[]{:S(2)}, u32[]{:S(2)}) collective-permute-start(f32[128,128]{1,0:T(8,128)S(1)} %get-tuple-element.81), channel_id=1, source_target_pairs={{0,8},{8,0},{16,24},{24,16},{1,9},{9,1},{17,25},{25,17},{2,10},{10... | collective-permute-start | bytes 196616 | tf_op jit(solution)/shard_map/ppermute | solution.py:364
  9.6 5.0 %collective-permute-start.2 = (f32[128,128]{1,0:T(8,128)S(1)}, f32[128,128]{1,0:T(8,128)S(1)}, u32[]{:S(2)}, u32[]{:S(2)}) collective-permute-start(f32[128,128]{1,0:T(8,128)S(1)} %get-tuple-element.82), channel_id=1, source_target_pairs={{0,16},{8,24},{16,0},{24,8},{1,17},{9,25},{17,1},{25,9},{2,18},{10... | collective-permute-start | bytes 196616 | tf_op jit(solution)/shard_map/ppermute | solution.py:364
  14.6 5.5 %collective-permute-start.5 = (f32[128,128]{1,0:T(8,128)S(1)}, f32[128,128]{1,0:T(8,128)S(1)}, u32[]{:S(2)}, u32[]{:S(2)}) collective-permute-start(f32[128,128]{1,0:T(8,128)S(1)} %shard_map.81.refs_0_), channel_id=1, source_target_pairs={{0,48},{8,56},{16,32},{24,40},{32,16},{40,24},{48,0},{56,8},{1,49}... | collective-permute-start | bytes 196616 | tf_op jit(solution)/shard_map/ppermute | solution.py:364
  20.2 4.5 %collective-permute-start.8 = (f32[128,128]{1,0:T(8,128)S(1)}, f32[128,128]{1,0:T(8,128)S(1)}, u32[]{:S(2)}, u32[]{:S(2)}) collective-permute-start(f32[128,128]{1,0:T(8,128)S(1)} %shard_map.82), channel_id=1, source_target_pairs={{0,192},{64,128},{128,64},{192,0},{1,193},{65,129},{129,65},{193,1... | collective-permute-start | bytes 196616 | tf_op jit(solution)/shard_map/ppermute | solution.py:364
  23.0 4.7 %collective-permute-start.7 = (f32[128,128]{1,0:T(8,128)S(1)}, f32[128,128]{1,0:T(8,128)S(1)}, u32[]{:S(2)}, u32[]{:S(2)}) collective-permute-start(f32[128,128]{1,0:T(8,128)S(1)} %shard_map.82), channel_id=1, source_target_pairs={{0,128},{64,192},{128,0},{192,64},{1,129},{65,193},{129,1},{193,65... | collective-permute-start | bytes 196616 | tf_op jit(solution)/shard_map/ppermute | solution.py:364
  23.3 4.4 %collective-permute-start.6 = (f32[128,128]{1,0:T(8,128)S(1)}, f32[128,128]{1,0:T(8,128)S(1)}, u32[]{:S(2)}, u32[]{:S(2)}) collective-permute-start(f32[128,128]{1,0:T(8,128)S(1)} %shard_map.82), channel_id=1, source_target_pairs={{0,64},{64,0},{128,192},{192,128},{1,65},{65,1},{129,193},{193,129... | collective-permute-start | bytes 196616 | tf_op jit(solution)/shard_map/ppermute | solution.py:364
  27.8 5.1 %collective-permute-start.9 = (f32[128,128]{1,0:T(8,128)S(1)}, f32[128,128]{1,0:T(8,128)S(1)}, u32[]{:S(2)}, u32[]{:S(2)}) collective-permute-start(f32[128,128]{1,0:T(8,128)S(1)} %get-tuple-element.86), channel_id=1, source_target_pairs={{0,24},{8,16},{16,8},{24,0},{1,25},{9,17},{17,9},{25,1},{2,26},{10... | collective-permute-start | bytes 196616 | tf_op jit(solution)/shard_map/ppermute | solution.py:364
  29.7 5.0 %collective-permute-start.10 = (f32[128,128]{1,0:T(8,128)S(1)}, f32[128,128]{1,0:T(8,128)S(1)}, u32[]{:S(2)}, u32[]{:S(2)}) collective-permute-start(f32[128,128]{1,0:T(8,128)S(1)} %get-tuple-element.87), channel_id=1, source_target_pairs={{0,16},{8,24},{16,0},{24,8},{1,17},{9,25},{17,1},{25,9},{2,18},{10... | collective-permute-start | bytes 196616 | tf_op jit(solution)/shard_map/ppermute | solution.py:364
  30.9 8.8 %collective-permute-start.11 = (f32[128,128]{1,0:T(8,128)S(1)}, f32[128,128]{1,0:T(8,128)S(1)}, u32[]{:S(2)}, u32[]{:S(2)}) collective-permute-start(f32[128,128]{1,0:T(8,128)S(1)} %get-tuple-element.91), channel_id=1, source_target_pairs={{0,8},{8,0},{16,24},{24,16},{1,9},{9,1},{17,25},{25,17},{2,10},{10... | collective-permute-start | bytes 196616 | tf_op jit(solution)/shard_map/ppermute | solution.py:364
  34.8 6.0 %collective-permute-start.13 = (f32[3,128,128]{2,1,0:T(8,128)S(1)}, f32[3,128,128]{2,1,0:T(8,128)S(1)}, u32[]{:S(2)}, u32[]{:S(2)}) collective-permute-start(f32[3,128,128]{2,1,0:T(8,128)S(1)} %get-tuple-element.98), channel_id=1, source_target_pairs={{0,4},{4,0},{1,5},{5,1},{2,6},{6,2},{3,7},{7,3},{8,12},{12,8},{9,1... | collective-permute-start | bytes 589832 | tf_op jit(solution)/shard_map/ppermute | solution.py:364
  39.7 1.3 %collective-permute-start.12 = (f32[1,128,128]{2,1,0:T(8,128)S(1)}, f32[1,128,128]{2,1,0:T(8,128)S(1)}, u32[]{:S(2)}, u32[]{:S(2)}) collective-permute-start(f32[1,128,128]{2,1,0:T(8,128)S(1)} %get-tuple-element.96), channel_id=1, source_target_pairs={{0,4},{4,0},{1,5},{5,1},{2,6},{6,2},{3,7},{7,3},{8,12},{12,8},{9,1... | collective-permute-start | bytes 196616 | tf_op jit(solution)/shard_map/ppermute | solution.py:364
  41.4 3.7 %collective-permute-start.16 = (f32[2,256]{1,0:T(2,128)S(1)}, f32[2,256]{1,0:T(2,128)S(1)}, u32[]{:S(2)}, u32[]{:S(2)}) collective-permute-start(f32[2,256]{1,0:T(2,128)S(1)} %get-tuple-element.103.refs_3_), channel_id=1, source_target_pairs={{0,3},{1,2},{2,1},{3,0},{4,7},{5,6},{6,5},{7,4},{8,11},{9,10},{10,... | collective-permute-start | bytes 6152 | tf_op jit(solution)/shard_map/ppermute | solution.py:364
  43.9 3.9 %collective-permute-start.15 = (f32[2,256]{1,0:T(2,128)S(1)}, f32[2,256]{1,0:T(2,128)S(1)}, u32[]{:S(2)}, u32[]{:S(2)}) collective-permute-start(f32[2,256]{1,0:T(2,128)S(1)} %get-tuple-element.103.refs_3_), channel_id=1, source_target_pairs={{0,2},{1,3},{2,0},{3,1},{4,6},{5,7},{6,4},{7,5},{8,10},{9,11},{10,... | collective-permute-start | bytes 6152 | tf_op jit(solution)/shard_map/ppermute | solution.py:364
  44.5 3.4 %collective-permute-start.14 = (f32[2,256]{1,0:T(2,128)S(1)}, f32[2,256]{1,0:T(2,128)S(1)}, u32[]{:S(2)}, u32[]{:S(2)}) collective-permute-start(f32[2,256]{1,0:T(2,128)S(1)} %get-tuple-element.103.refs_3_), channel_id=1, source_target_pairs={{0,1},{1,0},{2,3},{3,2},{4,5},{5,4},{6,7},{7,6},{8,9},{9,8},{10,11... | collective-permute-start | bytes 6152 | tf_op jit(solution)/shard_map/ppermute | solution.py:364
  48.3 4.9 %collective-permute-start.17 = (f32[3,128,128]{2,1,0:T(8,128)S(1)}, f32[3,128,128]{2,1,0:T(8,128)S(1)}, u32[]{:S(2)}, u32[]{:S(2)}) collective-permute-start(f32[3,128,128]{2,1,0:T(8,128)S(1)} %get-tuple-element.113), channel_id=1, source_target_pairs={{0,4},{4,0},{1,5},{5,1},{2,6},{6,2},{3,7},{7,3},{8,12},{12,8},{9,1... | collective-permute-start | bytes 589832 | tf_op jit(solution)/shard_map/ppermute | solution.py:364
  50.2 1.3 %collective-permute-start.20 = (f32[1,128,128]{2,1,0:T(8,128)S(1)}, f32[1,128,128]{2,1,0:T(8,128)S(1)}, u32[]{:S(2)}, u32[]{:S(2)}) collective-permute-start(f32[1,128,128]{2,1,0:T(8,128)S(1)} %get-tuple-element.121), channel_id=1, source_target_pairs={{0,4},{4,0},{1,5},{5,1},{2,6},{6,2},{3,7},{7,3},{8,12},{12,8},{9,1... | collective-permute-start | bytes 196616 | tf_op jit(solution)/shard_map/ppermute | solution.py:364
  51.5 8.6 %collective-permute-start.21 = (f32[128,128]{1,0:T(8,128)S(1)}, f32[128,128]{1,0:T(8,128)S(1)}, u32[]{:S(2)}, u32[]{:S(2)}) collective-permute-start(f32[128,128]{1,0:T(8,128)S(1)} %shard_map.95), channel_id=1, source_target_pairs={{0,24},{8,16},{16,8},{24,0},{1,25},{9,17},{17,9},{25,1},{2,26},{10... | collective-permute-start | bytes 196616 | tf_op jit(solution)/shard_map/ppermute | solution.py:364
  53.2 6.9 %collective-permute-start.18 = (f32[128,128]{1,0:T(8,128)S(1)}, f32[128,128]{1,0:T(8,128)S(1)}, u32[]{:S(2)}, u32[]{:S(2)}) collective-permute-start(f32[128,128]{1,0:T(8,128)S(1)} %get-tuple-element.118), channel_id=1, source_target_pairs={{0,8},{8,0},{16,24},{24,16},{1,9},{9,1},{17,25},{25,17},{2,10},{10... | collective-permute-start | bytes 196616 | tf_op jit(solution)/shard_map/ppermute | solution.py:364
  53.3 6.8 %collective-permute-start.19 = (f32[128,128]{1,0:T(8,128)S(1)}, f32[128,128]{1,0:T(8,128)S(1)}, u32[]{:S(2)}, u32[]{:S(2)}) collective-permute-start(f32[128,128]{1,0:T(8,128)S(1)} %get-tuple-element.119), channel_id=1, source_target_pairs={{0,16},{8,24},{16,0},{24,8},{1,17},{9,25},{17,1},{25,9},{2,18},{10... | collective-permute-start | bytes 196616 | tf_op jit(solution)/shard_map/ppermute | solution.py:364
  60.2 5.4 %collective-permute-start.22 = (f32[128,128]{1,0:T(8,128)S(1)}, f32[128,128]{1,0:T(8,128)S(1)}, u32[]{:S(2)}, u32[]{:S(2)}) collective-permute-start(f32[128,128]{1,0:T(8,128)S(1)} %shard_map.97.refs_0_), channel_id=1, source_target_pairs={{0,48},{8,56},{16,32},{24,40},{32,16},{40,24},{48,0},{56,8},{1,49}... | collective-permute-start | bytes 196616 | tf_op jit(solution)/shard_map/ppermute | solution.py:364
  65.6 4.4 %collective-permute-start.25 = (f32[128,128]{1,0:T(8,128)S(1)}, f32[128,128]{1,0:T(8,128)S(1)}, u32[]{:S(2)}, u32[]{:S(2)}) collective-permute-start(f32[128,128]{1,0:T(8,128)S(1)} %shard_map.98), channel_id=1, source_target_pairs={{0,192},{64,128},{128,64},{192,0},{1,193},{65,129},{129,65},{193,1... | collective-permute-start | bytes 196616 | tf_op jit(solution)/shard_map/ppermute | solution.py:364
  66.7 4.6 %collective-permute-start.24 = (f32[128,128]{1,0:T(8,128)S(1)}, f32[128,128]{1,0:T(8,128)S(1)}, u32[]{:S(2)}, u32[]{:S(2)}) collective-permute-start(f32[128,128]{1,0:T(8,128)S(1)} %shard_map.98), channel_id=1, source_target_pairs={{0,128},{64,192},{128,0},{192,64},{1,129},{65,193},{129,1},{193,65... | collective-permute-start | bytes 196616 | tf_op jit(solution)/shard_map/ppermute | solution.py:364
  67.5 3.8 %collective-permute-start.23 = (f32[128,128]{1,0:T(8,128)S(1)}, f32[128,128]{1,0:T(8,128)S(1)}, u32[]{:S(2)}, u32[]{:S(2)}) collective-permute-start(f32[128,128]{1,0:T(8,128)S(1)} %shard_map.98), channel_id=1, source_target_pairs={{0,64},{64,0},{128,192},{192,128},{1,65},{65,1},{129,193},{193,129... | collective-permute-start | bytes 196616 | tf_op jit(solution)/shard_map/ppermute | solution.py:364
  71.4 5.1 %collective-permute-start.28 = (f32[128,128]{1,0:T(8,128)S(1)}, f32[128,128]{1,0:T(8,128)S(1)}, u32[]{:S(2)}, u32[]{:S(2)}) collective-permute-start(f32[128,128]{1,0:T(8,128)S(1)} %get-tuple-element.128), channel_id=1, source_target_pairs={{0,24},{8,16},{16,8},{24,0},{1,25},{9,17},{17,9},{25,1},{2,26},{10... | collective-permute-start | bytes 196616 | tf_op jit(solution)/shard_map/ppermute | solution.py:364
  73.1 5.1 %collective-permute-start.29 = (f32[128,128]{1,0:T(8,128)S(1)}, f32[128,128]{1,0:T(8,128)S(1)}, u32[]{:S(2)}, u32[]{:S(2)}) collective-permute-start(f32[128,128]{1,0:T(8,128)S(1)} %get-tuple-element.129), channel_id=1, source_target_pairs={{0,16},{8,24},{16,0},{24,8},{1,17},{9,25},{17,1},{25,9},{2,18},{10... | collective-permute-start | bytes 196616 | tf_op jit(solution)/shard_map/ppermute | solution.py:364
  74.5 8.6 %collective-permute-start.26 = (f32[128,128]{1,0:T(8,128)S(1)}, f32[128,128]{1,0:T(8,128)S(1)}, u32[]{:S(2)}, u32[]{:S(2)}) collective-permute-start(f32[128,128]{1,0:T(8,128)S(1)} %get-tuple-element.124), channel_id=1, source_target_pairs={{0,8},{8,0},{16,24},{24,16},{1,9},{9,1},{17,25},{25,17},{2,10},{10... | collective-permute-start | bytes 196616 | tf_op jit(solution)/shard_map/ppermute | solution.py:364
  78.3 5.8 %collective-permute-start.30 = (f32[3,128,128]{2,1,0:T(8,128)S(1)}, f32[3,128,128]{2,1,0:T(8,128)S(1)}, u32[]{:S(2)}, u32[]{:S(2)}) collective-permute-start(f32[3,128,128]{2,1,0:T(8,128)S(1)} %get-tuple-element.134), channel_id=1, source_target_pairs={{0,4},{4,0},{1,5},{5,1},{2,6},{6,2},{3,7},{7,3},{8,12},{12,8},{9,1... | collective-permute-start | bytes 589832 | tf_op jit(solution)/shard_map/ppermute | solution.py:364
  83.1 1.4 %collective-permute-start.27 = (f32[1,128,128]{2,1,0:T(8,128)S(1)}, f32[1,128,128]{2,1,0:T(8,128)S(1)}, u32[]{:S(2)}, u32[]{:S(2)}) collective-permute-start(f32[1,128,128]{2,1,0:T(8,128)S(1)} %get-tuple-element.125), channel_id=1, source_target_pairs={{0,4},{4,0},{1,5},{5,1},{2,6},{6,2},{3,7},{7,3},{8,12},{12,8},{9,1... | collective-permute-start | bytes 196616 | tf_op jit(solution)/shard_map/ppermute | solution.py:364

commit v8 on v7

--- a/solution.py
+++ b/solution.py
@@ -425,7 +425,7 @@
         other_totals_kernel,
         (*states, inner_blocks, *[half_wide] * 4),
         far=2,
-        scratch_shapes=[pltpu.SemaphoreType.DMA((2, 2, 4))],
+        scratch_shapes=[pltpu.SemaphoreType.DMA((2, 2, 1))],
     )(keys, values)
     *mine, sooner_0 = call(key_value_states, (*states, inner_blocks))(keys_0, values_0)
     sooner, keys, values = (sooner_0, sooner_1), (keys_0, keys_1), (values_0, values_1)

time: 86.3 us -> 86.1 us (level)
  no operation moved by 1% of the time
where the time goes in v8:
time: 86.1 us; the launch traced here: 85.9 us
  starting transfers between devices  47.7 us (55%)
  waiting for transfers between devices  23.4 us (27%)
  Pallas kernels  13.2 us (15%)
  between operations  1.04 us (1%)
    ppermute x31, starting transfers between devices, swap(): lax.ppermute(array, axis, [(at, at ^ distance) for at in range(count)])  47.7 us
    ppermute x31, waiting for transfers between devices, swap(): lax.ppermute(array, axis, [(at, at ^ distance) for at in range(count)])  23.4 us
    pallas_call x29, Pallas kernels, run(): pl.pallas_call(kernel, out_shape=out_shape, in_specs=[pl.BlockSpec(memory...  13.2 us
  transfers between devices with their start and end apart: 31, of which 17 were waited for; matrix products, arithmetic and copies ran while one was open for 1% of the time, Pallas kernels for 11%

profile of v8, /device:TPU:1, one launch (start us, length us, event | category | flops | bytes accessed | tf_op | source)
XLA Modules:
  0.0 85.9 jit_solution(8962457631173935791)
XLA Ops:
  0.6 1.3 %shard_map.76 = (f32[1,128,128]{2,1,0:T(8,128)S(1)}, f32[3,128,128]{2,1,0:T(8,128)S(1)}, f32[4,1,128,128]{3,2,1,0:T(8,128)S(1)}, bf16[256,512]{1,0:T(8,128)(2,1)...) custom-call(bf16[256,1024]{1,0:T(8,128)(2,1)} %keys_far.1, ...), custom_call_target="tpu_custom_call" | custom-call | flops 1000000000 | bytes 2097152 | tf_op jit(solution)/shard_map/pallas_call | solution.py:73
  2.0 3.3 %collective-permute-start = (f32[3,128,128]{2,1,0:T(8,128)S(1)}, f32[3,128,128]{2,1,0:T(8,128)S(1)}, u32[]{:S(2)}, u32[]{:S(2)}) collective-permute-start(f32[3,128,128]{2,1,0:T(8,128)S(1)} %get-tuple-element.76), channel_id=1, source_target_pairs={{0,4},{4,0},{1,5},{5,1},{2,6},{6,2},{3,7},{7,3},{8,12},{12,8},{9,1... | collective-permute-start | bytes 589832 | tf_op jit(solution)/shard_map/ppermute | solution.py:364
  5.4 0.6 reshape.9.gain_far
  6.6 2.7 %collective-permute-start.4 = (f32[128,128]{1,0:T(8,128)S(1)}, f32[128,128]{1,0:T(8,128)S(1)}, u32[]{:S(2)}, u32[]{:S(2)}) collective-permute-start(f32[128,128]{1,0:T(8,128)S(1)} %shard_map.80), channel_id=1, source_target_pairs={{0,24},{8,16},{16,8},{24,0},{1,25},{9,17},{17,9},{25,1},{2,26},{10... | collective-permute-start | bytes 196616 | tf_op jit(solution)/shard_map/ppermute | solution.py:364
  9.4 0.9 %collective-permute-start.2 = (f32[128,128]{1,0:T(8,128)S(1)}, f32[128,128]{1,0:T(8,128)S(1)}, u32[]{:S(2)}, u32[]{:S(2)}) collective-permute-start(f32[128,128]{1,0:T(8,128)S(1)} %get-tuple-element.82), channel_id=1, source_target_pairs={{0,16},{8,24},{16,0},{24,8},{1,17},{9,25},{17,1},{25,9},{2,18},{10... | collective-permute-start | bytes 196616 | tf_op jit(solution)/shard_map/ppermute | solution.py:364
  10.3 2.3 %shard_map.79 = (f32[256,1024]{1,0:T(8,128)S(1)}, f32[256,1024]{1,0:T(8,128)S(1)}, bf16[256,1024]{1,0:T(8,128)(2,1)S(1)}) custom-call(bf16[256,1024]{1,0:T(8,128)(2,1)} %queries_far.1, bf16[256,1024]{1,0:T(8,128)(2,1)} %grad_far.1, bf16[1,1024]{1,0:T(2,128)(2,1)} %reshape.9.gain_far, bf16[256,512]{1,0:T(8,128)(2,1)S(1)} %get-tuple-element.71.keys.keys_0.refs_0_, ...), custom_call_target="tpu_custom_call" | custom-call | flops 1000000000 | bytes 2097152 | tf_op jit(solution)/shard_map/pallas_call | solution.py:73
  12.7 1.8 %collective-permute-done.1.refs_1_ = f32[128,128]{1,0:T(8,128)S(1)} collective-permute-done((f32[128,128]{1,0:T(8,128)S(1)}, f32[128,128]{1,0:T(8,128)S(1)}, u32[]{:S(2)}, u32[]{:S(2)}) %collective-permute-start.1) | collective-permute-done | bytes 65568 | tf_op jit(solution)/shard_map/ppermute | solution.py:364
  14.5 3.9 %collective-permute-start.5 = (f32[128,128]{1,0:T(8,128)S(1)}, f32[128,128]{1,0:T(8,128)S(1)}, u32[]{:S(2)}, u32[]{:S(2)}) collective-permute-start(f32[128,128]{1,0:T(8,128)S(1)} %shard_map.81.refs_0_), channel_id=1, source_target_pairs={{0,48},{8,56},{16,32},{24,40},{32,16},{40,24},{48,0},{56,8},{1,49}... | collective-permute-start | bytes 196616 | tf_op jit(solution)/shard_map/ppermute | solution.py:364
  18.3 1.7 %collective-permute-done.5.refs_1_.refs_4_ = f32[128,128]{1,0:T(8,128)S(1)} collective-permute-done((f32[128,128]{1,0:T(8,128)S(1)}, f32[128,128]{1,0:T(8,128)S(1)}, u32[]{:S(2)}, u32[]{:S(2)}) %collective-permute-start.5) | collective-permute-done | bytes 65568 | tf_op jit(solution)/shard_map/ppermute | solution.py:364
  20.0 2.8 %collective-permute-start.8 = (f32[128,128]{1,0:T(8,128)S(1)}, f32[128,128]{1,0:T(8,128)S(1)}, u32[]{:S(2)}, u32[]{:S(2)}) collective-permute-start(f32[128,128]{1,0:T(8,128)S(1)} %shard_map.82), channel_id=1, source_target_pairs={{0,192},{64,128},{128,64},{192,0},{1,193},{65,129},{129,65},{193,1... | collective-permute-start | bytes 196616 | tf_op jit(solution)/shard_map/ppermute | solution.py:364
  23.5 1.0 %collective-permute-done.8.refs_7_ = f32[128,128]{1,0:T(8,128)S(1)} collective-permute-done((f32[128,128]{1,0:T(8,128)S(1)}, f32[128,128]{1,0:T(8,128)S(1)}, u32[]{:S(2)}, u32[]{:S(2)}) %collective-permute-start.8) | collective-permute-done | bytes 65568 | tf_op jit(solution)/shard_map/ppermute | solution.py:364
  24.5 3.1 %collective-permute-done.7.refs_6_ = f32[128,128]{1,0:T(8,128)S(1)} collective-permute-done((f32[128,128]{1,0:T(8,128)S(1)}, f32[128,128]{1,0:T(8,128)S(1)}, u32[]{:S(2)}, u32[]{:S(2)}) %collective-permute-start.7) | collective-permute-done | bytes 65568 | tf_op jit(solution)/shard_map/ppermute | solution.py:364
  27.6 1.9 %collective-permute-start.9 = (f32[128,128]{1,0:T(8,128)S(1)}, f32[128,128]{1,0:T(8,128)S(1)}, u32[]{:S(2)}, u32[]{:S(2)}) collective-permute-start(f32[128,128]{1,0:T(8,128)S(1)} %get-tuple-element.86), channel_id=1, source_target_pairs={{0,24},{8,16},{16,8},{24,0},{1,25},{9,17},{17,9},{25,1},{2,26},{10... | collective-permute-start | bytes 196616 | tf_op jit(solution)/shard_map/ppermute | solution.py:364
  29.6 1.2 %collective-permute-start.10 = (f32[128,128]{1,0:T(8,128)S(1)}, f32[128,128]{1,0:T(8,128)S(1)}, u32[]{:S(2)}, u32[]{:S(2)}) collective-permute-start(f32[128,128]{1,0:T(8,128)S(1)} %get-tuple-element.87), channel_id=1, source_target_pairs={{0,16},{8,24},{16,0},{24,8},{1,17},{9,25},{17,1},{25,9},{2,18},{10... | collective-permute-start | bytes 196616 | tf_op jit(solution)/shard_map/ppermute | solution.py:364
  30.8 0.5 collective-permute-start.11
  31.3 1.5 %collective-permute-done.9.refs_1_ = f32[128,128]{1,0:T(8,128)S(1)} collective-permute-done((f32[128,128]{1,0:T(8,128)S(1)}, f32[128,128]{1,0:T(8,128)S(1)}, u32[]{:S(2)}, u32[]{:S(2)}) %collective-permute-start.9) | collective-permute-done | bytes 65568 | tf_op jit(solution)/shard_map/ppermute | solution.py:364
  32.8 1.8 %collective-permute-done.10.refs_2_ = f32[128,128]{1,0:T(8,128)S(1)} collective-permute-done((f32[128,128]{1,0:T(8,128)S(1)}, f32[128,128]{1,0:T(8,128)S(1)}, u32[]{:S(2)}, u32[]{:S(2)}) %collective-permute-start.10) | collective-permute-done | bytes 65568 | tf_op jit(solution)/shard_map/ppermute | solution.py:364
  34.6 4.9 %collective-permute-start.13 = (f32[3,128,128]{2,1,0:T(8,128)S(1)}, f32[3,128,128]{2,1,0:T(8,128)S(1)}, u32[]{:S(2)}, u32[]{:S(2)}) collective-permute-start(f32[3,128,128]{2,1,0:T(8,128)S(1)} %get-tuple-element.98), channel_id=1, source_target_pairs={{0,4},{4,0},{1,5},{5,1},{2,6},{6,2},{3,7},{7,3},{8,12},{12,8},{9,1... | collective-permute-start | bytes 589832 | tf_op jit(solution)/shard_map/ppermute | solution.py:364
  40.1 0.5 collective-permute-done.13.state
  41.2 2.6 %collective-permute-start.16 = (f32[2,256]{1,0:T(2,128)S(1)}, f32[2,256]{1,0:T(2,128)S(1)}, u32[]{:S(2)}, u32[]{:S(2)}) collective-permute-start(f32[2,256]{1,0:T(2,128)S(1)} %get-tuple-element.103.refs_3_), channel_id=1, source_target_pairs={{0,3},{1,2},{2,1},{3,0},{4,7},{5,6},{6,5},{7,4},{8,11},{9,10},{10,... | collective-permute-start | bytes 6152 | tf_op jit(solution)/shard_map/ppermute | solution.py:364
  43.8 0.5 collective-permute-start.15
  44.6 0.4 collective-permute-done.16.refs_2_
  45.0 2.8 %collective-permute-done.15.refs_1_ = f32[2,256]{1,0:T(2,128)S(1)} collective-permute-done((f32[2,256]{1,0:T(2,128)S(1)}, f32[2,256]{1,0:T(2,128)S(1)}, u32[]{:S(2)}, u32[]{:S(2)}) %collective-permute-start.15) | collective-permute-done | bytes 2080 | tf_op jit(solution)/shard_map/ppermute | solution.py:364
  47.7 0.4 shard_map.91
  48.2 1.9 %collective-permute-start.17 = (f32[3,128,128]{2,1,0:T(8,128)S(1)}, f32[3,128,128]{2,1,0:T(8,128)S(1)}, u32[]{:S(2)}, u32[]{:S(2)}) collective-permute-start(f32[3,128,128]{2,1,0:T(8,128)S(1)} %get-tuple-element.113), channel_id=1, source_target_pairs={{0,4},{4,0},{1,5},{5,1},{2,6},{6,2},{3,7},{7,3},{8,12},{12,8},{9,1... | collective-permute-start | bytes 589832 | tf_op jit(solution)/shard_map/ppermute | solution.py:364
  50.2 0.4 shard_map.90
  50.6 0.7 collective-permute-done.20.got.refs_3_.refs_5_
  51.3 1.7 %collective-permute-start.21 = (f32[128,128]{1,0:T(8,128)S(1)}, f32[128,128]{1,0:T(8,128)S(1)}, u32[]{:S(2)}, u32[]{:S(2)}) collective-permute-start(f32[128,128]{1,0:T(8,128)S(1)} %shard_map.95), channel_id=1, source_target_pairs={{0,24},{8,16},{16,8},{24,0},{1,25},{9,17},{17,9},{25,1},{2,26},{10... | collective-permute-start | bytes 196616 | tf_op jit(solution)/shard_map/ppermute | solution.py:364
  53.2 1.9 %collective-permute-start.19 = (f32[128,128]{1,0:T(8,128)S(1)}, f32[128,128]{1,0:T(8,128)S(1)}, u32[]{:S(2)}, u32[]{:S(2)}) collective-permute-start(f32[128,128]{1,0:T(8,128)S(1)} %get-tuple-element.119), channel_id=1, source_target_pairs={{0,16},{8,24},{16,0},{24,8},{1,17},{9,25},{17,1},{25,9},{2,18},{10... | collective-permute-start | bytes 196616 | tf_op jit(solution)/shard_map/ppermute | solution.py:364
  55.1 0.9 %shard_map.94 = (f32[256,512]{1,0:T(8,128)S(1)}, f32[256,512]{1,0:T(8,128)S(1)}) custom-call(bf16[256,1024]{1,0:T(8,128)(2,1)S(1)} %get-tuple-element.78.refs_6_.queries, bf16[256,512]{1,0:T(8,128)(2,1)S(1)} %get-tuple-element.72.keys_1.refs_1_.keys.refs_0_, bf16[256,512]{1,0:T(8,128)(2,1)S(1)} %get-tuple-element.74.values_1.refs_3_.values.refs_1_, ...), custom_call_target="tpu_custom_call" | custom-call | flops 1000000000 | bytes 2097152 | tf_op jit(solution)/shard_map/pallas_call | solution.py:73
  56.0 0.9 %shard_map.96 = (f32[256,512]{1,0:T(8,128)S(1)}, f32[256,512]{1,0:T(8,128)S(1)}) custom-call(bf16[256,1024]{1,0:T(8,128)(2,1)S(1)} %get-tuple-element.78.refs_6_.queries, bf16[256,512]{1,0:T(8,128)(2,1)S(1)} %get-tuple-element.71.keys.keys_0.refs_0_, bf16[256,512]{1,0:T(8,128)(2,1)S(1)} %get-tuple-element.73.values.values_0.refs_2_.refs_1_, ...), custom_call_target="tpu_custom_call" | custom-call | flops 1000000000 | bytes 2097152 | tf_op jit(solution)/shard_map/pallas_call | solution.py:73
  57.0 3.0 %shard_map.93.refs_0_ = bf16[256,1024]{1,0:T(8,128)(2,1)} custom-call(bf16[256,512]{1,0:T(8,128)(2,1)S(1)} %get-tuple-element.71.keys.keys_0.refs_0_, bf16[256,512]{1,0:T(8,128)(2,1)S(1)} %get-tuple-element.72.keys_1.refs_1_.keys.refs_0_, bf16[256,512]{1,0:T(8,128)(2,1)S(1)} %get-tuple-element.73.values.values_0.refs_2_.refs_1_, ...), custom_call_target="tpu_custom_call" | custom-call | flops 1000000000 | bytes 2097152 | tf_op jit(solution)/shard_map/pallas_call | solution.py:73
  60.0 3.6 %collective-permute-start.22 = (f32[128,128]{1,0:T(8,128)S(1)}, f32[128,128]{1,0:T(8,128)S(1)}, u32[]{:S(2)}, u32[]{:S(2)}) collective-permute-start(f32[128,128]{1,0:T(8,128)S(1)} %shard_map.97.refs_0_), channel_id=1, source_target_pairs={{0,48},{8,56},{16,32},{24,40},{32,16},{40,24},{48,0},{56,8},{1,49}... | collective-permute-start | bytes 196616 | tf_op jit(solution)/shard_map/ppermute | solution.py:364
  63.6 1.8 %collective-permute-done.22.refs_1_.refs_4_ = f32[128,128]{1,0:T(8,128)S(1)} collective-permute-done((f32[128,128]{1,0:T(8,128)S(1)}, f32[128,128]{1,0:T(8,128)S(1)}, u32[]{:S(2)}, u32[]{:S(2)}) %collective-permute-start.22) | collective-permute-done | bytes 65568 | tf_op jit(solution)/shard_map/ppermute | solution.py:364
  65.4 1.1 %collective-permute-start.25 = (f32[128,128]{1,0:T(8,128)S(1)}, f32[128,128]{1,0:T(8,128)S(1)}, u32[]{:S(2)}, u32[]{:S(2)}) collective-permute-start(f32[128,128]{1,0:T(8,128)S(1)} %shard_map.98), channel_id=1, source_target_pairs={{0,192},{64,128},{128,64},{192,0},{1,193},{65,129},{129,65},{193,1... | collective-permute-start | bytes 196616 | tf_op jit(solution)/shard_map/ppermute | solution.py:364
  66.5 0.8 collective-permute-start.24
  67.3 1.4 %collective-permute-start.23 = (f32[128,128]{1,0:T(8,128)S(1)}, f32[128,128]{1,0:T(8,128)S(1)}, u32[]{:S(2)}, u32[]{:S(2)}) collective-permute-start(f32[128,128]{1,0:T(8,128)S(1)} %shard_map.98), channel_id=1, source_target_pairs={{0,64},{64,0},{128,192},{192,128},{1,65},{65,1},{129,193},{193,129... | collective-permute-start | bytes 196616 | tf_op jit(solution)/shard_map/ppermute | solution.py:364
  68.7 1.1 %collective-permute-done.25.refs_7_ = f32[128,128]{1,0:T(8,128)S(1)} collective-permute-done((f32[128,128]{1,0:T(8,128)S(1)}, f32[128,128]{1,0:T(8,128)S(1)}, u32[]{:S(2)}, u32[]{:S(2)}) %collective-permute-start.25) | collective-permute-done | bytes 65568 | tf_op jit(solution)/shard_map/ppermute | solution.py:364
  69.8 1.3 %collective-permute-done.24.refs_6_ = f32[128,128]{1,0:T(8,128)S(1)} collective-permute-done((f32[128,128]{1,0:T(8,128)S(1)}, f32[128,128]{1,0:T(8,128)S(1)}, u32[]{:S(2)}, u32[]{:S(2)}) %collective-permute-start.24) | collective-permute-done | bytes 65568 | tf_op jit(solution)/shard_map/ppermute | solution.py:364
  71.2 1.7 %collective-permute-start.28 = (f32[128,128]{1,0:T(8,128)S(1)}, f32[128,128]{1,0:T(8,128)S(1)}, u32[]{:S(2)}, u32[]{:S(2)}) collective-permute-start(f32[128,128]{1,0:T(8,128)S(1)} %get-tuple-element.128), channel_id=1, source_target_pairs={{0,24},{8,16},{16,8},{24,0},{1,25},{9,17},{17,9},{25,1},{2,26},{10... | collective-permute-start | bytes 196616 | tf_op jit(solution)/shard_map/ppermute | solution.py:364
  72.9 1.4 %collective-permute-start.29 = (f32[128,128]{1,0:T(8,128)S(1)}, f32[128,128]{1,0:T(8,128)S(1)}, u32[]{:S(2)}, u32[]{:S(2)}) collective-permute-start(f32[128,128]{1,0:T(8,128)S(1)} %get-tuple-element.129), channel_id=1, source_target_pairs={{0,16},{8,24},{16,0},{24,8},{1,17},{9,25},{17,1},{25,9},{2,18},{10... | collective-permute-start | bytes 196616 | tf_op jit(solution)/shard_map/ppermute | solution.py:364
  74.3 0.5 collective-permute-start.26
  74.9 1.5 %collective-permute-done.28.refs_1_ = f32[128,128]{1,0:T(8,128)S(1)} collective-permute-done((f32[128,128]{1,0:T(8,128)S(1)}, f32[128,128]{1,0:T(8,128)S(1)}, u32[]{:S(2)}, u32[]{:S(2)}) %collective-permute-start.28) | collective-permute-done | bytes 65568 | tf_op jit(solution)/shard_map/ppermute | solution.py:364
  76.3 1.7 %collective-permute-done.29.refs_2_ = f32[128,128]{1,0:T(8,128)S(1)} collective-permute-done((f32[128,128]{1,0:T(8,128)S(1)}, f32[128,128]{1,0:T(8,128)S(1)}, u32[]{:S(2)}, u32[]{:S(2)}) %collective-permute-start.29) | collective-permute-done | bytes 65568 | tf_op jit(solution)/shard_map/ppermute | solution.py:364
  78.1 4.8 %collective-permute-start.30 = (f32[3,128,128]{2,1,0:T(8,128)S(1)}, f32[3,128,128]{2,1,0:T(8,128)S(1)}, u32[]{:S(2)}, u32[]{:S(2)}) collective-permute-start(f32[3,128,128]{2,1,0:T(8,128)S(1)} %get-tuple-element.134), channel_id=1, source_target_pairs={{0,4},{4,0},{1,5},{5,1},{2,6},{6,2},{3,7},{7,3},{8,12},{12,8},{9,1... | collective-permute-start | bytes 589832 | tf_op jit(solution)/shard_map/ppermute | solution.py:364
  83.0 0.4 shard_map.102
  83.4 0.5 collective-permute-done.30.refs_5_
  84.3 1.5 %shard_map.104 = (bf16[256,1024]{1,0:T(8,128)(2,1)}, bf16[256,1024]{1,0:T(8,128)(2,1)}) custom-call(bf16[256,512]{1,0:T(8,128)(2,1)S(1)} %get-tuple-element.72.keys_1.refs_1_.keys.refs_0_, bf16[256,512]{1,0:T(8,128)(2,1)S(1)} %get-tuple-element.74.values_1.refs_3_.values.refs_1_, f32[256,512]{1,0:T(8,128)S(1)} %get-tuple-element.115.refs_7_.refs_2_, ...), custom_call_target="tpu_custom_call" | custom-call | flops 1000000000 | bytes 2097152 | tf_op jit(solution)/shard_map/pallas_call | solution.py:73
  (46 shorter events, 3.9 us)
Async XLA Ops:
  2.0 3.4 %copy-start = (bf16[1024]{0:T(1024)(128)(2,1)S(1)}, bf16[1024]{0:T(1024)(128)(2,1)}, u32[]{:S(2)}) copy-start(bf16[1024]{0:T(1024)(128)(2,1)} %param.9) | copy-start | bytes 6148
  2.0 7.3 %collective-permute-start = (f32[3,128,128]{2,1,0:T(8,128)S(1)}, f32[3,128,128]{2,1,0:T(8,128)S(1)}, u32[]{:S(2)}, u32[]{:S(2)}) collective-permute-start(f32[3,128,128]{2,1,0:T(8,128)S(1)} %get-tuple-element.76), channel_id=1, source_target_pairs={{0,4},{4,0},{1,5},{5,1},{2,6},{6,2},{3,7},{7,3},{8,12},{12,8},{9,1... | collective-permute-start | bytes 589832 | tf_op jit(solution)/shard_map/ppermute | solution.py:364
  5.3 1.3 %collective-permute-start.3 = (f32[1,128,128]{2,1,0:T(8,128)S(1)}, f32[1,128,128]{2,1,0:T(8,128)S(1)}, u32[]{:S(2)}, u32[]{:S(2)}) collective-permute-start(f32[1,128,128]{2,1,0:T(8,128)S(1)} %get-tuple-element.84), channel_id=1, source_target_pairs={{0,4},{4,0},{1,5},{5,1},{2,6},{6,2},{3,7},{7,3},{8,12},{12,8},{9,1... | collective-permute-start | bytes 196616 | tf_op jit(solution)/shard_map/ppermute | solution.py:364
  6.6 6.1 %collective-permute-start.4 = (f32[128,128]{1,0:T(8,128)S(1)}, f32[128,128]{1,0:T(8,128)S(1)}, u32[]{:S(2)}, u32[]{:S(2)}) collective-permute-start(f32[128,128]{1,0:T(8,128)S(1)} %shard_map.80), channel_id=1, source_target_pairs={{0,24},{8,16},{16,8},{24,0},{1,25},{9,17},{17,9},{25,1},{2,26},{10... | collective-permute-start | bytes 196616 | tf_op jit(solution)/shard_map/ppermute | solution.py:364
  9.3 5.1 %collective-permute-start.1 = (f32[128,128]{1,0:T(8,128)S(1)}, f32[128,128]{1,0:T(8,128)S(1)}, u32[]{:S(2)}, u32[]{:S(2)}) collective-permute-start(f32[128,128]{1,0:T(8,128)S(1)} %get-tuple-element.81), channel_id=1, source_target_pairs={{0,8},{8,0},{16,24},{24,16},{1,9},{9,1},{17,25},{25,17},{2,10},{10... | collective-permute-start | bytes 196616 | tf_op jit(solution)/shard_map/ppermute | solution.py:364
  9.4 5.0 %collective-permute-start.2 = (f32[128,128]{1,0:T(8,128)S(1)}, f32[128,128]{1,0:T(8,128)S(1)}, u32[]{:S(2)}, u32[]{:S(2)}) collective-permute-start(f32[128,128]{1,0:T(8,128)S(1)} %get-tuple-element.82), channel_id=1, source_target_pairs={{0,16},{8,24},{16,0},{24,8},{1,17},{9,25},{17,1},{25,9},{2,18},{10... | collective-permute-start | bytes 196616 | tf_op jit(solution)/shard_map/ppermute | solution.py:364
  14.5 5.5 %collective-permute-start.5 = (f32[128,128]{1,0:T(8,128)S(1)}, f32[128,128]{1,0:T(8,128)S(1)}, u32[]{:S(2)}, u32[]{:S(2)}) collective-permute-start(f32[128,128]{1,0:T(8,128)S(1)} %shard_map.81.refs_0_), channel_id=1, source_target_pairs={{0,48},{8,56},{16,32},{24,40},{32,16},{40,24},{48,0},{56,8},{1,49}... | collective-permute-start | bytes 196616 | tf_op jit(solution)/shard_map/ppermute | solution.py:364
  20.0 4.5 %collective-permute-start.8 = (f32[128,128]{1,0:T(8,128)S(1)}, f32[128,128]{1,0:T(8,128)S(1)}, u32[]{:S(2)}, u32[]{:S(2)}) collective-permute-start(f32[128,128]{1,0:T(8,128)S(1)} %shard_map.82), channel_id=1, source_target_pairs={{0,192},{64,128},{128,64},{192,0},{1,193},{65,129},{129,65},{193,1... | collective-permute-start | bytes 196616 | tf_op jit(solution)/shard_map/ppermute | solution.py:364
  22.8 4.7 %collective-permute-start.7 = (f32[128,128]{1,0:T(8,128)S(1)}, f32[128,128]{1,0:T(8,128)S(1)}, u32[]{:S(2)}, u32[]{:S(2)}) collective-permute-start(f32[128,128]{1,0:T(8,128)S(1)} %shard_map.82), channel_id=1, source_target_pairs={{0,128},{64,192},{128,0},{192,64},{1,129},{65,193},{129,1},{193,65... | collective-permute-start | bytes 196616 | tf_op jit(solution)/shard_map/ppermute | solution.py:364
  23.2 4.4 %collective-permute-start.6 = (f32[128,128]{1,0:T(8,128)S(1)}, f32[128,128]{1,0:T(8,128)S(1)}, u32[]{:S(2)}, u32[]{:S(2)}) collective-permute-start(f32[128,128]{1,0:T(8,128)S(1)} %shard_map.82), channel_id=1, source_target_pairs={{0,64},{64,0},{128,192},{192,128},{1,65},{65,1},{129,193},{193,129... | collective-permute-start | bytes 196616 | tf_op jit(solution)/shard_map/ppermute | solution.py:364
  27.6 5.1 %collective-permute-start.9 = (f32[128,128]{1,0:T(8,128)S(1)}, f32[128,128]{1,0:T(8,128)S(1)}, u32[]{:S(2)}, u32[]{:S(2)}) collective-permute-start(f32[128,128]{1,0:T(8,128)S(1)} %get-tuple-element.86), channel_id=1, source_target_pairs={{0,24},{8,16},{16,8},{24,0},{1,25},{9,17},{17,9},{25,1},{2,26},{10... | collective-permute-start | bytes 196616 | tf_op jit(solution)/shard_map/ppermute | solution.py:364
  29.6 5.0 %collective-permute-start.10 = (f32[128,128]{1,0:T(8,128)S(1)}, f32[128,128]{1,0:T(8,128)S(1)}, u32[]{:S(2)}, u32[]{:S(2)}) collective-permute-start(f32[128,128]{1,0:T(8,128)S(1)} %get-tuple-element.87), channel_id=1, source_target_pairs={{0,16},{8,24},{16,0},{24,8},{1,17},{9,25},{17,1},{25,9},{2,18},{10... | collective-permute-start | bytes 196616 | tf_op jit(solution)/shard_map/ppermute | solution.py:364
  30.8 8.8 %collective-permute-start.11 = (f32[128,128]{1,0:T(8,128)S(1)}, f32[128,128]{1,0:T(8,128)S(1)}, u32[]{:S(2)}, u32[]{:S(2)}) collective-permute-start(f32[128,128]{1,0:T(8,128)S(1)} %get-tuple-element.91), channel_id=1, source_target_pairs={{0,8},{8,0},{16,24},{24,16},{1,9},{9,1},{17,25},{25,17},{2,10},{10... | collective-permute-start | bytes 196616 | tf_op jit(solution)/shard_map/ppermute | solution.py:364
  34.6 6.0 %collective-permute-start.13 = (f32[3,128,128]{2,1,0:T(8,128)S(1)}, f32[3,128,128]{2,1,0:T(8,128)S(1)}, u32[]{:S(2)}, u32[]{:S(2)}) collective-permute-start(f32[3,128,128]{2,1,0:T(8,128)S(1)} %get-tuple-element.98), channel_id=1, source_target_pairs={{0,4},{4,0},{1,5},{5,1},{2,6},{6,2},{3,7},{7,3},{8,12},{12,8},{9,1... | collective-permute-start | bytes 589832 | tf_op jit(solution)/shard_map/ppermute | solution.py:364
  39.6 1.3 %collective-permute-start.12 = (f32[1,128,128]{2,1,0:T(8,128)S(1)}, f32[1,128,128]{2,1,0:T(8,128)S(1)}, u32[]{:S(2)}, u32[]{:S(2)}) collective-permute-start(f32[1,128,128]{2,1,0:T(8,128)S(1)} %get-tuple-element.96), channel_id=1, source_target_pairs={{0,4},{4,0},{1,5},{5,1},{2,6},{6,2},{3,7},{7,3},{8,12},{12,8},{9,1... | collective-permute-start | bytes 196616 | tf_op jit(solution)/shard_map/ppermute | solution.py:364
  41.2 3.7 %collective-permute-start.16 = (f32[2,256]{1,0:T(2,128)S(1)}, f32[2,256]{1,0:T(2,128)S(1)}, u32[]{:S(2)}, u32[]{:S(2)}) collective-permute-start(f32[2,256]{1,0:T(2,128)S(1)} %get-tuple-element.103.refs_3_), channel_id=1, source_target_pairs={{0,3},{1,2},{2,1},{3,0},{4,7},{5,6},{6,5},{7,4},{8,11},{9,10},{10,... | collective-permute-start | bytes 6152 | tf_op jit(solution)/shard_map/ppermute | solution.py:364
  43.8 3.9 %collective-permute-start.15 = (f32[2,256]{1,0:T(2,128)S(1)}, f32[2,256]{1,0:T(2,128)S(1)}, u32[]{:S(2)}, u32[]{:S(2)}) collective-permute-start(f32[2,256]{1,0:T(2,128)S(1)} %get-tuple-element.103.refs_3_), channel_id=1, source_target_pairs={{0,2},{1,3},{2,0},{3,1},{4,6},{5,7},{6,4},{7,5},{8,10},{9,11},{10,... | collective-permute-start | bytes 6152 | tf_op jit(solution)/shard_map/ppermute | solution.py:364
  44.3 3.4 %collective-permute-start.14 = (f32[2,256]{1,0:T(2,128)S(1)}, f32[2,256]{1,0:T(2,128)S(1)}, u32[]{:S(2)}, u32[]{:S(2)}) collective-permute-start(f32[2,256]{1,0:T(2,128)S(1)} %get-tuple-element.103.refs_3_), channel_id=1, source_target_pairs={{0,1},{1,0},{2,3},{3,2},{4,5},{5,4},{6,7},{7,6},{8,9},{9,8},{10,11... | collective-permute-start | bytes 6152 | tf_op jit(solution)/shard_map/ppermute | solution.py:364
  48.2 4.9 %collective-permute-start.17 = (f32[3,128,128]{2,1,0:T(8,128)S(1)}, f32[3,128,128]{2,1,0:T(8,128)S(1)}, u32[]{:S(2)}, u32[]{:S(2)}) collective-permute-start(f32[3,128,128]{2,1,0:T(8,128)S(1)} %get-tuple-element.113), channel_id=1, source_target_pairs={{0,4},{4,0},{1,5},{5,1},{2,6},{6,2},{3,7},{7,3},{8,12},{12,8},{9,1... | collective-permute-start | bytes 589832 | tf_op jit(solution)/shard_map/ppermute | solution.py:364
  50.1 1.3 %collective-permute-start.20 = (f32[1,128,128]{2,1,0:T(8,128)S(1)}, f32[1,128,128]{2,1,0:T(8,128)S(1)}, u32[]{:S(2)}, u32[]{:S(2)}) collective-permute-start(f32[1,128,128]{2,1,0:T(8,128)S(1)} %get-tuple-element.121), channel_id=1, source_target_pairs={{0,4},{4,0},{1,5},{5,1},{2,6},{6,2},{3,7},{7,3},{8,12},{12,8},{9,1... | collective-permute-start | bytes 196616 | tf_op jit(solution)/shard_map/ppermute | solution.py:364
  51.3 8.6 %collective-permute-start.21 = (f32[128,128]{1,0:T(8,128)S(1)}, f32[128,128]{1,0:T(8,128)S(1)}, u32[]{:S(2)}, u32[]{:S(2)}) collective-permute-start(f32[128,128]{1,0:T(8,128)S(1)} %shard_map.95), channel_id=1, source_target_pairs={{0,24},{8,16},{16,8},{24,0},{1,25},{9,17},{17,9},{25,1},{2,26},{10... | collective-permute-start | bytes 196616 | tf_op jit(solution)/shard_map/ppermute | solution.py:364
  53.1 6.9 %collective-permute-start.18 = (f32[128,128]{1,0:T(8,128)S(1)}, f32[128,128]{1,0:T(8,128)S(1)}, u32[]{:S(2)}, u32[]{:S(2)}) collective-permute-start(f32[128,128]{1,0:T(8,128)S(1)} %get-tuple-element.118), channel_id=1, source_target_pairs={{0,8},{8,0},{16,24},{24,16},{1,9},{9,1},{17,25},{25,17},{2,10},{10... | collective-permute-start | bytes 196616 | tf_op jit(solution)/shard_map/ppermute | solution.py:364
  53.2 6.8 %collective-permute-start.19 = (f32[128,128]{1,0:T(8,128)S(1)}, f32[128,128]{1,0:T(8,128)S(1)}, u32[]{:S(2)}, u32[]{:S(2)}) collective-permute-start(f32[128,128]{1,0:T(8,128)S(1)} %get-tuple-element.119), channel_id=1, source_target_pairs={{0,16},{8,24},{16,0},{24,8},{1,17},{9,25},{17,1},{25,9},{2,18},{10... | collective-permute-start | bytes 196616 | tf_op jit(solution)/shard_map/ppermute | solution.py:364
  60.0 5.4 %collective-permute-start.22 = (f32[128,128]{1,0:T(8,128)S(1)}, f32[128,128]{1,0:T(8,128)S(1)}, u32[]{:S(2)}, u32[]{:S(2)}) collective-permute-start(f32[128,128]{1,0:T(8,128)S(1)} %shard_map.97.refs_0_), channel_id=1, source_target_pairs={{0,48},{8,56},{16,32},{24,40},{32,16},{40,24},{48,0},{56,8},{1,49}... | collective-permute-start | bytes 196616 | tf_op jit(solution)/shard_map/ppermute | solution.py:364
  65.4 4.4 %collective-permute-start.25 = (f32[128,128]{1,0:T(8,128)S(1)}, f32[128,128]{1,0:T(8,128)S(1)}, u32[]{:S(2)}, u32[]{:S(2)}) collective-permute-start(f32[128,128]{1,0:T(8,128)S(1)} %shard_map.98), channel_id=1, source_target_pairs={{0,192},{64,128},{128,64},{192,0},{1,193},{65,129},{129,65},{193,1... | collective-permute-start | bytes 196616 | tf_op jit(solution)/shard_map/ppermute | solution.py:364
  66.5 4.6 %collective-permute-start.24 = (f32[128,128]{1,0:T(8,128)S(1)}, f32[128,128]{1,0:T(8,128)S(1)}, u32[]{:S(2)}, u32[]{:S(2)}) collective-permute-start(f32[128,128]{1,0:T(8,128)S(1)} %shard_map.98), channel_id=1, source_target_pairs={{0,128},{64,192},{128,0},{192,64},{1,129},{65,193},{129,1},{193,65... | collective-permute-start | bytes 196616 | tf_op jit(solution)/shard_map/ppermute | solution.py:364
  67.3 3.8 %collective-permute-start.23 = (f32[128,128]{1,0:T(8,128)S(1)}, f32[128,128]{1,0:T(8,128)S(1)}, u32[]{:S(2)}, u32[]{:S(2)}) collective-permute-start(f32[128,128]{1,0:T(8,128)S(1)} %shard_map.98), channel_id=1, source_target_pairs={{0,64},{64,0},{128,192},{192,128},{1,65},{65,1},{129,193},{193,129... | collective-permute-start | bytes 196616 | tf_op jit(solution)/shard_map/ppermute | solution.py:364
  71.2 5.1 %collective-permute-start.28 = (f32[128,128]{1,0:T(8,128)S(1)}, f32[128,128]{1,0:T(8,128)S(1)}, u32[]{:S(2)}, u32[]{:S(2)}) collective-permute-start(f32[128,128]{1,0:T(8,128)S(1)} %get-tuple-element.128), channel_id=1, source_target_pairs={{0,24},{8,16},{16,8},{24,0},{1,25},{9,17},{17,9},{25,1},{2,26},{10... | collective-permute-start | bytes 196616 | tf_op jit(solution)/shard_map/ppermute | solution.py:364
  72.9 5.1 %collective-permute-start.29 = (f32[128,128]{1,0:T(8,128)S(1)}, f32[128,128]{1,0:T(8,128)S(1)}, u32[]{:S(2)}, u32[]{:S(2)}) collective-permute-start(f32[128,128]{1,0:T(8,128)S(1)} %get-tuple-element.129), channel_id=1, source_target_pairs={{0,16},{8,24},{16,0},{24,8},{1,17},{9,25},{17,1},{25,9},{2,18},{10... | collective-permute-start | bytes 196616 | tf_op jit(solution)/shard_map/ppermute | solution.py:364
  74.3 8.6 %collective-permute-start.26 = (f32[128,128]{1,0:T(8,128)S(1)}, f32[128,128]{1,0:T(8,128)S(1)}, u32[]{:S(2)}, u32[]{:S(2)}) collective-permute-start(f32[128,128]{1,0:T(8,128)S(1)} %get-tuple-element.124), channel_id=1, source_target_pairs={{0,8},{8,0},{16,24},{24,16},{1,9},{9,1},{17,25},{25,17},{2,10},{10... | collective-permute-start | bytes 196616 | tf_op jit(solution)/shard_map/ppermute | solution.py:364
  78.1 5.8 %collective-permute-start.30 = (f32[3,128,128]{2,1,0:T(8,128)S(1)}, f32[3,128,128]{2,1,0:T(8,128)S(1)}, u32[]{:S(2)}, u32[]{:S(2)}) collective-permute-start(f32[3,128,128]{2,1,0:T(8,128)S(1)} %get-tuple-element.134), channel_id=1, source_target_pairs={{0,4},{4,0},{1,5},{5,1},{2,6},{6,2},{3,7},{7,3},{8,12},{12,8},{9,1... | collective-permute-start | bytes 589832 | tf_op jit(solution)/shard_map/ppermute | solution.py:364
  82.9 1.4 %collective-permute-start.27 = (f32[1,128,128]{2,1,0:T(8,128)S(1)}, f32[1,128,128]{2,1,0:T(8,128)S(1)}, u32[]{:S(2)}, u32[]{:S(2)}) collective-permute-start(f32[1,128,128]{2,1,0:T(8,128)S(1)} %get-tuple-element.125), channel_id=1, source_target_pairs={{0,4},{4,0},{1,5},{5,1},{2,6},{6,2},{3,7},{7,3},{8,12},{12,8},{9,1... | collective-permute-start | bytes 196616 | tf_op jit(solution)/shard_map/ppermute | solution.py:364
